TPU v7x, 512 devices: a whole 4x8x8 slice. The times are simulated.
512 devices in a mesh: dp: 16 (over y, core), expert: 8 (over z), mp: 4 (over x).
Axes of the slice: x: 4, y: 8, z: 8, core: 2. Of those that a mesh axis runs over, the one named last changes fastest.
Arguments:
- tokens: bfloat16 [2048, 4096], P('dp', 'mp'), may hold values from -6 to 6
- slot_ids: int32 [2048, 2], P('dp'), may hold values from 0 to 7, all different within a row; in each aligned block of 128 rows (0 to 127, 128 to 255, ...) at most 40 rows name the same one
- gate_values: float32 [2048, 2], P('dp'), may hold values from 0.2 to 1
- slot_expert: int32 [8], replicated, may hold values from 0 to 3, as said below
- w_gate: bfloat16 [4, 7168, 4096], P(None, ('dp', 'expert'), 'mp'), may hold values from -0.09375 to 0.09375
- w_up: bfloat16 [4, 7168, 4096], P(None, ('dp', 'expert'), 'mp'), may hold values from -0.09375 to 0.09375
- w_down: bfloat16 [4, 7168, 4096], P(None, ('dp', 'expert'), 'mp'), may hold values from -0.0625 to 0.0625
- cotangent: bfloat16 [2048, 4096], P('dp', 'mp'), may hold values from -6 to 6
Outputs:
- mixed: bfloat16 [2048, 4096], P('dp', 'mp')
- grad_tokens: bfloat16 [2048, 4096], P('dp', 'mp')
- grad_gate: bfloat16 [4, 7168, 4096], P(None, ('dp', 'expert'), 'mp')
- grad_up: bfloat16 [4, 7168, 4096], P(None, ('dp', 'expert'), 'mp')
- grad_down: bfloat16 [4, 7168, 4096], P(None, ('dp', 'expert'), 'mp')
Inputs may be any that keep to these rules, and one draw needn't show every extreme that they name: `slot_ids`: the two slots of a token differ. Among the tokens of one index of dp no slot is named more than 40 times, a bound that some block reaches in some of them. `slot_expert`: every one of the 4 experts is held by one slot or more.
All inputs are finite; a program needn't handle non-finite values.
Results may differ from a plain program's by a relative error of at most 0.024.
Values may be sent and summed in bfloat16 or wider, within the bound.
No kernel may reach another device: no remote copies, remote signals or barrier semaphores. Data moves between devices by JAX's collectives and lax.ppermute only.
A program may use at most 64 MiB of HBM per device.

v0:
```python
import jax
import jax.numpy as jnp
from jax import lax
from jax.sharding import PartitionSpec as P


def as_sent(x):

    def short(part):
        return part.astype(jnp.bfloat16) if part.dtype == jnp.float32 else part

    return jax.tree.map(short, x)


def gather_rows(buffer, handler):
    return handler(lax.all_gather(buffer, "dp", axis=0, tiled=True), jnp.int32(0))


def sum_features(partials):
    return jax.tree.map(lambda part: part.astype(jnp.float32), lax.psum(as_sent(partials), "mp"))


def send_back(partial_value, capacity):
    blocks = partial_value.reshape(-1, capacity, partial_value.shape[1])
    arrived = lax.all_to_all(
        blocks.astype(jnp.bfloat16), "dp", split_axis=0, concat_axis=0, tiled=True
    ).astype(blocks.dtype)
    return jnp.sum(arrived, axis=0)


def token_total(partial_value):
    return lax.psum(partial_value.astype(jnp.bfloat16), "expert").astype(jnp.float32)


def contract_last(left, right):
    return lax.dot_general(
        left, right, (((1,), (1,)), ((), ())), preferred_element_type=jnp.float32
    )


def contract_first(left, right):
    return lax.dot_general(
        left, right, (((0,), (0,)), ((), ())), preferred_element_type=jnp.float32
    )


def body(tokens, slot_ids, gate_values, slot_expert, w_gate, w_up, w_down, cotangent):
    tok_count, width = tokens.shape
    slot_count = lax.axis_size("expert")
    capacity = min(tok_count, tok_count * 10 // (4 * slot_count))
    own_slot = lax.axis_index("expert")
    stack_gate = jnp.take(w_gate, slot_expert, axis=0)
    stack_up = jnp.take(w_up, slot_expert, axis=0)
    stack_down = jnp.take(w_down, slot_expert, axis=0)
    fetched = (
        lax.all_to_all(stack_gate, "expert", split_axis=0, concat_axis=1, tiled=True),
        lax.all_to_all(stack_up, "expert", split_axis=0, concat_axis=1, tiled=True),
        lax.all_to_all(stack_down, "expert", split_axis=0, concat_axis=1, tiled=True),
    )
    slot_gate = fetched[0][0]
    slot_up = fetched[1][0]
    slot_down = fetched[2][0]
    flattened = slot_ids.reshape(-1)
    chosen = flattened == own_slot
    position = jnp.cumsum(chosen.astype(jnp.int32)) - 1
    placing = (
        (position[None, :] == jnp.arange(capacity, dtype=jnp.int32)[:, None]) & chosen[None, :]
    ).astype(jnp.float32)
    gate_buf = jnp.dot(placing, gate_values.reshape(-1), precision=lax.Precision.HIGHEST)
    selected = jnp.sum(placing.reshape(capacity, tok_count, 2), axis=2)
    selected_bf = selected.astype(jnp.bfloat16)
    input_buf = jnp.dot(selected_bf, tokens, preferred_element_type=jnp.float32).astype(
        jnp.bfloat16
    )

    def forward_rows(shard_rows, first_row):
        gate_part = contract_last(shard_rows, slot_gate).astype(jnp.bfloat16)
        up_part = contract_last(shard_rows, slot_up).astype(jnp.bfloat16)
        return (shard_rows, gate_part, up_part)

    input_rows, gate_part, up_part = gather_rows(input_buf, forward_rows)
    gate_sum, up_sum = sum_features((gate_part, up_part))
    sigm = jax.nn.sigmoid(gate_sum)
    active = gate_sum * sigm
    hidden_local = (active * up_sum).astype(jnp.bfloat16)
    out_part = jnp.dot(hidden_local, slot_down, preferred_element_type=jnp.float32)
    out_buf = send_back(out_part, capacity)
    mixed_rows = lax.dot_general(
        selected,
        gate_buf[:, None] * out_buf,
        (((0,), (0,)), ((), ())),
        precision=lax.Precision.HIGHEST,
    )
    mixed = token_total(mixed_rows).astype(jnp.bfloat16)
    upstream_buf = (
        gate_buf[:, None] * jnp.dot(selected_bf, cotangent, preferred_element_type=jnp.float32)
    ).astype(jnp.bfloat16)

    def backward_rows(shard_rows, first_row):
        grad_part = contract_last(shard_rows, slot_down).astype(jnp.bfloat16)
        return (shard_rows, grad_part)

    upstream_rows, grad_part = gather_rows(upstream_buf, backward_rows)
    grad_hidden = sum_features((grad_part,))[0]
    grad_gate_local = (grad_hidden * up_sum * sigm * (1.0 + gate_sum * (1.0 - sigm))).astype(
        jnp.bfloat16
    )
    grad_up_local = (grad_hidden * active).astype(jnp.bfloat16)
    grad_gatev, grad_upv = (grad_gate_local, grad_up_local)
    back_part = jnp.dot(grad_gatev, slot_gate, preferred_element_type=jnp.float32) + jnp.dot(
        grad_upv, slot_up, preferred_element_type=jnp.float32
    )
    back_buf = send_back(back_part, capacity)
    back_rows = lax.dot_general(
        selected, back_buf, (((0,), (0,)), ((), ())), precision=lax.Precision.HIGHEST
    )
    grad_tokens = token_total(back_rows).astype(jnp.bfloat16)
    part_gate = contract_first(grad_gatev, input_rows).astype(jnp.bfloat16)
    part_up = contract_first(grad_upv, input_rows).astype(jnp.bfloat16)
    part_down = contract_first(hidden_local, upstream_rows).astype(jnp.bfloat16)
    returned = (
        lax.all_to_all(part_gate, "expert", split_axis=0, concat_axis=0, tiled=True),
        lax.all_to_all(part_up, "expert", split_axis=0, concat_axis=0, tiled=True),
        lax.all_to_all(part_down, "expert", split_axis=0, concat_axis=0, tiled=True),
    )
    experts = w_gate.shape[0]
    owners = (slot_expert[:, None] == jnp.arange(experts, dtype=jnp.int32)[None, :]).astype(
        jnp.float32
    )
    results = []
    for received in returned:
        blocks = received.reshape(slot_count, -1, width).astype(jnp.float32)
        summed = jnp.einsum("se,sfd->efd", owners, blocks, precision=lax.Precision.HIGHEST)
        results.append(summed.astype(jnp.bfloat16))
    return (mixed, grad_tokens, results[0], results[1], results[2])


def solution(mesh):
    placed = (
        P("dp", "mp"),
        P("dp", None),
        P("dp", None),
        P(),
        P(None, ("dp", "expert"), "mp"),
        P(None, ("dp", "expert"), "mp"),
        P(None, ("dp", "expert"), "mp"),
        P("dp", "mp"),
    )
    return jax.shard_map(
        body,
        mesh=mesh,
        in_specs=placed,
        out_specs=(
            P("dp", "mp"),
            P("dp", "mp"),
            P(None, ("dp", "expert"), "mp"),
            P(None, ("dp", "expert"), "mp"),
            P(None, ("dp", "expert"), "mp"),
        ),
        check_vma=False,
    )
```

profile of v0, /device:TPU:6, one launch (start us, length us, event | category | flops | bytes accessed | tf_op | source)
XLA Modules:
  0.0 413.3 jit_solution(12547623237573192888)
XLA Ops:
  7.2 0.7 fusion.31
  8.0 0.1 copy.53
  8.1 0.1 reshape.111
  8.2 0.3 reduce-window.9
  8.5 0.1 slice.7
  8.6 0.1 reshape.107
  8.8 0.1 slice_reduce_fusion
  8.9 0.1 broadcast.57
  9.0 0.1 reshape.109
  9.2 1.8 convolution_convert_fusion.12
  11.0 0.7 compare_and_fusion
  11.7 0.7 compare_select_fusion
  12.3 0.6 gather_fusion.2
  13.0 0.6 gather_fusion.1
  13.6 1.6 gather_fusion
  15.2 1.6 broadcast_select_fusion
  16.9 36.0 %all_to_all.64 = bf16[8,56,1024]{2,1,0:T(8,128)(2,1)S(1)} all-to-all(bf16[8,56,1024]{2,1,0:T(8,128)(2,1)S(1)} %get-tuple-element.39), channel_id=1, replica_groups=mesh['dp'=16,'expert'=8,'mp'=4] {'expert'}, dimensions={0} | all-to-all | bytes 1835008 | tf_op jit(solution)/shard_map/all_to_all | solution.py:57
  52.9 3.7 all-to-all-start
  56.6 0.1 copy.55
  56.8 0.1 eq.57
  56.9 0.1 copy.56
  57.0 0.1 reshape.145
  57.3 0.1 convolution_bitcast_fusion
  57.4 0.8 fusion.9
  58.2 23.0 %all-to-all-done = bf16[8,56,1024]{2,1,0:T(8,128)(2,1)S(1)} async-done(((bf16[8,56,1024]{2,1,0:T(8,128)(2,1)}), bf16[8,56,1024]{2,1,0:T(8,128)(2,1)S(1)}, u32[]{:S(2)}, u32[]{:S(2)}) %all-to-all-start) | async-done | bytes 917536 | tf_op jit(solution)/shard_map/all_to_all | solution.py:56
  81.3 3.6 all-to-all-start.2
  84.9 3.2 convolution_convert_fusion.6
  88.1 1.7 convolution_convert_fusion.5
  89.9 19.8 %all-to-all-done.2 = bf16[8,56,1024]{2,1,0:T(8,128)(2,1)S(1)} async-done(((bf16[8,56,1024]{2,1,0:T(8,128)(2,1)}), bf16[8,56,1024]{2,1,0:T(8,128)(2,1)S(1)}, u32[]{:S(2)}, u32[]{:S(2)}) %all-to-all-start.2) | async-done | bytes 917536 | tf_op jit(solution)/shard_map/all_to_all | solution.py:58
  109.7 3.4 convolution_convert_fusion.4
  113.2 58.6 %all-reduce.7.cloned.1.call-done = (bf16[640,448]{0,1:T(8,128)(2,1)}, bf16[640,448]{0,1:T(8,128)(2,1)}, bf16[640,448]{0,1:T(8,128)(2,1)}) async-done(((bf16[640,448]{0,1:T(8,128)(2,1)}, bf16[640,448]{0,1:T(8,128)(2,1)}, bf16[640,448]{0,1:T(8,128)(2,1)}), (bf16[640,448]{0,1:T(8,128)(2,1)}, bf16[640,448]{0,1:T(8,128)(2,1)}, bf16[640,448]{0,1:T(8,128)(2,1)})) %all-reduce.7.cloned.1.call-update) | async-done | bytes 1720336 | tf_op jit(solution)/shard_map/psum | solution.py:20
  171.8 1.6 fusion
  173.4 1.8 convolution_convert_fusion.1
  175.3 7.5 %all-to-all-start.7 = ((bf16[8,56,1024]{2,1,0:T(8,128)(2,1)}), bf16[8,56,1024]{2,1,0:T(8,128)(2,1)S(1)}, u32[]{:S(2)}, u32[]{:S(2)}) async-start(bf16[8,56,1024]{2,1,0:T(8,128)(2,1)} %bitcast.11), calls=%async_computation.7 | async-start | bytes 1835008 | tf_op jit(solution)/shard_map/all_to_all | solution.py:124
  182.8 3.5 convolution_convert_fusion.3
  186.3 22.1 %all-to-all-done.7 = bf16[8,56,1024]{2,1,0:T(8,128)(2,1)S(1)} async-done(((bf16[8,56,1024]{2,1,0:T(8,128)(2,1)}), bf16[8,56,1024]{2,1,0:T(8,128)(2,1)S(1)}, u32[]{:S(2)}, u32[]{:S(2)}) %all-to-all-start.7) | async-done | bytes 917536 | tf_op jit(solution)/shard_map/all_to_all | solution.py:124
  208.4 3.6 all-to-all-start.5
  211.9 0.2 copy.57
  212.2 3.2 convolution_convert_fusion
  215.4 22.8 %all-to-all-done.5 = bf16[8,56,1024]{2,1,0:T(8,128)(2,1)S(1)} async-done(((bf16[8,56,1024]{2,1,0:T(8,128)(2,1)}), bf16[8,56,1024]{2,1,0:T(8,128)(2,1)S(1)}, u32[]{:S(2)}, u32[]{:S(2)}) %all-to-all-start.5) | async-done | bytes 917536 | tf_op jit(solution)/shard_map/all_to_all | solution.py:122
  238.2 0.9 copy-done.3
  239.2 6.8 %all-to-all-start.3 = ((bf16[16,40,1024]{2,1,0:T(8,128)(2,1)}), bf16[16,40,1024]{2,1,0:T(8,128)(2,1)S(1)}, u32[]{:S(2)}, u32[]{:S(2)}) async-start(bf16[16,40,1024]{2,1,0:T(8,128)(2,1)} %convolution_convert_fusion), calls=%async_computation.3 | async-start | bytes 2621440 | tf_op jit(solution)/shard_map/all_to_all | solution.py:25
  246.0 2.7 fusion.29
  248.7 2.1 add_convert_fusion
  250.8 27.4 %all-to-all-done.3 = bf16[16,40,1024]{2,1,0:T(8,128)(2,1)S(1)} async-done(((bf16[16,40,1024]{2,1,0:T(8,128)(2,1)}), bf16[16,40,1024]{2,1,0:T(8,128)(2,1)S(1)}, u32[]{:S(2)}, u32[]{:S(2)}) %all-to-all-start.3) | async-done | bytes 1310752 | tf_op jit(solution)/shard_map/all_to_all | solution.py:25
  278.2 4.9 %all-to-all-start.4 = ((bf16[16,40,1024]{2,1,0:T(8,128)(2,1)}), bf16[16,40,1024]{2,1,0:T(8,128)(2,1)S(1)}, u32[]{:S(2)}, u32[]{:S(2)}) async-start(bf16[16,40,1024]{2,1,0:T(8,128)(2,1)} %bitcast.39), calls=%async_computation.4 | async-start | bytes 2621440 | tf_op jit(solution)/shard_map/all_to_all | solution.py:25
  283.1 3.5 convolution_convert_fusion.2
  286.6 28.7 %all-to-all-done.4 = bf16[16,40,1024]{2,1,0:T(8,128)(2,1)S(1)} async-done(((bf16[16,40,1024]{2,1,0:T(8,128)(2,1)}), bf16[16,40,1024]{2,1,0:T(8,128)(2,1)S(1)}, u32[]{:S(2)}, u32[]{:S(2)}) %all-to-all-start.4) | async-done | bytes 1310752 | tf_op jit(solution)/shard_map/all_to_all | solution.py:25
  315.3 4.2 %all-to-all-start.6 = ((bf16[8,56,1024]{2,1,0:T(8,128)(2,1)}), bf16[8,56,1024]{2,1,0:T(8,128)(2,1)}, u32[]{:S(2)}, u32[]{:S(2)}) async-start(bf16[8,56,1024]{2,1,0:T(8,128)(2,1)} %bitcast.46), calls=%async_computation.6 | async-start | bytes 1835008 | tf_op jit(solution)/shard_map/all_to_all | solution.py:123
  319.5 0.2 all-reduce.5.cloned.1.call-start
  319.7 0.2 convert_reduce_fusion.1
  320.0 0.2 convert_reduce_fusion
  320.3 1.3 convolution_convert_fusion.10
  321.6 1.4 convolution_convert_fusion.11
  323.0 0.7 convolution_convert_fusion.7
  323.7 0.9 copy.63
  324.6 0.7 convolution_convert_fusion.9
  325.2 0.9 copy.61
  326.1 21.3 %all-to-all-done.6 = bf16[8,56,1024]{2,1,0:T(8,128)(2,1)} async-done(((bf16[8,56,1024]{2,1,0:T(8,128)(2,1)}), bf16[8,56,1024]{2,1,0:T(8,128)(2,1)}, u32[]{:S(2)}, u32[]{:S(2)}) %all-to-all-start.6) | async-done | bytes 917536 | tf_op jit(solution)/shard_map/all_to_all | solution.py:123
  347.4 1.8 convolution_convert_fusion.8
  349.3 0.9 copy.62
  350.2 53.3 %all-reduce.5.cloned.1.call-done = (bf16[128,1024]{1,0:T(8,128)(2,1)}, bf16[128,1024]{1,0:T(8,128)(2,1)}) async-done(((bf16[128,1024]{1,0:T(8,128)(2,1)}, bf16[128,1024]{1,0:T(8,128)(2,1)}), (bf16[128,1024]{1,0:T(8,128)(2,1)}, bf16[128,1024]{1,0:T(8,128)(2,1)})) %all-reduce.5.cloned.1.call-update) | async-done | bytes 524304 | tf_op jit(solution)/shard_map/psum | solution.py:32
  403.5 1.7 copy.75
  405.1 1.7 copy.76
  (54 shorter events, 0.5 us)
Async XLA Ops:
  7.2 5.2 %copy-start = (bf16[4,56,1024]{2,1,0:T(8,128)(2,1)S(1)}, bf16[4,56,1024]{2,1,0:T(8,128)(2,1)}, u32[]{:S(2)}) copy-start(bf16[4,56,1024]{2,1,0:T(8,128)(2,1)} %param.16) | copy-start | bytes 1376260
  7.2 77.7 %all-gather.3.cloned.1.call-start = ((), (), s32[]{:S(2)}) async-start(), calls=%async_computation.8 | async-start | bytes 1392640 | tf_op jit(solution)/shard_map/all_gather | solution.py:16
  9.2 3.8 copy-start.5
  52.9 35.2 %copy-start.6 = (bf16[8,56,1024]{2,1,0:T(8,128)(2,1)}, bf16[8,56,1024]{2,1,0:T(8,128)(2,1)S(1)}, u32[]{:S(2)}) copy-start(bf16[8,56,1024]{2,1,0:T(8,128)(2,1)S(1)} %all_to_all.64) | copy-start | bytes 2752516
  52.9 4.0 copy-start.16
  52.9 4.5 %copy-start.14 = (bf16[128,1024]{1,0:T(8,128)(2,1)S(1)}, bf16[128,1024]{1,0:T(8,128)(2,1)}, u32[]{:S(2)}) copy-start(bf16[128,1024]{1,0:T(8,128)(2,1)} %param.17) | copy-start | bytes 786436
  52.9 28.4 %all-to-all-start = ((bf16[8,56,1024]{2,1,0:T(8,128)(2,1)}), bf16[8,56,1024]{2,1,0:T(8,128)(2,1)S(1)}, u32[]{:S(2)}, u32[]{:S(2)}) async-start(bf16[8,56,1024]{2,1,0:T(8,128)(2,1)} %get-tuple-element.40), calls=%async_computation | async-start | bytes 1835008 | tf_op jit(solution)/shard_map/all_to_all | solution.py:56
  56.6 53.1 %all-gather.5.cloned.1.call-start = ((), (), s32[]{:S(2)}) async-start(), calls=%async_computation.9 | async-start | bytes 1392640 | tf_op jit(solution)/shard_map/all_gather | solution.py:16
  81.3 6.8 %copy-start.8 = (bf16[8,56,1024]{2,1,0:T(8,128)(2,1)}, bf16[8,56,1024]{2,1,0:T(8,128)(2,1)S(1)}, u32[]{:S(2)}) copy-start(bf16[8,56,1024]{2,1,0:T(8,128)(2,1)S(1)} %all-to-all-done) | copy-start | bytes 2752516
  81.3 28.4 %all-to-all-start.2 = ((bf16[8,56,1024]{2,1,0:T(8,128)(2,1)}), bf16[8,56,1024]{2,1,0:T(8,128)(2,1)S(1)}, u32[]{:S(2)}, u32[]{:S(2)}) async-start(bf16[8,56,1024]{2,1,0:T(8,128)(2,1)} %get-tuple-element.38), calls=%async_computation.2 | async-start | bytes 1835008 | tf_op jit(solution)/shard_map/all_to_all | solution.py:58
  84.8 87.0 %all-reduce.7.cloned.1.call-start = ((), (), s32[]{:S(2)}) async-start(), calls=%async_computation.11 | async-start | bytes 3440640 | tf_op jit(solution)/shard_map/psum | solution.py:20
  84.9 3.2 copy-start.17
  109.7 3.5 copy-start.10
  113.2 60.2 %copy-start.18 = (bf16[640,1024]{1,0:T(8,128)(2,1)S(1)}, bf16[640,1024]{1,0:T(8,128)(2,1)}, u32[]{:S(2)}) copy-start(bf16[640,1024]{1,0:T(8,128)(2,1)} %all-gather.5.cloned.1.call-done) | copy-start | bytes 3932164
  175.3 7.5 %copy-start.11 = (bf16[640,448]{0,1:T(8,128)(2,1)S(1)}, bf16[640,448]{0,1:T(8,128)(2,1)}, u32[]{:S(2)}) copy-start(bf16[640,448]{0,1:T(8,128)(2,1)} %get-tuple-element.34) | copy-start | bytes 1720324
  175.3 7.5 %copy-start.13 = (bf16[640,448]{0,1:T(8,128)(2,1)S(1)}, bf16[640,448]{0,1:T(8,128)(2,1)}, u32[]{:S(2)}) copy-start(bf16[640,448]{0,1:T(8,128)(2,1)} %get-tuple-element.33) | copy-start | bytes 1720324
  175.3 33.1 %all-to-all-start.7 = ((bf16[8,56,1024]{2,1,0:T(8,128)(2,1)}), bf16[8,56,1024]{2,1,0:T(8,128)(2,1)S(1)}, u32[]{:S(2)}, u32[]{:S(2)}) async-start(bf16[8,56,1024]{2,1,0:T(8,128)(2,1)} %bitcast.11), calls=%async_computation.7 | async-start | bytes 1835008 | tf_op jit(solution)/shard_map/all_to_all | solution.py:124
  208.4 3.8 copy-start.1
  208.4 29.9 %all-to-all-start.5 = ((bf16[8,56,1024]{2,1,0:T(8,128)(2,1)}), bf16[8,56,1024]{2,1,0:T(8,128)(2,1)S(1)}, u32[]{:S(2)}, u32[]{:S(2)}) async-start(bf16[8,56,1024]{2,1,0:T(8,128)(2,1)} %bitcast.47), calls=%async_computation.5 | async-start | bytes 1835008 | tf_op jit(solution)/shard_map/all_to_all | solution.py:122
  215.4 30.6 %copy-start.9 = (bf16[8,56,1024]{2,1,0:T(8,128)(2,1)S(1)}, bf16[8,56,1024]{2,1,0:T(8,128)(2,1)}, u32[]{:S(2)}) copy-start(bf16[8,56,1024]{2,1,0:T(8,128)(2,1)} %copy-done.8) | copy-start | bytes 2752516
  238.2 0.9 copy-start.3
  239.2 39.0 %all-to-all-start.3 = ((bf16[16,40,1024]{2,1,0:T(8,128)(2,1)}), bf16[16,40,1024]{2,1,0:T(8,128)(2,1)S(1)}, u32[]{:S(2)}, u32[]{:S(2)}) async-start(bf16[16,40,1024]{2,1,0:T(8,128)(2,1)} %convolution_convert_fusion), calls=%async_computation.3 | async-start | bytes 2621440 | tf_op jit(solution)/shard_map/all_to_all | solution.py:25
  246.0 2.7 copy-start.7
  246.0 2.7 copy-start.12
  246.0 2.7 copy-start.19
  278.2 37.1 %all-to-all-start.4 = ((bf16[16,40,1024]{2,1,0:T(8,128)(2,1)}), bf16[16,40,1024]{2,1,0:T(8,128)(2,1)S(1)}, u32[]{:S(2)}, u32[]{:S(2)}) async-start(bf16[16,40,1024]{2,1,0:T(8,128)(2,1)} %bitcast.39), calls=%async_computation.4 | async-start | bytes 2621440 | tf_op jit(solution)/shard_map/all_to_all | solution.py:25
  315.3 32.2 %all-to-all-start.6 = ((bf16[8,56,1024]{2,1,0:T(8,128)(2,1)}), bf16[8,56,1024]{2,1,0:T(8,128)(2,1)}, u32[]{:S(2)}, u32[]{:S(2)}) async-start(bf16[8,56,1024]{2,1,0:T(8,128)(2,1)} %bitcast.46), calls=%async_computation.6 | async-start | bytes 1835008 | tf_op jit(solution)/shard_map/all_to_all | solution.py:123
  319.5 83.9 %all-reduce.5.cloned.1.call-start = ((), (), s32[]{:S(2)}) async-start(), calls=%async_computation.10 | async-start | bytes 1048576 | tf_op jit(solution)/shard_map/psum | solution.py:32
  320.0 3.0 copy-start.2
  320.0 3.0 copy-start.15
  323.0 1.6 copy-start.4
Sparse Core Ops, SparseCore 0:
  11.1 45.7 all-gather.2
  60.1 42.5 all-gather.4
  113.3 58.4 all-reduce.6
  323.1 80.3 all-reduce.4
where the time goes:
time: 414 us; the launch traced here: 413 us
  waiting for transfers between devices  277 us (67%)
  blocking collectives  36 us (9%)
  starting transfers between devices  34.6 us (8%)
  matrix products  33.8 us (8%)
  between operations  14.1 us (3%)
  local copies, waits for them, and re-layouts  11.5 us (3%)
  other arithmetic  6.24 us (2%)
    psum x1, waiting for transfers between devices, sum_features(): lax.psum(as_sent(partials), 'mp')  58.6 us
    all_to_all x2, waiting for transfers between devices, send_back(): lax.all_to_all(blocks.astype(jnp.bfloat16), 'dp', split_axis=0, concat_ax...  56.1 us
    psum x1, waiting for transfers between devices, token_total(): lax.psum(partial_value.astype(jnp.bfloat16), 'expert').astype(jnp.float32)  53.3 us
    all_to_all x1, blocking collectives, body(): lax.all_to_all(stack_up, 'expert', split_axis=0, concat_axis=1, tiled=True)  36 us
    all_to_all x1, waiting for transfers between devices, body(): lax.all_to_all(stack_gate, 'expert', split_axis=0, concat_axis=1, tiled=T...  23 us
    all_to_all x1, waiting for transfers between devices, body(): lax.all_to_all(part_gate, 'expert', split_axis=0, concat_axis=0, tiled=True)  22.8 us
    all_to_all x1, waiting for transfers between devices, body(): lax.all_to_all(part_down, 'expert', split_axis=0, concat_axis=0, tiled=True)  22.1 us
    all_to_all x1, waiting for transfers between devices, body(): lax.all_to_all(part_up, 'expert', split_axis=0, concat_axis=0, tiled=True)  21.3 us
  transfers between devices with their start and end apart: 11, of which 9 were waited for; matrix products, arithmetic and copies ran while one was open for 9% of the time, Pallas kernels for 0%

commit v1 on v0

v1 whole, which is shorter than its diff:
```python
import jax
import jax.numpy as jnp
from jax import lax
from jax.sharding import Mesh, PartitionSpec as P

F32 = jnp.float32
BF16 = jnp.bfloat16


def short(value):
    return lax.reduce_precision(value, exponent_bits=8, mantissa_bits=7)


def swap_cores(value):
    return lax.ppermute(value, "core", [(0, 1), (1, 0)])


def contract_last(left, right):
    return lax.dot_general(left, right, (((1,), (1,)), ((), ())), preferred_element_type=F32)


def contract_first(left, right):
    return lax.dot_general(left, right, (((0,), (0,)), ((), ())), preferred_element_type=F32)


def spread(value, axis):
    count = lax.axis_size(axis)
    copies = jnp.broadcast_to(value[None], (count,) + value.shape)
    copies = lax.optimization_barrier(copies)
    return lax.all_to_all(copies, axis, split_axis=0, concat_axis=0, tiled=True)


def body(tokens, slot_ids, gate_values, slot_expert, w_gate, w_up, w_down, cotangent):
    rows, width = tokens.shape
    experts, units, _ = w_gate.shape
    ny, nz, nx = lax.axis_size("y"), lax.axis_size("z"), lax.axis_size("x")
    top = slot_ids.shape[1]
    total = ny * rows
    both = 2 * units

    chosen = jnp.sum(
        jnp.where(
            slot_ids[:, :, None] == jnp.arange(slot_expert.shape[0], dtype=jnp.int32),
            slot_expert[None, None, :],
            0,
        ),
        axis=-1,
    ).astype(F32)
    part0 = short(gate_values)
    part1 = short(gate_values - part0)
    part2 = short(gate_values - part0 - part1)
    meta = jnp.stack([chosen, part0, part1, part2]).transpose(0, 2, 1).astype(BF16)
    meta = jnp.pad(meta.reshape(1, 4 * top * rows), ((0, 15), (0, width - 4 * top * rows)))
    packed = jnp.concatenate([tokens, cotangent, meta], axis=0)
    held = packed.shape[0]
    everything = lax.all_gather(packed, "y", axis=0, tiled=True).reshape(ny, held, width)

    own = jnp.stack([w_gate, w_up, w_down])
    other = swap_cores(own)
    weights = jnp.concatenate([own, other], axis=2).reshape(3, experts * both, width)

    rows_x = everything[:, :rows].reshape(total, width)
    rows_c = everything[:, rows : 2 * rows].reshape(total, width)
    facts = everything[:, 2 * rows, : 4 * top * rows].reshape(ny, 4, top, rows).astype(F32)
    facts = facts.transpose(1, 2, 0, 3).reshape(4, top, total)
    expert_of = facts[0]
    scale = facts[1] + facts[2] + facts[3]
    mask = expert_of[None] == jnp.arange(experts, dtype=F32)[:, None, None]

    def pick(weight, values):
        sums = contract_last(weight, values).astype(BF16).reshape(experts, both, total)
        return [
            sum(
                jnp.where(mask[e, k][None], sums[e], jnp.zeros((), BF16)) for e in range(experts)
            )
            for k in range(top)
        ]

    picked = jnp.stack(
        pick(weights[0], rows_x) + pick(weights[1], rows_x) + pick(weights[2], rows_c)
    )
    share = total // nx
    picked = picked.reshape(3 * top * both, nx, share).transpose(1, 0, 2)
    arrived = lax.all_to_all(picked, "x", split_axis=0, concat_axis=0, tiled=True)
    summed = jnp.sum(arrived.astype(F32), axis=0).reshape(3, top, both, share)
    gate, up, dh = summed[0], summed[1], summed[2]
    own_scale = lax.dynamic_slice_in_dim(scale, lax.axis_index("x") * share, share, axis=1)[:, None]
    dh = own_scale * dh
    sg = jax.nn.sigmoid(gate)
    active = gate * sg
    hidden = own_scale * (active * up)
    dgate = dh * up * sg * (1.0 + gate * (1.0 - sg))
    dup = dh * active
    mine = jnp.stack([hidden, dgate, dup]).astype(BF16).reshape(3 * top * both, share)
    shared = spread(mine, "x").reshape(nx, 3, top, both, share)

    def expand(which):
        values = shared[:, which].transpose(1, 2, 0, 3).reshape(top, both, total)
        wide = [
            sum(jnp.where(mask[e, k][None], values[k], jnp.zeros((), BF16)) for k in range(top))
            for e in range(experts)
        ]
        return jnp.stack(wide).reshape(experts * both, total)

    hidden_all, dgate_all, dup_all = expand(0), expand(1), expand(2)
    mixed_part = contract_first(hidden_all, weights[2]).astype(BF16)
    mixed_y = lax.psum_scatter(mixed_part, "y", scatter_dimension=0, tiled=True)
    back_part = (
        contract_first(dgate_all, weights[0]) + contract_first(dup_all, weights[1])
    ).astype(BF16)
    back = lax.all_to_all(
        back_part.reshape(ny * nz, rows // nz, width),
        ("y", "z"),
        split_axis=0,
        concat_axis=0,
        tiled=True,
    )
    back = jnp.sum(back.astype(F32), axis=0)
    mixed = lax.all_to_all(
        mixed_y.reshape(nz, rows // nz, width), "z", split_axis=0, concat_axis=0, tiled=True
    )
    mixed = jnp.sum(mixed.astype(F32), axis=0)
    ends = spread(jnp.stack([mixed, back]).astype(BF16), "z")
    mixed_out = ends[:, 0].reshape(rows, width)
    back_out = ends[:, 1].reshape(rows, width)

    def weight_gradient(left, right):
        part = jnp.dot(left, right, preferred_element_type=F32)
        return part.reshape(experts, 2, units, width)

    parts = [
        weight_gradient(dgate_all, rows_x),
        weight_gradient(dup_all, rows_x),
        weight_gradient(hidden_all, rows_c),
    ]
    sent = swap_cores(jnp.stack([part[:, 1] for part in parts]).astype(BF16))
    gradients = [
        (part[:, 0].astype(BF16).astype(F32) + sent[i].astype(F32)).astype(BF16) for i, part in enumerate(parts)
    ]
    return (mixed_out, back_out, gradients[0], gradients[1], gradients[2])


def solution(mesh):
    dp, ep, mp = mesh.shape["dp"], mesh.shape["expert"], mesh.shape["mp"]
    split = Mesh(mesh.devices.reshape(dp // 2, 2, ep, mp), ("y", "core", "z", "x"))
    rows = ("y", "core")
    stored = P(None, ("y", "core", "z"), "x")
    return jax.shard_map(
        body,
        mesh=split,
        in_specs=(
            P(rows, "x"),
            P(rows, None),
            P(rows, None),
            P(),
            stored,
            stored,
            stored,
            P(rows, "x"),
        ),
        out_specs=(P(rows, "x"), P(rows, "x"), stored, stored, stored),
        check_vma=False,
    )
```

time: 414 us -> 277 us (0.67)
  waiting for transfers between devices: 277 us -> 153 us
  matrix products: 33.8 us -> 13.6 us
  blocking collectives: 36 us -> 20.1 us
  other arithmetic: 6.24 us -> 20.2 us
  local copies, waits for them, and re-layouts: 11.5 us -> 24 us
  starting transfers between devices: 34.6 us -> 30.2 us
    psum x2 -> x0, waiting for transfers between devices: 112 us -> none  [the longest x1 58.6 us: sum_features(): lax.psum(as_sent(partials), 'mp')]
    all_to_all x7 -> x4, waiting for transfers between devices: 165 us -> 91.7 us  [the longest x1 52.9 us: body(): lax.all_to_all(back_part.reshape(ny * nz, rows // nz, width), ('y', 'z'),...]
    all_gather x2 -> x1, waiting for transfers between devices: 0.02 us -> 58.6 us  [body(): lax.all_gather(packed, 'y', axis=0, tiled=True).reshape(ny, held, width)]
    all_to_all x1, blocking collectives: 36 us -> 20.1 us  [spread(): return lax.all_to_all(copies, axis, split_axis=0, concat_axis=0, tiled=True)]
    dot_general x11 -> x3, matrix products: 16.5 us -> 3.39 us  [weight_gradient(): part = jnp.dot(left, right, preferred_element_type=F32)]
    squeeze x0 -> x12, local copies, waits for them, and re-layouts: none -> 8.19 us  [expand(): values[k]]
    all_to_all x7 -> x4, starting transfers between devices: 34.2 us -> 26.3 us  [the longest x1 11.2 us: body(): lax.all_to_all(back_part.reshape(ny * nz, rows // nz, width), ('y', 'z'),...]
    slice x1 -> x9, local copies, waits for them, and re-layouts: 0.07 us -> 5.32 us  [the longest x1 2.7 us: body(): rows_c = everything[:, rows:2 * rows].reshape(total, width)]
  transfers between devices with their start and end apart: 11 -> 8, of which waited for: 9 -> 6; matrix products, arithmetic and copies ran while one was open for 9% -> 8% of each run, Pallas kernels for 0% -> 0%
where the time goes in v1:
time: 277 us; the launch traced here: 276 us
  waiting for transfers between devices  153 us (55%)
  starting transfers between devices  30.2 us (11%)
  local copies, waits for them, and re-layouts  24 us (9%)
  other arithmetic  20.2 us (7%)
  blocking collectives  20.1 us (7%)
  between operations  14.6 us (5%)
  matrix products  13.6 us (5%)
    all_gather x1, waiting for transfers between devices, body(): lax.all_gather(packed, 'y', axis=0, tiled=True).reshape(ny, held, width)  58.6 us
    all_to_all x1, waiting for transfers between devices, body(): lax.all_to_all(back_part.reshape(ny * nz, rows // nz, width), ('y', 'z'),...  52.9 us
    all_to_all x1, blocking collectives, spread(): return lax.all_to_all(copies, axis, split_axis=0, concat_axis=0, tiled=True)  20.1 us
    all_to_all x1, waiting for transfers between devices, body(): lax.all_to_all(picked, 'x', split_axis=0, concat_axis=0, tiled=True)  16.5 us
    all_to_all x1, waiting for transfers between devices, spread(): return lax.all_to_all(copies, axis, split_axis=0, concat_axis=0, tiled=True)  12.1 us
    all_to_all x1, starting transfers between devices, body(): lax.all_to_all(back_part.reshape(ny * nz, rows // nz, width), ('y', 'z'),...  11.2 us
    all_to_all x1, waiting for transfers between devices, body(): lax.all_to_all(mixed_y.reshape(nz, rows // nz, width), 'z', split_axis=0,...  10.2 us
    squeeze x12, local copies, waits for them, and re-layouts, expand(): values[k]  8.19 us
  transfers between devices with their start and end apart: 8, of which 6 were waited for; matrix products, arithmetic and copies ran while one was open for 8% of the time, Pallas kernels for 0%

profile of v1, /device:TPU:6, one launch (start us, length us, event | category | flops | bytes accessed | tf_op | source)
XLA Modules:
  0.0 276.1 jit_solution(1550793357931221704)
XLA Ops:
  7.2 0.9 select_reduce_fusion
  8.1 0.7 fusion.19
  8.8 1.9 fusion.13
  10.9 1.9 collective-permute-start
  12.9 3.1 %collective-permute-done = bf16[3,4,56,1024]{3,2,1,0:T(8,128)(2,1)S(1)} collective-permute-done((bf16[3,4,56,1024]{3,2,1,0:T(8,128)(2,1)S(1)}, bf16[3,4,56,1024]{3,2,1,0:T(8,128)(2,1)S(1)}, u32[]{:S(2)}, u32[]{:S(2)}) %collective-permute-start) | collective-permute-done | bytes 1376288 | tf_op jit(solution)/shard_map/ppermute | solution.py:15
  16.0 0.2 pad_maximum_fusion
  16.2 0.3 fusion.24
  16.5 58.6 %all-gather.2.cloned.1.call-done = bf16[2176,1024]{1,0:T(8,128)(2,1)} async-done(((bf16[272,1024]{1,0:T(8,128)(2,1)}), bf16[2176,1024]{1,0:T(8,128)(2,1)}) %all-gather.2.cloned.1.call-update) | async-done | bytes 4456464 | tf_op jit(solution)/shard_map/all_gather | solution.py:56
  75.1 0.9 slice_convert_fusion
  76.0 2.7 fusion.23
  78.9 1.2 convolution_convert_fusion.5
  80.1 1.2 convolution_convert_fusion.6
  81.3 0.9 bitcast_dynamic-update-slice_fusion.5
  82.2 0.9 bitcast_dynamic-update-slice_fusion.4
  83.1 0.9 bitcast_dynamic-update-slice_fusion.3
  84.0 0.9 bitcast_dynamic-update-slice_fusion.2
  84.8 1.2 convolution_convert_fusion.4
  86.0 0.9 bitcast_dynamic-update-slice_fusion.1
  86.9 0.9 bitcast_dynamic-update-slice_fusion
  87.8 3.0 %reshape.1485 = bf16[672,4,256]{2,1,0:T(4,128)(2,1)S(1)} reshape(bf16[6,112,1024]{2,1,0:T(8,128)(2,1)} %bitcast_dynamic-update-slice_fusion) | data formatting | bytes 2752512 | tf_op jit(solution)/shard_map/reshape | solution.py:83
  90.8 1.3 copy.49
  92.1 4.8 %all-to-all-start = ((bf16[4,672,256]{2,1,0:T(8,128)(2,1)}), bf16[4,672,256]{2,1,0:T(8,128)(2,1)S(1)}, u32[]{:S(2)}, u32[]{:S(2)}) async-start(bf16[4,672,256]{2,1,0:T(8,128)(2,1)} %bitcast.125), calls=%async_computation | async-start | bytes 2752512 | tf_op jit(solution)/shard_map/all_to_all | solution.py:84
  96.9 16.5 %all-to-all-done = bf16[4,672,256]{2,1,0:T(8,128)(2,1)S(1)} async-done(((bf16[4,672,256]{2,1,0:T(8,128)(2,1)}), bf16[4,672,256]{2,1,0:T(8,128)(2,1)S(1)}, u32[]{:S(2)}, u32[]{:S(2)}) %all-to-all-start) | async-done | bytes 1376288 | tf_op jit(solution)/shard_map/all_to_all | solution.py:84
  113.4 0.2 convert_reduce_fusion
  114.0 20.1 %all_to_all.25 = bf16[4,672,256]{2,1,0:T(8,128)(2,1)S(1)} all-to-all(bf16[4,672,256]{2,1,0:T(8,128)(2,1)S(1)} %broadcast_in_dim.314), channel_id=1, replica_groups=mesh['y'=8,'core'=2,'z'=8,'x'=4] {'x'}, dimensions={0} | all-to-all | bytes 2752512 | tf_op jit(solution)/shard_map/all_to_all | solution.py:30
  134.1 0.9 fusion.25
  135.0 0.4 copy.50
  135.3 0.2 fusion.28
  135.5 0.8 squeeze.49
  136.3 0.8 squeeze.50
  137.2 1.7 copy_bitcast_fusion.1
  138.9 0.2 fusion.30
  139.1 0.8 squeeze.55
  139.9 0.8 squeeze.56
  141.2 2.3 select_add_fusion.15
  143.7 1.1 copy-done.26
  144.8 2.7 convolution_convert_fusion
  147.5 0.9 copy-done.11
  148.8 0.2 copy-done.24
  149.0 1.3 fusion.31
  150.5 2.8 add_convert_fusion
  153.2 11.2 %all-to-all-start.3 = ((bf16[64,16,1024]{2,1,0:T(8,128)(2,1)}), bf16[64,16,1024]{2,1,0:T(8,128)(2,1)S(1)}, u32[]{:S(2)}, u32[]{:S(2)}) async-start(bf16[64,16,1024]{2,1,0:T(8,128)(2,1)} %bitcast.127), calls=%async_computation.4 | async-start | bytes 4194304 | tf_op jit(solution)/shard_map/all_to_all | solution.py:111
  164.5 0.8 squeeze.61
  165.3 0.8 squeeze.62
  166.1 0.8 squeeze.59
  167.1 1.1 squeeze.57
  168.2 0.8 squeeze.58
  169.1 1.7 select_add_fusion.3
  170.9 1.1 convolution_convert_fusion.1
  172.1 0.4 copy-done.1
  172.5 1.1 convolution_convert_fusion.3
  173.7 1.1 convolution_convert_fusion.2
  174.9 1.3 pad_maximum_fusion.2
  176.2 1.9 collective-permute-start.1
  178.1 52.9 %all-to-all-done.3 = bf16[64,16,1024]{2,1,0:T(8,128)(2,1)S(1)} async-done(((bf16[64,16,1024]{2,1,0:T(8,128)(2,1)}), bf16[64,16,1024]{2,1,0:T(8,128)(2,1)S(1)}, u32[]{:S(2)}, u32[]{:S(2)}) %all-to-all-start.3) | async-done | bytes 2097184 | tf_op jit(solution)/shard_map/all_to_all | solution.py:111
  231.0 6.8 %all-to-all-start.2 = ((bf16[8,16,1024]{2,1,0:T(8,128)(2,1)}), bf16[8,16,1024]{2,1,0:T(8,128)(2,1)}, u32[]{:S(2)}, u32[]{:S(2)}) async-start(bf16[8,16,1024]{2,1,0:T(8,128)(2,1)} %bitcast.157), calls=%async_computation.3 | async-start | bytes 524288 | tf_op jit(solution)/shard_map/all_to_all | solution.py:119
  237.8 0.4 reduce.1
  238.2 10.2 %all-to-all-done.2 = bf16[8,16,1024]{2,1,0:T(8,128)(2,1)} async-done(((bf16[8,16,1024]{2,1,0:T(8,128)(2,1)}), bf16[8,16,1024]{2,1,0:T(8,128)(2,1)}, u32[]{:S(2)}, u32[]{:S(2)}) %all-to-all-start.2) | async-done | bytes 262176 | tf_op jit(solution)/shard_map/all_to_all | solution.py:119
  248.4 1.0 reduce
  249.4 0.9 broadcast_in_dim.323
  250.3 3.5 %all-to-all-start.4 = ((bf16[8,2,16,1024]{3,2,1,0:T(8,128)(2,1)}), bf16[8,2,16,1024]{3,2,1,0:T(8,128)(2,1)S(1)}, u32[]{:S(2)}, u32[]{:S(2)}) async-start(bf16[8,2,16,1024]{3,2,1,0:T(8,128)(2,1)} %broadcast_in_dim.323), calls=%async_computation.5 | async-start | bytes 1048576 | tf_op jit(solution)/shard_map/all_to_all | solution.py:30
  253.8 2.6 fusion.8
  256.4 12.1 %all-to-all-done.4 = bf16[8,2,16,1024]{3,2,1,0:T(8,128)(2,1)S(1)} async-done(((bf16[8,2,16,1024]{3,2,1,0:T(8,128)(2,1)}), bf16[8,2,16,1024]{3,2,1,0:T(8,128)(2,1)S(1)}, u32[]{:S(2)}, u32[]{:S(2)}) %all-to-all-start.4) | async-done | bytes 524320 | tf_op jit(solution)/shard_map/all_to_all | solution.py:30
  268.4 0.8 fusion.27
  (79 shorter events, 2.4 us)
Async XLA Ops:
  7.2 3.6 %copy-start.5 = (bf16[4,56,1024]{2,1,0:T(8,128)(2,1)S(1)}, bf16[4,56,1024]{2,1,0:T(8,128)(2,1)}, u32[]{:S(2)}) copy-start(bf16[4,56,1024]{2,1,0:T(8,128)(2,1)} %param.14) | copy-start | bytes 1376260
  7.2 3.6 %copy-start.6 = (bf16[4,56,1024]{2,1,0:T(8,128)(2,1)S(1)}, bf16[4,56,1024]{2,1,0:T(8,128)(2,1)}, u32[]{:S(2)}) copy-start(bf16[4,56,1024]{2,1,0:T(8,128)(2,1)} %param.13) | copy-start | bytes 1376260
  7.2 3.6 %copy-start.7 = (bf16[4,56,1024]{2,1,0:T(8,128)(2,1)S(1)}, bf16[4,56,1024]{2,1,0:T(8,128)(2,1)}, u32[]{:S(2)}) copy-start(bf16[4,56,1024]{2,1,0:T(8,128)(2,1)} %param.12) | copy-start | bytes 1376260
  7.2 67.9 %all-gather.2.cloned.1.call-start = ((), (), s32[]{:S(2)}) async-start(), calls=%async_computation.6 | async-start | bytes 5013504 | tf_op jit(solution)/shard_map/all_gather | solution.py:56
  10.9 5.0 %collective-permute-start = (bf16[3,4,56,1024]{3,2,1,0:T(8,128)(2,1)S(1)}, bf16[3,4,56,1024]{3,2,1,0:T(8,128)(2,1)S(1)}, u32[]{:S(2)}, u32[]{:S(2)}) collective-permute-start(bf16[3,4,56,1024]{3,2,1,0:T(8,128)(2,1)S(1)} %pad_maximum_fusion.1), channel_id=1, source_target_pairs={{0,32},{32,0},{1,33},{33,1},{2,34},{34,2},{3,35},{35,3},{4,36},{36... | collective-permute-start | bytes 4128776 | tf_op jit(solution)/shard_map/ppermute | solution.py:15
  16.5 62.4 %copy-start.23 = (bf16[1,4,112,1024]{3,2,1,0:T(8,128)(2,1)}, bf16[1,4,112,1024]{3,2,1,0:T(8,128)(2,1)S(1)}, u32[]{:S(2)}) copy-start(bf16[1,4,112,1024]{3,2,1,0:T(8,128)(2,1)S(1)} %get-tuple-element.16) | copy-start | bytes 2752516
  16.5 68.3 %copy-start.25 = (bf16[1,4,112,1024]{3,2,1,0:T(8,128)(2,1)}, bf16[1,4,112,1024]{3,2,1,0:T(8,128)(2,1)S(1)}, u32[]{:S(2)}) copy-start(bf16[1,4,112,1024]{3,2,1,0:T(8,128)(2,1)S(1)} %get-tuple-element.15) | copy-start | bytes 2752516
  78.7 1.4 copy-start
  78.7 6.1 %copy-start.2 = (bf16[8,128,1024]{2,1,0:T(8,128)(2,1)}, bf16[8,128,1024]{2,1,0:T(8,128)(2,1)S(1)}, u32[]{:S(2)}) copy-start(bf16[8,128,1024]{2,1,0:T(8,128)(2,1)S(1)} %get-tuple-element.13) | copy-start | bytes 6291460
  92.1 21.3 %all-to-all-start = ((bf16[4,672,256]{2,1,0:T(8,128)(2,1)}), bf16[4,672,256]{2,1,0:T(8,128)(2,1)S(1)}, u32[]{:S(2)}, u32[]{:S(2)}) async-start(bf16[4,672,256]{2,1,0:T(8,128)(2,1)} %bitcast.125), calls=%async_computation | async-start | bytes 2752512 | tf_op jit(solution)/shard_map/all_to_all | solution.py:84
  96.9 134.1 %reduce-scatter.2.cloned.1.call-start = ((), (), s32[]{:S(2)}) async-start(), calls=%async_computation.7 | async-start | bytes 2359296 | tf_op jit(solution)/shard_map/reduce_scatter | solution.py:107
  139.1 2.2 copy-start.19
  139.1 2.2 copy-start.20
  140.9 6.5 %copy-start.4 = (bf16[1,112,4,256]{3,2,1,0:T(4,128)(2,1)}, bf16[1,112,4,256]{3,2,1,0:T(4,128)(2,1)S(1)}, u32[]{:S(2)}) copy-start(bf16[1,112,4,256]{3,2,1,0:T(4,128)(2,1)S(1)} %get-tuple-element.54) | copy-start | bytes 688132
  143.6 1.2 copy-start.26
  147.4 0.9 copy-start.11
  147.4 1.0 copy-start.12
  147.4 1.2 copy-start.13
  147.4 1.3 copy-start.14
  147.5 1.6 copy-start.24
  149.0 1.3 copy-start.8
  149.0 1.3 copy-start.9
  149.0 1.3 copy-start.10
  153.2 77.8 %all-to-all-start.3 = ((bf16[64,16,1024]{2,1,0:T(8,128)(2,1)}), bf16[64,16,1024]{2,1,0:T(8,128)(2,1)S(1)}, u32[]{:S(2)}, u32[]{:S(2)}) async-start(bf16[64,16,1024]{2,1,0:T(8,128)(2,1)} %bitcast.127), calls=%async_computation.4 | async-start | bytes 4194304 | tf_op jit(solution)/shard_map/all_to_all | solution.py:111
  165.3 3.7 %copy-start.21 = (bf16[1,2,56,1024]{3,2,1,0:T(8,128)(2,1)S(1)}, bf16[1,2,56,1024]{3,2,1,0:T(8,128)(2,1)}, u32[]{:S(2)}) copy-start(bf16[1,2,56,1024]{3,2,1,0:T(8,128)(2,1)} %squeeze.61) | copy-start | bytes 688132
  166.1 2.9 %copy-start.22 = (bf16[1,2,56,1024]{3,2,1,0:T(8,128)(2,1)S(1)}, bf16[1,2,56,1024]{3,2,1,0:T(8,128)(2,1)}, u32[]{:S(2)}) copy-start(bf16[1,2,56,1024]{3,2,1,0:T(8,128)(2,1)} %squeeze.62) | copy-start | bytes 688132
  169.1 1.8 copy-start.3
  170.9 1.6 copy-start.1
  172.0 1.6 copy-start.15
  173.6 1.2 copy-start.17
  174.8 1.4 copy-start.18
  176.2 77.6 %collective-permute-start.1 = (bf16[3,4,56,1024]{3,2,1,0:T(8,128)(2,1)}, bf16[3,4,56,1024]{3,2,1,0:T(8,128)(2,1)S(1)}, u32[]{:S(2)}, u32[]{:S(2)}) collective-permute-start(bf16[3,4,56,1024]{3,2,1,0:T(8,128)(2,1)} %pad_maximum_fusion.2), channel_id=1, source_target_pairs={{0,32},{32,0},{1,33},{33,1},{2,34},{34,2},{3,35},{35,3},{4,36},{36... | collective-permute-start | bytes 4128776 | tf_op jit(solution)/shard_map/ppermute | solution.py:15
  231.0 17.4 %all-to-all-start.2 = ((bf16[8,16,1024]{2,1,0:T(8,128)(2,1)}), bf16[8,16,1024]{2,1,0:T(8,128)(2,1)}, u32[]{:S(2)}, u32[]{:S(2)}) async-start(bf16[8,16,1024]{2,1,0:T(8,128)(2,1)} %bitcast.157), calls=%async_computation.3 | async-start | bytes 524288 | tf_op jit(solution)/shard_map/all_to_all | solution.py:119
  238.2 15.6 %copy-start.16 = (bf16[4,2,56,1024]{3,2,0,1:T(8,128)(2,1)S(1)}, bf16[4,2,56,1024]{3,2,0,1:T(8,128)(2,1)}, u32[]{:S(2)}) copy-start(bf16[4,2,56,1024]{3,2,0,1:T(8,128)(2,1)} %copy-done.15) | copy-start | bytes 2752516
  250.3 18.2 %all-to-all-start.4 = ((bf16[8,2,16,1024]{3,2,1,0:T(8,128)(2,1)}), bf16[8,2,16,1024]{3,2,1,0:T(8,128)(2,1)S(1)}, u32[]{:S(2)}, u32[]{:S(2)}) async-start(bf16[8,2,16,1024]{3,2,1,0:T(8,128)(2,1)} %broadcast_in_dim.323), calls=%async_computation.5 | async-start | bytes 1048576 | tf_op jit(solution)/shard_map/all_to_all | solution.py:30
Sparse Core Ops, SparseCore 0:
  10.9 64.1 all-gather.1
  147.6 79.3 reduce-scatter.1

commit v2 on v1

v2 whole, which is shorter than its diff:
```python
import functools
import jax
import jax.numpy as jnp
from jax import lax
from jax.experimental import pallas as pl
from jax.experimental.pallas import tpu as pltpu
from jax.sharding import Mesh, PartitionSpec as P

F32 = jnp.float32
BF16 = jnp.bfloat16
VMEM_BYTES = 48 * 1024 * 1024


def short(value):
    return lax.reduce_precision(value, exponent_bits=8, mantissa_bits=7)


def swap(value, axis):
    return lax.ppermute(value, axis, [(0, 1), (1, 0)])


def contract_last(left, right):
    return lax.dot_general(left, right, (((1,), (1,)), ((), ())), preferred_element_type=F32)


def contract_first(left, right):
    return lax.dot_general(left, right, (((0,), (0,)), ((), ())), preferred_element_type=F32)


def spread(value, axis, count):
    copies = jnp.broadcast_to(value[None], (count,) + value.shape)
    copies = lax.optimization_barrier(copies)
    return lax.all_to_all(copies, axis, split_axis=0, concat_axis=0, tiled=True)


def pick_kernel(mats, top, nx, weight_ref, rows_ref, mask_ref, out_ref):
    expert = pl.program_id(0)
    rows = rows_ref[...].reshape(-1, rows_ref.shape[2])
    share = rows.shape[0] // nx
    mask = mask_ref[0]
    for m in range(mats):
        sums = contract_last(weight_ref[m, 0], rows)
        for k in range(top):
            part = (sums * mask[k : k + 1]).astype(BF16)
            for q in range(nx):
                piece = part[:, q * share : (q + 1) * share]

                @pl.when(expert == 0)
                def _():
                    out_ref[q, m * top + k] = piece

                @pl.when(expert > 0)
                def _():
                    out_ref[q, m * top + k] += piece


def pick(weights, everything, mask, place, rows, nx):
    mats, experts, units, width = weights.shape
    top, total = mask.shape[1:]
    ny = everything.shape[0]
    return pl.pallas_call(
        functools.partial(pick_kernel, mats, top, nx),
        grid=(experts,),
        in_specs=[
            pl.BlockSpec((mats, 1, units, width), lambda e: (0, e, 0, 0)),
            pl.BlockSpec((ny, rows, width), lambda e: (0, place, 0)),
            pl.BlockSpec((1, top, total), lambda e: (e, 0, 0)),
        ],
        out_specs=pl.BlockSpec((nx, mats * top, units, total // nx), lambda e: (0, 0, 0, 0)),
        out_shape=jax.ShapeDtypeStruct((nx, mats * top, units, total // nx), BF16),
        compiler_params=pltpu.CompilerParams(vmem_limit_bytes=VMEM_BYTES),
        cost_estimate=pl.CostEstimate(
            flops=2 * mats * experts * units * width * total,
            bytes_accessed=2 * (weights.size + total * width + mats * top * units * total),
            transcendentals=0,
        ),
        name="pick",
    )(weights, everything, mask)


def output_kernel(mats, top, nx, split, shared_ref, weight_ref, mask_ref, wide_ref, out_ref, acc_ref):
    expert = pl.program_id(0)
    mask = mask_ref[0]
    share = shared_ref.shape[3]
    product = None
    for m in range(mats):
        pieces = []
        for q in range(nx):
            piece = None
            for k in range(top):
                value = shared_ref[q, m * top + k].astype(F32)
                term = value * mask[k : k + 1, q * share : (q + 1) * share]
                piece = term if piece is None else piece + term
            pieces.append(piece.astype(BF16))
        wide = jnp.concatenate(pieces, axis=1)
        wide_ref[m, 0] = wide
        term = contract_first(wide, weight_ref[m, 0])
        product = term if product is None else product + term

    @pl.when(expert == 0)
    def _():
        acc_ref[...] = product

    @pl.when(expert > 0)
    def _():
        acc_ref[...] += product

    @pl.when(expert == pl.num_programs(0) - 1)
    def _():
        total = acc_ref[...].astype(BF16)
        if split is None:
            out_ref[...] = total
        else:
            ny, nh = split
            blocks = total.reshape(ny, nh, total.shape[0] // (ny * nh), total.shape[1])
            for h in range(nh):
                out_ref[h] = blocks[:, h]


def output(shared, weights, mask, split):
    mats, experts, units, width = weights.shape
    top, total = mask.shape[1:]
    nx, _, _, share = shared.shape
    if split is None:
        shape = (total, width)
    else:
        shape = (split[1], split[0], total // (split[0] * split[1]), width)
    return pl.pallas_call(
        functools.partial(output_kernel, mats, top, nx, split),
        grid=(experts,),
        in_specs=[
            pl.BlockSpec(shared.shape, lambda e: (0, 0, 0, 0)),
            pl.BlockSpec((mats, 1, units, width), lambda e: (0, e, 0, 0)),
            pl.BlockSpec((1, top, total), lambda e: (e, 0, 0)),
        ],
        out_specs=[
            pl.BlockSpec((mats, 1, units, total), lambda e: (0, e, 0, 0)),
            pl.BlockSpec(shape, lambda e: (0,) * len(shape)),
        ],
        out_shape=[
            jax.ShapeDtypeStruct((mats, experts, units, total), BF16),
            jax.ShapeDtypeStruct(shape, BF16),
        ],
        scratch_shapes=[pltpu.VMEM((total, width), F32)],
        compiler_params=pltpu.CompilerParams(vmem_limit_bytes=VMEM_BYTES),
        cost_estimate=pl.CostEstimate(
            flops=2 * mats * experts * units * width * total,
            bytes_accessed=2 * (weights.size + total * width + 2 * shared.size),
            transcendentals=0,
        ),
        name="output",
    )(shared, weights, mask)


def body(tokens, slot_ids, gate_values, slot_expert, w_gate, w_up, w_down, cotangent):
    block, width = tokens.shape
    experts, units, _ = w_gate.shape
    ny, nh, nl, nx = (lax.axis_size(a) for a in ("y", "zh", "zl", "x"))
    top = slot_ids.shape[1]
    rows = block // nl
    total = ny * rows
    share = total // nx
    many = 2 * nl * units

    def own_rows(value):
        return lax.dynamic_slice_in_dim(value, lax.axis_index("zl") * rows, rows, axis=0)

    ids, values = own_rows(slot_ids), own_rows(gate_values)
    numbers = jnp.arange(slot_expert.shape[0], dtype=jnp.int32)
    chosen = jnp.sum(
        jnp.where(ids[:, :, None] == numbers, slot_expert[None, None, :], 0), axis=-1
    ).astype(F32)
    part0 = short(values)
    part1 = short(values - part0)
    part2 = short(values - part0 - part1)
    meta = jnp.stack([chosen, part0, part1, part2]).transpose(0, 2, 1).astype(BF16)
    facts_of = 4 * top * rows
    meta = jnp.pad(meta.reshape(1, facts_of), ((0, 15), (0, width - facts_of)))
    packed = jnp.concatenate([own_rows(tokens), own_rows(cotangent), meta], axis=0)
    held = packed.shape[0]
    everything = lax.all_gather(packed, "y", axis=0, tiled=True).reshape(ny, held, width)

    own = jnp.stack([w_gate, w_up, w_down])
    near = swap(own, "zl")
    weights = jnp.concatenate([own, swap(own, "core"), near, swap(near, "core")], axis=2)

    facts = everything[:, 2 * rows, :facts_of].reshape(ny, 4, top, rows).astype(F32)
    facts = facts.transpose(1, 2, 0, 3).reshape(4, top, total)
    scale = facts[1] + facts[2] + facts[3]
    mask = (facts[0][None] == jnp.arange(experts, dtype=F32)[:, None, None]).astype(F32)
    own_scale = lax.dynamic_slice_in_dim(scale, lax.axis_index("x") * share, share, axis=1)[:, None]

    def add_up(picked):
        arrived = lax.all_to_all(picked, "x", split_axis=0, concat_axis=0, tiled=True)
        return jnp.sum(arrived.astype(F32), axis=0).reshape(-1, top, many, share)

    gate, up = add_up(pick(weights[:2], everything, mask, 0, rows, nx))
    dh = own_scale * add_up(pick(weights[2:], everything, mask, 1, rows, nx))[0]
    sg = jax.nn.sigmoid(gate)
    active = gate * sg
    hidden = (own_scale * (active * up)).astype(BF16)
    dgate = (dh * up * sg * (1.0 + gate * (1.0 - sg))).astype(BF16)
    dup = (dh * active).astype(BF16)
    hidden_all = spread(hidden, "x", nx)
    grads_all = spread(jnp.concatenate([dgate, dup]), "x", nx)

    hidden_wide, mixed_part = output(hidden_all, weights[2:], mask, (ny, nh))
    grads_wide, back_part = output(grads_all, weights[:2], mask, None)

    small = rows // nh
    mixed = lax.all_to_all(mixed_part, "zh", split_axis=0, concat_axis=0, tiled=True)
    mixed = jnp.sum(mixed.astype(F32), axis=0).astype(BF16)
    mixed = lax.all_to_all(mixed, "y", split_axis=0, concat_axis=0, tiled=True)
    mixed = jnp.sum(mixed.astype(F32), axis=0).astype(BF16)

    back = lax.psum_scatter(back_part, "y", scatter_dimension=0, tiled=True)
    back = back.reshape(nh, small, width)
    back = lax.all_to_all(back, "zh", split_axis=0, concat_axis=0, tiled=True)
    back = jnp.sum(back.astype(F32), axis=0).astype(BF16)

    def finish(piece):
        pieces = spread(piece, ("zh", "zl"), nh * nl).reshape(nh, nl, small, width)
        return pieces.transpose(1, 0, 2, 3).reshape(block, width)

    def weight_gradient(wide, values):
        part = jnp.dot(wide.reshape(-1, total), values, preferred_element_type=F32)
        part = part.astype(BF16).reshape(experts, nl, 2, units, width)
        sent = swap(part[:, :, 1], "core")
        part = part[:, :, 0].astype(F32) + sent.astype(F32)
        sent = swap(part[:, 1].astype(BF16), "zl")
        return (part[:, 0] + sent.astype(F32)).astype(BF16)

    rows_x = everything[:, :rows].reshape(total, width)
    rows_c = everything[:, rows : 2 * rows].reshape(total, width)
    grad_down = weight_gradient(hidden_wide[0], rows_c)
    grad_gate = weight_gradient(grads_wide[0], rows_x)
    grad_up = weight_gradient(grads_wide[1], rows_x)
    return (finish(mixed), finish(back), grad_gate, grad_up, grad_down)


def solution(mesh):
    dp, ep, mp = mesh.shape["dp"], mesh.shape["expert"], mesh.shape["mp"]
    split = Mesh(
        mesh.devices.reshape(dp // 2, 2, ep // 2, 2, mp), ("y", "core", "zh", "zl", "x")
    )
    rows = ("y", "core")
    stored = P(None, ("y", "core", "zh", "zl"), "x")
    return jax.shard_map(
        body,
        mesh=split,
        in_specs=(
            P(rows, "x"),
            P(rows, None),
            P(rows, None),
            P(),
            stored,
            stored,
            stored,
            P(rows, "x"),
        ),
        out_specs=(P(rows, "x"), P(rows, "x"), stored, stored, stored),
        check_vma=False,
    )
```

time: 277 us -> 238 us (0.86)
  waiting for transfers between devices: 153 us -> 72.4 us
  starting transfers between devices: 30.2 us -> 75 us
  Pallas kernels: 0 us -> 20.8 us
  blocking collectives: 20.1 us -> 0 us
  matrix products: 13.6 us -> 3.35 us
  other arithmetic: 20.2 us -> 26.3 us
    all_to_all x3 -> x5, waiting for transfers between devices: 79.7 us -> 16.3 us  [the longest x2 7.04 us: add_up(): lax.all_to_all(picked, 'x', split_axis=0, concat_axis=0, tiled=True)]
    all_gather x1, waiting for transfers between devices: 58.6 us -> 6.49 us  [body(): lax.all_gather(packed, 'y', axis=0, tiled=True).reshape(ny, held, width)]
    ppermute x2 -> x9, waiting for transfers between devices: 3.1 us -> 31.5 us  [swap(): return lax.ppermute(value, axis, [(0, 1), (1, 0)])]
    ppermute x2 -> x9, starting transfers between devices: 3.83 us -> 29.1 us  [swap(): return lax.ppermute(value, axis, [(0, 1), (1, 0)])]
    pallas_call x0 -> x4, Pallas kernels: none -> 20.8 us  [the longest x2 10.6 us: pick(): pl.pallas_call(functools.partial(pick_kernel, mats, top, nx), grid=(exper...]
    all_to_all x1 -> x0, blocking collectives: 20.1 us -> none  [spread(): return lax.all_to_all(copies, axis, split_axis=0, concat_axis=0, tiled=True)]
    all_to_all x1 -> x4, starting transfers between devices: 3.49 us -> 17.9 us  [spread(): return lax.all_to_all(copies, axis, split_axis=0, concat_axis=0, tiled=True)]
    dot_general x9 -> x3, matrix products: 13.6 us -> 3.35 us  [weight_gradient(): part = jnp.dot(wide.reshape(-1, total), values, preferred_element_type=F32)]
  transfers between devices with their start and end apart: 8 -> 20, of which waited for: 6 -> 10; matrix products, arithmetic and copies ran while one was open for 8% -> 18% of each run, Pallas kernels for 0% -> 7%
where the time goes in v2:
time: 238 us; the launch traced here: 236 us
  starting transfers between devices  75 us (32%)
  waiting for transfers between devices  72.4 us (30%)
  other arithmetic  26.3 us (11%)
  local copies, waits for them, and re-layouts  23.3 us (10%)
  Pallas kernels  20.8 us (9%)
  between operations  14.4 us (6%)
  matrix products  3.35 us (1%)
    ppermute x9, waiting for transfers between devices, swap(): return lax.ppermute(value, axis, [(0, 1), (1, 0)])  31.5 us
    ppermute x9, starting transfers between devices, swap(): return lax.ppermute(value, axis, [(0, 1), (1, 0)])  29.1 us
    all_to_all x4, starting transfers between devices, spread(): return lax.all_to_all(copies, axis, split_axis=0, concat_axis=0, tiled=True)  17.9 us
    all_to_all x4, waiting for transfers between devices, spread(): return lax.all_to_all(copies, axis, split_axis=0, concat_axis=0, tiled=True)  12.9 us
    pallas_call x2, Pallas kernels, pick(): pl.pallas_call(functools.partial(pick_kernel, mats, top, nx), grid=(exper...  10.6 us
    pallas_call x2, Pallas kernels, output(): pl.pallas_call(functools.partial(output_kernel, mats, top, nx, split), gr...  10.2 us
    all_to_all x2, starting transfers between devices, add_up(): lax.all_to_all(picked, 'x', split_axis=0, concat_axis=0, tiled=True)  9.61 us
    all_to_all x1, starting transfers between devices, body(): back = lax.all_to_all(back, 'zh', split_axis=0, concat_axis=0, tiled=True)  7.54 us
  transfers between devices with their start and end apart: 20, of which 10 were waited for; matrix products, arithmetic and copies ran while one was open for 18% of the time, Pallas kernels for 7%

profile of v2, /device:TPU:6, one launch (start us, length us, event | category | flops | bytes accessed | tf_op | source)
XLA Modules:
  0.0 235.5 jit_solution(6263409063026286066)
XLA Ops:
  7.2 0.8 fusion.16
  8.9 1.0 constant_dynamic-slice_fusion.3
  10.7 1.4 pad_maximum_fusion.2
  12.1 4.3 %collective-permute-start.1 = (bf16[3,4,56,1024]{3,2,1,0:T(8,128)(2,1)S(1)}, bf16[3,4,56,1024]{3,2,1,0:T(8,128)(2,1)S(1)}, u32[]{:S(2)}, u32[]{:S(2)}) collective-permute-start(bf16[3,4,56,1024]{3,2,1,0:T(8,128)(2,1)S(1)} %pad_maximum_fusion.2), channel_id=1, source_target_pairs={{0,4},{4,0},{1,5},{5,1},{2,6},{6,2},{3,7},{7,3},{8,12},{12,8},{9,1... | collective-permute-start | bytes 4128776 | tf_op jit(solution)/shard_map/ppermute | solution.py:19
  16.4 1.9 collective-permute-start
  18.3 28.2 %collective-permute-done.1 = bf16[3,4,56,1024]{3,2,1,0:T(8,128)(2,1)S(1)} collective-permute-done((bf16[3,4,56,1024]{3,2,1,0:T(8,128)(2,1)S(1)}, bf16[3,4,56,1024]{3,2,1,0:T(8,128)(2,1)S(1)}, u32[]{:S(2)}, u32[]{:S(2)}) %collective-permute-start.1) | collective-permute-done | bytes 1376288 | tf_op jit(solution)/shard_map/ppermute | solution.py:19
  46.6 1.9 collective-permute-start.2
  48.5 3.2 %collective-permute-done.2 = bf16[3,4,56,1024]{3,2,1,0:T(8,128)(2,1)} collective-permute-done((bf16[3,4,56,1024]{3,2,1,0:T(8,128)(2,1)S(1)}, bf16[3,4,56,1024]{3,2,1,0:T(8,128)(2,1)}, u32[]{:S(2)}, u32[]{:S(2)}) %collective-permute-start.2) | collective-permute-done | bytes 1376288 | tf_op jit(solution)/shard_map/ppermute | solution.py:19
  51.7 1.5 pad_maximum_fusion.1.weight_ref
  53.3 6.5 %all-gather.2.cloned.1.call-done = bf16[1152,1024]{1,0:T(8,128)(2,1)} async-done(((bf16[144,1024]{1,0:T(8,128)(2,1)}), bf16[1152,1024]{1,0:T(8,128)(2,1)}) %all-gather.2.cloned.1.call-update) | async-done | bytes 2359312 | tf_op jit(solution)/shard_map/all_gather | solution.py:181
  59.7 0.9 fusion.12
  60.9 1.7 copy-done.1
  62.5 3.4 %pick.3 = bf16[4,2,224,128]{3,2,1,0:T(8,128)(2,1)} custom-call(bf16[1,4,224,1024]{3,2,1,0:T(8,128)(2,1)S(1)} %pad_maximum_fusion.1.weight_ref, bf16[8,144,1024]{2,1,0:T(8,128)(2,1)S(1)} %bitcast.93, f32[4,2,512]{2,1,0:T(2,128)S(1)} %compare_convert_fusion.mask_ref), custom_call_target="tpu_custom_call" | custom-call | flops 939524096 | bytes 3342336 | tf_op jit(solution)/shard_map/pick/pallas_call | solution.py:61
  65.9 4.8 %all-to-all-start.5 = ((bf16[4,2,224,128]{3,2,1,0:T(8,128)(2,1)}), bf16[4,2,224,128]{3,2,1,0:T(8,128)(2,1)}, u32[]{:S(2)}, u32[]{:S(2)}) async-start(bf16[4,2,224,128]{3,2,1,0:T(8,128)(2,1)} %pick.3), calls=%async_computation.5 | async-start | bytes 917504 | tf_op jit(solution)/shard_map/all_to_all | solution.py:194
  70.8 3.0 %pad_maximum_fusion = bf16[3,4,224,1024]{3,2,1,0:T(8,128)(2,1)S(1)} fusion(bf16[3,4,56,1024]{3,2,1,0:T(8,128)(2,1)} %collective-permute-done.2, bf16[3,4,56,1024]{3,2,1,0:T(8,128)(2,1)S(1)} %collective-permute-done.1, bf16[3,4,56,1024]{3,2,1,0:T(8,128)(2,1)} %collective-permute-done, bf16[1,4,56,1024]{3,2,1,0:T(8,128)(2,1)} %bitcast.99, ...), kind=kLoop, calls=%fused_computation | loop fusion | flops 33030144 | bytes 11010048 | tf_op jit(solution)/shard_map/concatenate | solution.py:185
  73.8 2.2 slice.107.weight_ref
  76.2 7.2 %pick.2 = bf16[4,4,224,128]{3,2,1,0:T(8,128)(2,1)} custom-call(bf16[2,4,224,1024]{3,2,1,0:T(8,128)(2,1)} %slice.107.weight_ref, bf16[8,144,1024]{2,1,0:T(8,128)(2,1)S(1)} %bitcast.94, f32[4,2,512]{2,1,0:T(2,128)S(1)} %compare_convert_fusion.mask_ref), custom_call_target="tpu_custom_call" | custom-call | flops 1879048192 | bytes 5636096 | tf_op jit(solution)/shard_map/pick/pallas_call | solution.py:61
  83.4 4.8 %all-to-all-start = ((bf16[4,4,224,128]{3,2,1,0:T(8,128)(2,1)}), bf16[4,4,224,128]{3,2,1,0:T(8,128)(2,1)}, u32[]{:S(2)}, u32[]{:S(2)}) async-start(bf16[4,4,224,128]{3,2,1,0:T(8,128)(2,1)} %pick.2), calls=%async_computation | async-start | bytes 1835008 | tf_op jit(solution)/shard_map/all_to_all | solution.py:194
  88.3 1.1 convert_reduce_fusion.1
  89.4 7.0 %all-to-all-done = bf16[4,4,224,128]{3,2,1,0:T(8,128)(2,1)} async-done(((bf16[4,4,224,128]{3,2,1,0:T(8,128)(2,1)}), bf16[4,4,224,128]{3,2,1,0:T(8,128)(2,1)}, u32[]{:S(2)}, u32[]{:S(2)}) %all-to-all-start) | async-done | bytes 917536 | tf_op jit(solution)/shard_map/all_to_all | solution.py:194
  96.4 1.4 convert_reduce_fusion
  98.0 0.8 broadcast_in_dim.22
  98.8 5.5 %all-to-all-start.1 = ((bf16[4,2,224,128]{3,2,1,0:T(8,128)(2,1)}), bf16[4,2,224,128]{3,2,1,0:T(8,128)(2,1)S(1)}, u32[]{:S(2)}, u32[]{:S(2)}) async-start(bf16[4,2,224,128]{3,2,1,0:T(8,128)(2,1)} %broadcast_in_dim.22), calls=%async_computation.1 | async-start | bytes 917504 | tf_op jit(solution)/shard_map/all_to_all | solution.py:33
  104.3 1.5 fusion.19
  105.8 1.1 broadcast_in_dim.24
  106.9 3.0 %all-to-all-done.1.shared_ref = bf16[4,2,224,128]{3,2,1,0:T(8,128)(2,1)S(1)} async-done(((bf16[4,2,224,128]{3,2,1,0:T(8,128)(2,1)}), bf16[4,2,224,128]{3,2,1,0:T(8,128)(2,1)S(1)}, u32[]{:S(2)}, u32[]{:S(2)}) %all-to-all-start.1) | async-done | bytes 458784 | tf_op jit(solution)/shard_map/all_to_all | solution.py:33
  110.0 5.5 %all-to-all-start.6 = ((bf16[4,4,224,128]{3,2,1,0:T(8,128)(2,1)}), bf16[4,4,224,128]{3,2,1,0:T(8,128)(2,1)S(1)}, u32[]{:S(2)}, u32[]{:S(2)}) async-start(bf16[4,4,224,128]{3,2,1,0:T(8,128)(2,1)} %broadcast_in_dim.24), calls=%async_computation.6 | async-start | bytes 1835008 | tf_op jit(solution)/shard_map/all_to_all | solution.py:33
  115.5 3.8 %output.2 = (bf16[1,4,224,512]{3,2,1,0:T(8,128)(2,1)S(1)}, bf16[4,8,16,1024]{3,2,1,0:T(8,128)(2,1)}) custom-call(bf16[4,2,224,128]{3,2,1,0:T(8,128)(2,1)S(1)} %all-to-all-done.1.shared_ref, bf16[1,4,224,1024]{3,2,1,0:T(8,128)(2,1)S(1)} %copy-done.4, f32[4,2,512]{2,1,0:T(2,128)S(1)} %compare_convert_fusion.mask_ref), custom_call_target="tpu_custom_call" | custom-call | flops 939524096 | bytes 3801088 | tf_op jit(solution)/shard_map/output/pallas_call | solution.py:128
  119.3 1.1 convolution_convert_fusion
  120.4 1.1 fusion.20
  121.5 1.0 copy.67
  122.5 1.9 collective-permute-start.7
  124.5 7.4 %all-to-all-start.2 = ((bf16[4,8,16,1024]{3,2,1,0:T(8,128)(2,1)}), bf16[4,8,16,1024]{3,2,1,0:T(8,128)(2,1)}, u32[]{:S(2)}, u32[]{:S(2)}) async-start(bf16[4,8,16,1024]{3,2,1,0:T(8,128)(2,1)} %get-tuple-element.9), calls=%async_computation.2 | async-start | bytes 2097152 | tf_op jit(solution)/shard_map/all_to_all | solution.py:211
  131.9 6.4 %output.3 = (bf16[2,4,224,512]{3,2,1,0:T(8,128)(2,1)S(1)}, bf16[512,1024]{1,0:T(8,128)(2,1)}) custom-call(bf16[4,4,224,128]{3,2,1,0:T(8,128)(2,1)S(1)} %all-to-all-done.6.shared_ref, bf16[2,4,224,1024]{3,2,1,0:T(8,128)(2,1)} %slice.107.weight_ref, f32[4,2,512]{2,1,0:T(2,128)S(1)} %compare_convert_fusion.mask_ref), custom_call_target="tpu_custom_call" | custom-call | flops 1879048192 | bytes 6553600 | tf_op jit(solution)/shard_map/output/pallas_call | solution.py:128
  138.5 1.0 copy-done.7
  139.5 1.1 convolution_convert_fusion.2
  140.7 1.1 fusion.23
  141.8 1.0 copy.69
  142.8 2.1 collective-permute-start.3
  144.9 1.1 convolution_convert_fusion.1
  146.2 1.0 copy.68
  147.2 2.2 collective-permute-start.5
  149.4 1.5 convert_add_fusion
  150.9 0.8 fusion.9
  151.7 2.6 %collective-permute-start.8 = (bf16[4,56,1024]{2,1,0:T(8,128)(2,1)}, bf16[4,56,1024]{2,1,0:T(8,128)(2,1)}, u32[]{:S(2)}, u32[]{:S(2)}) collective-permute-start(bf16[4,56,1024]{2,1,0:T(8,128)(2,1)} %fusion.9), channel_id=1, source_target_pairs={{0,4},{4,0},{1,5},{5,1},{2,6},{6,2},{3,7},{7,3},{8,12},{12,8},{9,1... | collective-permute-start | bytes 1376264 | tf_op jit(solution)/shard_map/ppermute | solution.py:19
  154.4 4.0 %all-to-all-done.2 = bf16[4,8,16,1024]{3,2,1,0:T(8,128)(2,1)} async-done(((bf16[4,8,16,1024]{3,2,1,0:T(8,128)(2,1)}), bf16[4,8,16,1024]{3,2,1,0:T(8,128)(2,1)}, u32[]{:S(2)}, u32[]{:S(2)}) %all-to-all-start.2) | async-done | bytes 1048608 | tf_op jit(solution)/shard_map/all_to_all | solution.py:211
  158.4 2.2 reduce_sum.65
  160.6 3.5 %all-to-all-start.3 = ((bf16[8,16,1024]{2,1,0:T(8,128)(2,1)}), bf16[8,16,1024]{2,1,0:T(8,128)(2,1)S(1)}, u32[]{:S(2)}, u32[]{:S(2)}) async-start(bf16[8,16,1024]{2,1,0:T(8,128)(2,1)} %reduce_sum.65), calls=%async_computation.3 | async-start | bytes 524288 | tf_op jit(solution)/shard_map/all_to_all | solution.py:213
  164.1 3.0 %convert_add_fusion.2 = f32[4,2,56,1024]{3,2,0,1:T(8,128)} fusion(bf16[4,2,56,1024]{3,2,0,1:T(8,128)(2,1)} %collective-permute-done.3, bf16[4,2,1,56,1024]{4,3,2,1,0:T(8,128)(2,1)} %get-tuple-element.21), kind=kLoop, calls=%fused_computation.4 | loop fusion | flops 1376256 | bytes 3670016 | tf_op jit(solution)/shard_map/add | solution.py:229
  167.1 2.0 fusion.7
  169.1 8.3 %collective-permute-start.4 = (bf16[4,56,1024]{2,1,0:T(8,128)(2,1)}, bf16[4,56,1024]{2,1,0:T(8,128)(2,1)}, u32[]{:S(2)}, u32[]{:S(2)}) collective-permute-start(bf16[4,56,1024]{2,1,0:T(8,128)(2,1)} %fusion.7), channel_id=1, source_target_pairs={{0,4},{4,0},{1,5},{5,1},{2,6},{6,2},{3,7},{7,3},{8,12},{12,8},{9,1... | collective-permute-start | bytes 1376264 | tf_op jit(solution)/shard_map/ppermute | solution.py:19
  177.5 5.1 %reduce-scatter.2.cloned.1.call-done = bf16[64,1024]{1,0:T(8,128)(2,1)} async-done(((bf16[512,1024]{1,0:T(8,128)(2,1)}), bf16[64,1024]{1,0:T(8,128)(2,1)}) %reduce-scatter.2.cloned.1.call-update) | async-done | bytes 131088 | tf_op jit(solution)/shard_map/reduce_scatter | solution.py:216
  182.6 7.5 %all-to-all-start.7 = ((bf16[4,16,1024]{2,1,0:T(8,128)(2,1)}), bf16[4,16,1024]{2,1,0:T(8,128)(2,1)S(1)}, u32[]{:S(2)}, u32[]{:S(2)}) async-start(bf16[4,16,1024]{2,1,0:T(8,128)(2,1)} %bitcast.118), calls=%async_computation.8 | async-start | bytes 262144 | tf_op jit(solution)/shard_map/all_to_all | solution.py:218
  190.1 2.7 %convert_add_fusion.1 = f32[4,2,56,1024]{3,2,0,1:T(8,128)} fusion(bf16[4,2,56,1024]{3,2,0,1:T(8,128)(2,1)} %collective-permute-done.5, bf16[4,2,1,56,1024]{4,3,2,1,0:T(8,128)(2,1)S(1)} %get-tuple-element.17), kind=kLoop, calls=%fused_computation.3 | loop fusion | flops 1376256 | bytes 3670016 | tf_op jit(solution)/shard_map/add | solution.py:229
  193.7 5.2 %all-to-all-done.7 = bf16[4,16,1024]{2,1,0:T(8,128)(2,1)S(1)} async-done(((bf16[4,16,1024]{2,1,0:T(8,128)(2,1)}), bf16[4,16,1024]{2,1,0:T(8,128)(2,1)S(1)}, u32[]{:S(2)}, u32[]{:S(2)}) %all-to-all-start.7) | async-done | bytes 131104 | tf_op jit(solution)/shard_map/all_to_all | solution.py:218
  198.9 3.4 %all-to-all-start.4 = ((bf16[8,16,1024]{2,1,0:T(8,128)(2,1)}), bf16[8,16,1024]{2,1,0:T(8,128)(2,1)S(1)}, u32[]{:S(2)}, u32[]{:S(2)}) async-start(bf16[8,16,1024]{2,1,0:T(8,128)(2,1)} %broadcast_in_dim.23), calls=%async_computation.4 | async-start | bytes 524288 | tf_op jit(solution)/shard_map/all_to_all | solution.py:33
  202.3 2.0 fusion.8
  204.3 3.8 %collective-permute-start.6 = (bf16[4,56,1024]{2,1,0:T(8,128)(2,1)}, bf16[4,56,1024]{2,1,0:T(8,128)(2,1)S(1)}, u32[]{:S(2)}, u32[]{:S(2)}) collective-permute-start(bf16[4,56,1024]{2,1,0:T(8,128)(2,1)} %fusion.8), channel_id=1, source_target_pairs={{0,4},{4,0},{1,5},{5,1},{2,6},{6,2},{3,7},{7,3},{8,12},{12,8},{9,1... | collective-permute-start | bytes 1376264 | tf_op jit(solution)/shard_map/ppermute | solution.py:19
  208.2 1.9 fusion.1
  210.8 3.3 %all-to-all-done.4 = bf16[8,16,1024]{2,1,0:T(8,128)(2,1)S(1)} async-done(((bf16[8,16,1024]{2,1,0:T(8,128)(2,1)}), bf16[8,16,1024]{2,1,0:T(8,128)(2,1)S(1)}, u32[]{:S(2)}, u32[]{:S(2)}) %all-to-all-start.4) | async-done | bytes 262176 | tf_op jit(solution)/shard_map/all_to_all | solution.py:33
  214.2 3.4 %all-to-all-start.8 = ((bf16[8,16,1024]{2,1,0:T(8,128)(2,1)}), bf16[8,16,1024]{2,1,0:T(8,128)(2,1)S(1)}, u32[]{:S(2)}, u32[]{:S(2)}) async-start(bf16[8,16,1024]{2,1,0:T(8,128)(2,1)} %broadcast_in_dim.25), calls=%async_computation.9 | async-start | bytes 524288 | tf_op jit(solution)/shard_map/all_to_all | solution.py:33
  217.6 2.2 fusion.5
  219.8 0.9 fusion.3
  221.4 6.6 %all-to-all-done.8 = bf16[8,16,1024]{2,1,0:T(8,128)(2,1)S(1)} async-done(((bf16[8,16,1024]{2,1,0:T(8,128)(2,1)}), bf16[8,16,1024]{2,1,0:T(8,128)(2,1)S(1)}, u32[]{:S(2)}, u32[]{:S(2)}) %all-to-all-start.8) | async-done | bytes 262176 | tf_op jit(solution)/shard_map/all_to_all | solution.py:33
  (53 shorter events, 5.7 us)
Async XLA Ops:
  7.2 0.8 copy-start
  7.2 52.6 %all-gather.2.cloned.1.call-start = ((), (), s32[]{:S(2)}) async-start(), calls=%async_computation.10 | async-start | bytes 2654208 | tf_op jit(solution)/shard_map/all_gather | solution.py:181
  12.1 34.5 %collective-permute-start.1 = (bf16[3,4,56,1024]{3,2,1,0:T(8,128)(2,1)S(1)}, bf16[3,4,56,1024]{3,2,1,0:T(8,128)(2,1)S(1)}, u32[]{:S(2)}, u32[]{:S(2)}) collective-permute-start(bf16[3,4,56,1024]{3,2,1,0:T(8,128)(2,1)S(1)} %pad_maximum_fusion.2), channel_id=1, source_target_pairs={{0,4},{4,0},{1,5},{5,1},{2,6},{6,2},{3,7},{7,3},{8,12},{12,8},{9,1... | collective-permute-start | bytes 4128776 | tf_op jit(solution)/shard_map/ppermute | solution.py:19
  16.4 32.1 %collective-permute-start = (bf16[3,4,56,1024]{3,2,1,0:T(8,128)(2,1)S(1)}, bf16[3,4,56,1024]{3,2,1,0:T(8,128)(2,1)}, u32[]{:S(2)}, u32[]{:S(2)}) collective-permute-start(bf16[3,4,56,1024]{3,2,1,0:T(8,128)(2,1)S(1)} %pad_maximum_fusion.2), channel_id=1, source_target_pairs={{0,32},{32,0},{1,33},{33,1},{2,34},{34,2},{3,35},{35,3},{4,36},{36... | collective-permute-start | bytes 4128776 | tf_op jit(solution)/shard_map/ppermute | solution.py:19
  46.6 5.1 %collective-permute-start.2 = (bf16[3,4,56,1024]{3,2,1,0:T(8,128)(2,1)S(1)}, bf16[3,4,56,1024]{3,2,1,0:T(8,128)(2,1)}, u32[]{:S(2)}, u32[]{:S(2)}) collective-permute-start(bf16[3,4,56,1024]{3,2,1,0:T(8,128)(2,1)S(1)} %collective-permute-done.1), channel_id=1, source_target_pairs={{0,32},{32,0},{1,33},{33,1},{2,34},{34,2},{3,35},{35,3},{4,36},{36... | collective-permute-start | bytes 4128776 | tf_op jit(solution)/shard_map/ppermute | solution.py:19
  53.3 12.7 %copy-start.3 = (bf16[1,4,224,1024]{3,2,1,0:T(8,128)(2,1)}, bf16[1,4,224,1024]{3,2,1,0:T(8,128)(2,1)S(1)}, u32[]{:S(2)}) copy-start(bf16[1,4,224,1024]{3,2,1,0:T(8,128)(2,1)S(1)} %pad_maximum_fusion.1.weight_ref) | copy-start | bytes 5505028
  60.8 1.7 copy-start.1
  65.9 17.5 %all-to-all-start.5 = ((bf16[4,2,224,128]{3,2,1,0:T(8,128)(2,1)}), bf16[4,2,224,128]{3,2,1,0:T(8,128)(2,1)}, u32[]{:S(2)}, u32[]{:S(2)}) async-start(bf16[4,2,224,128]{3,2,1,0:T(8,128)(2,1)} %pick.3), calls=%async_computation.5 | async-start | bytes 917504 | tf_op jit(solution)/shard_map/all_to_all | solution.py:194
  73.8 2.4 %copy-start.2 = (bf16[1152,1024]{1,0:T(8,128)(2,1)S(1)}, bf16[1152,1024]{1,0:T(8,128)(2,1)}, u32[]{:S(2)}) copy-start(bf16[1152,1024]{1,0:T(8,128)(2,1)} %all-gather.2.cloned.1.call-done) | copy-start | bytes 7077892
  83.4 13.0 %all-to-all-start = ((bf16[4,4,224,128]{3,2,1,0:T(8,128)(2,1)}), bf16[4,4,224,128]{3,2,1,0:T(8,128)(2,1)}, u32[]{:S(2)}, u32[]{:S(2)}) async-start(bf16[4,4,224,128]{3,2,1,0:T(8,128)(2,1)} %pick.2), calls=%async_computation | async-start | bytes 1835008 | tf_op jit(solution)/shard_map/all_to_all | solution.py:194
  98.8 11.2 %all-to-all-start.1 = ((bf16[4,2,224,128]{3,2,1,0:T(8,128)(2,1)}), bf16[4,2,224,128]{3,2,1,0:T(8,128)(2,1)S(1)}, u32[]{:S(2)}, u32[]{:S(2)}) async-start(bf16[4,2,224,128]{3,2,1,0:T(8,128)(2,1)} %broadcast_in_dim.22), calls=%async_computation.1 | async-start | bytes 917504 | tf_op jit(solution)/shard_map/all_to_all | solution.py:33
  105.8 9.7 %copy-start.4 = (bf16[1,4,224,1024]{3,2,1,0:T(8,128)(2,1)S(1)}, bf16[1,4,224,1024]{3,2,1,0:T(8,128)(2,1)}, u32[]{:S(2)}) copy-start(bf16[1,4,224,1024]{3,2,1,0:T(8,128)(2,1)} %copy-done.3) | copy-start | bytes 5505028
  110.0 14.5 %all-to-all-start.6 = ((bf16[4,4,224,128]{3,2,1,0:T(8,128)(2,1)}), bf16[4,4,224,128]{3,2,1,0:T(8,128)(2,1)S(1)}, u32[]{:S(2)}, u32[]{:S(2)}) async-start(bf16[4,4,224,128]{3,2,1,0:T(8,128)(2,1)} %broadcast_in_dim.24), calls=%async_computation.6 | async-start | bytes 1835008 | tf_op jit(solution)/shard_map/all_to_all | solution.py:33
  115.5 3.8 %copy-start.8 = (bf16[8,64,1024]{2,1,0:T(8,128)(2,1)S(1)}, bf16[8,64,1024]{2,1,0:T(8,128)(2,1)}, u32[]{:S(2)}) copy-start(bf16[8,64,1024]{2,1,0:T(8,128)(2,1)} %get-tuple-element.13) | copy-start | bytes 3145732
  122.5 26.8 %collective-permute-start.7 = (bf16[4,2,56,1024]{3,2,0,1:T(8,128)(2,1)}, bf16[4,2,56,1024]{3,2,0,1:T(8,128)(2,1)}, u32[]{:S(2)}, u32[]{:S(2)}) collective-permute-start(bf16[4,2,56,1024]{3,2,0,1:T(8,128)(2,1)} %bitcast.88), channel_id=1, source_target_pairs={{0,32},{32,0},{1,33},{33,1},{2,34},{34,2},{3,35},{35,3},{4,36},{36... | collective-permute-start | bytes 2752520 | tf_op jit(solution)/shard_map/ppermute | solution.py:19
  124.5 33.9 %all-to-all-start.2 = ((bf16[4,8,16,1024]{3,2,1,0:T(8,128)(2,1)}), bf16[4,8,16,1024]{3,2,1,0:T(8,128)(2,1)}, u32[]{:S(2)}, u32[]{:S(2)}) async-start(bf16[4,8,16,1024]{3,2,1,0:T(8,128)(2,1)} %get-tuple-element.9), calls=%async_computation.2 | async-start | bytes 2097152 | tf_op jit(solution)/shard_map/all_to_all | solution.py:211
  131.9 50.8 %reduce-scatter.2.cloned.1.call-start = ((), (), s32[]{:S(2)}) async-start(), calls=%async_computation.11 | async-start | bytes 1179648 | tf_op jit(solution)/shard_map/reduce_scatter | solution.py:216
  138.3 1.2 copy-start.7
  142.8 21.3 %collective-permute-start.3 = (bf16[4,2,56,1024]{3,2,0,1:T(8,128)(2,1)}, bf16[4,2,56,1024]{3,2,0,1:T(8,128)(2,1)}, u32[]{:S(2)}, u32[]{:S(2)}) collective-permute-start(bf16[4,2,56,1024]{3,2,0,1:T(8,128)(2,1)} %bitcast.90), channel_id=1, source_target_pairs={{0,32},{32,0},{1,33},{33,1},{2,34},{34,2},{3,35},{35,3},{4,36},{36... | collective-permute-start | bytes 2752520 | tf_op jit(solution)/shard_map/ppermute | solution.py:19
  146.2 3.2 %copy-start.6 = (bf16[4,2,1,56,1024]{4,3,2,1,0:T(8,128)(2,1)S(1)}, bf16[4,2,1,56,1024]{4,3,2,1,0:T(8,128)(2,1)}, u32[]{:S(2)}) copy-start(bf16[4,2,1,56,1024]{4,3,2,1,0:T(8,128)(2,1)} %get-tuple-element.15) | copy-start | bytes 2752516
  147.2 43.0 %collective-permute-start.5 = (bf16[4,2,56,1024]{3,2,0,1:T(8,128)(2,1)}, bf16[4,2,56,1024]{3,2,0,1:T(8,128)(2,1)}, u32[]{:S(2)}, u32[]{:S(2)}) collective-permute-start(bf16[4,2,56,1024]{3,2,0,1:T(8,128)(2,1)} %bitcast.89), channel_id=1, source_target_pairs={{0,32},{32,0},{1,33},{33,1},{2,34},{34,2},{3,35},{35,3},{4,36},{36... | collective-permute-start | bytes 2752520 | tf_op jit(solution)/shard_map/ppermute | solution.py:19
  151.7 56.4 %collective-permute-start.8 = (bf16[4,56,1024]{2,1,0:T(8,128)(2,1)}, bf16[4,56,1024]{2,1,0:T(8,128)(2,1)}, u32[]{:S(2)}, u32[]{:S(2)}) collective-permute-start(bf16[4,56,1024]{2,1,0:T(8,128)(2,1)} %fusion.9), channel_id=1, source_target_pairs={{0,4},{4,0},{1,5},{5,1},{2,6},{6,2},{3,7},{7,3},{8,12},{12,8},{9,1... | collective-permute-start | bytes 1376264 | tf_op jit(solution)/shard_map/ppermute | solution.py:19
  160.6 16.8 %all-to-all-start.3 = ((bf16[8,16,1024]{2,1,0:T(8,128)(2,1)}), bf16[8,16,1024]{2,1,0:T(8,128)(2,1)S(1)}, u32[]{:S(2)}, u32[]{:S(2)}) async-start(bf16[8,16,1024]{2,1,0:T(8,128)(2,1)} %reduce_sum.65), calls=%async_computation.3 | async-start | bytes 524288 | tf_op jit(solution)/shard_map/all_to_all | solution.py:213
  169.1 48.5 %collective-permute-start.4 = (bf16[4,56,1024]{2,1,0:T(8,128)(2,1)}, bf16[4,56,1024]{2,1,0:T(8,128)(2,1)}, u32[]{:S(2)}, u32[]{:S(2)}) collective-permute-start(bf16[4,56,1024]{2,1,0:T(8,128)(2,1)} %fusion.7), channel_id=1, source_target_pairs={{0,4},{4,0},{1,5},{5,1},{2,6},{6,2},{3,7},{7,3},{8,12},{12,8},{9,1... | collective-permute-start | bytes 1376264 | tf_op jit(solution)/shard_map/ppermute | solution.py:19
  182.6 16.3 %all-to-all-start.7 = ((bf16[4,16,1024]{2,1,0:T(8,128)(2,1)}), bf16[4,16,1024]{2,1,0:T(8,128)(2,1)S(1)}, u32[]{:S(2)}, u32[]{:S(2)}) async-start(bf16[4,16,1024]{2,1,0:T(8,128)(2,1)} %bitcast.118), calls=%async_computation.8 | async-start | bytes 262144 | tf_op jit(solution)/shard_map/all_to_all | solution.py:218
  198.9 15.3 %all-to-all-start.4 = ((bf16[8,16,1024]{2,1,0:T(8,128)(2,1)}), bf16[8,16,1024]{2,1,0:T(8,128)(2,1)S(1)}, u32[]{:S(2)}, u32[]{:S(2)}) async-start(bf16[8,16,1024]{2,1,0:T(8,128)(2,1)} %broadcast_in_dim.23), calls=%async_computation.4 | async-start | bytes 524288 | tf_op jit(solution)/shard_map/all_to_all | solution.py:33
  204.3 15.4 %collective-permute-start.6 = (bf16[4,56,1024]{2,1,0:T(8,128)(2,1)}, bf16[4,56,1024]{2,1,0:T(8,128)(2,1)S(1)}, u32[]{:S(2)}, u32[]{:S(2)}) collective-permute-start(bf16[4,56,1024]{2,1,0:T(8,128)(2,1)} %fusion.8), channel_id=1, source_target_pairs={{0,4},{4,0},{1,5},{5,1},{2,6},{6,2},{3,7},{7,3},{8,12},{12,8},{9,1... | collective-permute-start | bytes 1376264 | tf_op jit(solution)/shard_map/ppermute | solution.py:19
  210.1 9.7 %copy-start.5 = (f32[4,2,56,1024]{3,2,0,1:T(8,128)S(1)}, f32[4,2,56,1024]{3,2,0,1:T(8,128)}, u32[]{:S(2)}) copy-start(f32[4,2,56,1024]{3,2,0,1:T(8,128)} %convert_add_fusion.1) | copy-start | bytes 5505028
  214.2 13.8 %all-to-all-start.8 = ((bf16[8,16,1024]{2,1,0:T(8,128)(2,1)}), bf16[8,16,1024]{2,1,0:T(8,128)(2,1)S(1)}, u32[]{:S(2)}, u32[]{:S(2)}) async-start(bf16[8,16,1024]{2,1,0:T(8,128)(2,1)} %broadcast_in_dim.25), calls=%async_computation.9 | async-start | bytes 524288 | tf_op jit(solution)/shard_map/all_to_all | solution.py:33
Sparse Core Ops, SparseCore 0:
  10.8 48.9 all-gather.1
  138.4 44.1 reduce-scatter.1

commit v3 on v2

v3 whole, which is shorter than its diff:
```python
import functools
import jax
import jax.numpy as jnp
from jax import lax
from jax.experimental import pallas as pl
from jax.experimental.pallas import tpu as pltpu
from jax.sharding import Mesh, PartitionSpec as P

F32 = jnp.float32
BF16 = jnp.bfloat16
VMEM_BYTES = 48 * 1024 * 1024


def short(value):
    return lax.reduce_precision(value, exponent_bits=8, mantissa_bits=7)


def swap(value, axis):
    return lax.ppermute(value, axis, [(0, 1), (1, 0)])


def contract_last(left, right):
    return lax.dot_general(left, right, (((1,), (1,)), ((), ())), preferred_element_type=F32)


def contract_first(left, right):
    return lax.dot_general(left, right, (((0,), (0,)), ((), ())), preferred_element_type=F32)


def spread(value, axis, count):
    copies = jnp.broadcast_to(value[None], (count,) + value.shape)
    copies = lax.optimization_barrier(copies)
    return lax.all_to_all(copies, axis, split_axis=0, concat_axis=0, tiled=True)


def pick_kernel(top, nx, experts, weight_ref, rows_ref, cots_ref, mask_ref, out_ref):
    width = rows_ref.shape[2]
    mats, parts, stored = weight_ref.shape[:3]
    units = stored // experts
    share = out_ref.shape[3]
    for m in range(mats):
        rows = (cots_ref if m == mats - 1 else rows_ref)[...].reshape(-1, width)
        picked = [[] for _ in range(top)]
        for p in range(parts):
            sums = contract_last(weight_ref[m, p], rows)
            for k in range(top):
                value = None
                for e in range(experts):
                    term = sums[e * units : (e + 1) * units] * mask_ref[e, k : k + 1]
                    value = term if value is None else value + term
                picked[k].append(value)
        for k in range(top):
            value = jnp.concatenate(picked[k], axis=0).astype(BF16)
            for q in range(nx):
                out_ref[q, m * top + k] = value[:, q * share : (q + 1) * share]


def pick(weights, experts, everything, mask, rows, nx):
    mats, parts, stored, width = weights.shape
    top, total = mask.shape[1:]
    ny = everything.shape[0]
    many = parts * stored // experts
    pieces = (nx, mats * top, many, total // nx)
    return pl.pallas_call(
        functools.partial(pick_kernel, top, nx, experts),
        grid=(1,),
        in_specs=[
            pl.BlockSpec(weights.shape, lambda i: (0, 0, 0, 0)),
            pl.BlockSpec((ny, rows, width), lambda i: (0, 0, 0)),
            pl.BlockSpec((ny, rows, width), lambda i: (0, 1, 0)),
            pl.BlockSpec((experts, top, total), lambda i: (0, 0, 0)),
        ],
        out_specs=pl.BlockSpec(pieces, lambda i: (0, 0, 0, 0)),
        out_shape=jax.ShapeDtypeStruct(pieces, BF16),
        compiler_params=pltpu.CompilerParams(vmem_limit_bytes=VMEM_BYTES),
        cost_estimate=pl.CostEstimate(
            flops=2 * mats * parts * stored * width * total,
            bytes_accessed=2 * mats * (parts * stored * width + top * many * total)
            + 4 * total * width,
            transcendentals=0,
        ),
        name="pick",
    )(weights, everything, everything, mask)


def middle_kernel(top, arrived_ref, scale_ref, out_ref):
    nx = arrived_ref.shape[0]

    def add_up(which):
        value = arrived_ref[0, which].astype(F32)
        for q in range(1, nx):
            value = value + arrived_ref[q, which].astype(F32)
        return value

    for k in range(top):
        scale = scale_ref[k : k + 1]
        gate, up, dh = add_up(k), add_up(top + k), scale * add_up(2 * top + k)
        sg = jax.nn.sigmoid(gate)
        active = gate * sg
        dgate = (dh * up * sg * (1.0 + gate * (1.0 - sg))).astype(BF16)
        dup = (dh * active).astype(BF16)
        hidden = (scale * (active * up)).astype(BF16)
        for q in range(nx):
            out_ref[q, k] = dgate
            out_ref[q, top + k] = dup
            out_ref[q, 2 * top + k] = hidden


def middle(arrived, scale):
    return pl.pallas_call(
        functools.partial(middle_kernel, scale.shape[0]),
        out_shape=jax.ShapeDtypeStruct(arrived.shape, BF16),
        compiler_params=pltpu.CompilerParams(vmem_limit_bytes=VMEM_BYTES),
        cost_estimate=pl.CostEstimate(
            flops=6 * arrived.size, bytes_accessed=4 * arrived.size, transcendentals=arrived.size
        ),
        name="middle",
    )(arrived, scale)


def output_kernel(top, nx, experts, shared_ref, weight_ref, mask_ref, wide_ref, out_ref):
    share = shared_ref.shape[3]
    mats, parts, stored = weight_ref.shape[:3]
    units = stored // experts
    ny, _, rows, width = out_ref.shape
    for m in range(mats):
        values = [
            [shared_ref[q, m * top + k].astype(F32) for k in range(top)] for q in range(nx)
        ]
        for p in range(parts):
            pieces = []
            for e in range(experts):
                line = []
                for q in range(nx):
                    piece = None
                    for k in range(top):
                        value = values[q][k][p * units : (p + 1) * units]
                        term = value * mask_ref[e, k : k + 1, q * share : (q + 1) * share]
                        piece = term if piece is None else piece + term
                    line.append(piece)
                pieces.append(jnp.concatenate(line, axis=1))
            wide_ref[p, m] = jnp.concatenate(pieces, axis=0).astype(BF16)
    for which, members in ((0, range(mats - 1, mats)), (1, range(mats - 1))):
        product = None
        for m in members:
            for p in range(parts):
                term = contract_first(wide_ref[p, m], weight_ref[m, p])
                product = term if product is None else product + term
        out_ref[:, which] = product.astype(BF16).reshape(ny, rows, width)


def output(shared, weights, experts, mask, ny):
    mats, parts, stored, width = weights.shape
    top, total = mask.shape[1:]
    nx = shared.shape[0]
    both = (ny, 2, total // ny, width)
    wide = (parts, mats, stored, total)
    return pl.pallas_call(
        functools.partial(output_kernel, top, nx, experts),
        grid=(1,),
        in_specs=[
            pl.BlockSpec(shared.shape, lambda i: (0, 0, 0, 0)),
            pl.BlockSpec(weights.shape, lambda i: (0, 0, 0, 0)),
            pl.BlockSpec((experts, top, total), lambda i: (0, 0, 0)),
        ],
        out_specs=[
            pl.BlockSpec(wide, lambda i: (0, 0, 0, 0)),
            pl.BlockSpec(both, lambda i: (0, 0, 0, 0)),
        ],
        out_shape=[jax.ShapeDtypeStruct(wide, BF16), jax.ShapeDtypeStruct(both, BF16)],
        compiler_params=pltpu.CompilerParams(vmem_limit_bytes=VMEM_BYTES),
        cost_estimate=pl.CostEstimate(
            flops=2 * mats * parts * stored * width * total,
            bytes_accessed=2 * (mats * parts * stored * (width + total) + 2 * total * width),
            transcendentals=0,
        ),
        name="output",
    )(shared, weights, mask)


def body(tokens, slot_ids, gate_values, slot_expert, w_gate, w_up, w_down, cotangent):
    block, width = tokens.shape
    experts, units, _ = w_gate.shape
    ny, nh, nl, nx = (lax.axis_size(a) for a in ("y", "zh", "zl", "x"))
    top = slot_ids.shape[1]
    rows = block // nl
    total = ny * rows
    share = total // nx
    many = 2 * nl * units
    stored = experts * units

    def own_rows(value):
        return lax.dynamic_slice_in_dim(value, lax.axis_index("zl") * rows, rows, axis=0)

    ids, values = own_rows(slot_ids), own_rows(gate_values)
    numbers = jnp.arange(slot_expert.shape[0], dtype=jnp.int32)
    chosen = jnp.sum(
        jnp.where(ids[:, :, None] == numbers, slot_expert[None, None, :], 0), axis=-1
    ).astype(F32)
    part0 = short(values)
    part1 = short(values - part0)
    part2 = short(values - part0 - part1)
    meta = jnp.stack([chosen, part0, part1, part2]).transpose(0, 2, 1).astype(BF16)
    facts_of = 4 * top * rows
    meta = jnp.pad(meta.reshape(1, facts_of), ((0, 15), (0, width - facts_of)))
    packed = jnp.concatenate([own_rows(tokens), own_rows(cotangent), meta], axis=0)
    held = packed.shape[0]
    everything = lax.all_gather(packed, "y", axis=0, tiled=True).reshape(ny, held, width)

    own = jnp.stack([w_gate, w_up, w_down]).reshape(3, 1, stored, width)
    near = swap(own, "zl")
    weights = jnp.concatenate([own, near, swap(own, "core"), swap(near, "core")], axis=1)
    everything, weights = lax.optimization_barrier((everything, weights))

    facts = everything[:, 2 * rows, :facts_of].reshape(ny, 4, top, rows).astype(F32)
    facts = facts.transpose(1, 2, 0, 3).reshape(4, top, total)
    scale = facts[1] + facts[2] + facts[3]
    mask = (facts[0][None] == jnp.arange(experts, dtype=F32)[:, None, None]).astype(F32)
    own_scale = lax.dynamic_slice_in_dim(scale, lax.axis_index("x") * share, share, axis=1)

    def exchange(value):
        return lax.all_to_all(value, "x", split_axis=0, concat_axis=0, tiled=True)

    picked = pick(weights, experts, everything, mask, rows, nx)
    shared = exchange(middle(exchange(picked), own_scale))
    wide, parts = output(shared, weights, experts, mask, ny)
    small = rows // nh
    parts = lax.psum_scatter(
        parts.reshape(ny * 2 * rows, width), "y", scatter_dimension=0, tiled=True
    )

    rows_x = everything[:, :rows].reshape(total, width)
    rows_c = everything[:, rows : 2 * rows].reshape(total, width)

    def products(wide):
        groups = ((wide[:, :2], rows_x), (wide[:, 2:], rows_c))
        return [
            jnp.dot(left.reshape(-1, total), right, preferred_element_type=F32).reshape(
                nl, -1, stored, width
            )
            for left, right in groups
        ]

    sent = [swap(value.astype(BF16), "core").astype(F32) for value in products(wide[nl:])]
    kept = products(wide[:nl])
    near = [swap((a[1] + b[1]).astype(BF16), "zl") for a, b in zip(kept, sent)]
    parts, near[0], near[1] = lax.optimization_barrier((parts, near[0], near[1]))
    done = [
        (a[0] + b[0] + c.astype(F32)).astype(BF16).reshape(-1, experts, units, width)
        for a, b, c in zip(kept, sent, near)
    ]

    parts = parts.reshape(2, nh, small, width).transpose(1, 0, 2, 3)
    parts = lax.all_to_all(parts, "zh", split_axis=0, concat_axis=0, tiled=True)
    parts = jnp.sum(parts.astype(F32), axis=0).astype(BF16)
    ends = spread(parts, ("zh", "zl"), nh * nl)
    ends = ends.reshape(nh, nl, 2, small, width).transpose(2, 1, 0, 3, 4).reshape(2, block, width)
    return (ends[0], ends[1], done[0][0], done[0][1], done[1][0])


def solution(mesh):
    dp, ep, mp = mesh.shape["dp"], mesh.shape["expert"], mesh.shape["mp"]
    split = Mesh(
        mesh.devices.reshape(dp // 2, 2, ep // 2, 2, mp), ("y", "core", "zh", "zl", "x")
    )
    rows = ("y", "core")
    stored = P(None, ("y", "core", "zh", "zl"), "x")
    return jax.shard_map(
        body,
        mesh=split,
        in_specs=(
            P(rows, "x"),
            P(rows, None),
            P(rows, None),
            P(),
            stored,
            stored,
            stored,
            P(rows, "x"),
        ),
        out_specs=(P(rows, "x"), P(rows, "x"), stored, stored, stored),
        check_vma=False,
    )
```

time: 238 us -> 216 us (0.908)
  starting transfers between devices: 75 us -> 26.8 us
  blocking collectives: 0 us -> 34.7 us
  waiting for transfers between devices: 72.4 us -> 91.3 us
  other arithmetic: 26.3 us -> 12.4 us
  local copies, waits for them, and re-layouts: 23.3 us -> 14.7 us
  Pallas kernels: 20.8 us -> 15.3 us
    all_to_all x0 -> x2, blocking collectives: none -> 34.7 us  [the longest x1 18.1 us: body(): parts = lax.all_to_all(parts, 'zh', split_axis=0, concat_axis=0, tiled=True)]
    ppermute x9 -> x7, waiting for transfers between devices: 31.5 us -> 57.6 us  [swap(): return lax.ppermute(value, axis, [(0, 1), (1, 0)])]
    all_to_all x5 -> x1, starting transfers between devices: 28 us -> 4.8 us  [exchange(): return lax.all_to_all(value, 'x', split_axis=0, concat_axis=0, tiled=True)]
    all_to_all x4 -> x1, starting transfers between devices: 17.9 us -> 3.49 us  [spread(): return lax.all_to_all(copies, axis, split_axis=0, concat_axis=0, tiled=True)]
    ppermute x9 -> x7, starting transfers between devices: 29.1 us -> 18.4 us  [swap(): return lax.ppermute(value, axis, [(0, 1), (1, 0)])]
    add x3 -> x0, other arithmetic: 7.3 us -> none  [weight_gradient(): part = part[:, :, 0].astype(F32) + sent.astype(F32)]
    pallas_call x4 -> x3, Pallas kernels: 20.8 us -> 15.3 us  [the longest x1 7.56 us: pick(): pl.pallas_call(functools.partial(pick_kernel, top, nx, experts), grid=(1,...]
    convert_element_type x3 -> x0, local copies, waits for them, and re-layouts: 4.89 us -> none  [weight_gradient(): sent = swap(part[:, 1].astype(BF16), 'zl')]
  transfers between devices with their start and end apart: 20 -> 11, of which waited for: 10 -> 7; matrix products, arithmetic and copies ran while one was open for 18% -> 7% of each run, Pallas kernels for 7% -> 0%
where the time goes in v3:
time: 216 us; the launch traced here: 213 us
  waiting for transfers between devices  91.3 us (42%)
  blocking collectives  34.7 us (16%)
  starting transfers between devices  26.8 us (12%)
  Pallas kernels  15.3 us (7%)
  local copies, waits for them, and re-layouts  14.7 us (7%)
  between operations  14.4 us (7%)
  other arithmetic  12.4 us (6%)
  matrix products  3.55 us (2%)
    ppermute x7, waiting for transfers between devices, swap(): return lax.ppermute(value, axis, [(0, 1), (1, 0)])  57.6 us
    ppermute x7, starting transfers between devices, swap(): return lax.ppermute(value, axis, [(0, 1), (1, 0)])  18.4 us
    all_to_all x1, blocking collectives, body(): parts = lax.all_to_all(parts, 'zh', split_axis=0, concat_axis=0, tiled=True)  18.1 us
    all_to_all x1, blocking collectives, exchange(): return lax.all_to_all(value, 'x', split_axis=0, concat_axis=0, tiled=True)  16.6 us
    all_to_all x1, waiting for transfers between devices, exchange(): return lax.all_to_all(value, 'x', split_axis=0, concat_axis=0, tiled=True)  13.3 us
    all_to_all x1, waiting for transfers between devices, spread(): return lax.all_to_all(copies, axis, split_axis=0, concat_axis=0, tiled=True)  10.5 us
    unnamed x30, local copies, waits for them, and re-layouts  8.3 us
    pallas_call x1, Pallas kernels, pick(): pl.pallas_call(functools.partial(pick_kernel, top, nx, experts), grid=(1,...  7.56 us
  transfers between devices with their start and end apart: 11, of which 7 were waited for; matrix products, arithmetic and copies ran while one was open for 7% of the time, Pallas kernels for 0%

profile of v3, /device:TPU:6, one launch (start us, length us, event | category | flops | bytes accessed | tf_op | source)
XLA Modules:
  0.0 213.0 jit_solution(7802996216324611455)
XLA Ops:
  7.2 0.0 copy-start
  7.2 0.0 all-gather.2.cloned.1.call-start
  7.2 0.6 copy-done
  7.9 0.1 constant_dynamic-slice_fusion.2
  7.9 0.7 select_reduce_fusion
  8.7 0.8 fusion.20
  9.4 0.1 reshape.104
  9.5 1.0 constant_dynamic-slice_fusion.3
  10.5 0.0 copy-start.9
  10.5 0.0 copy-start.10
  10.5 0.7 fusion.16
  11.3 0.0 all-gather.2.cloned.1.call-update
  11.3 1.4 pad_maximum_fusion.1
  12.8 4.3 %collective-permute-start = (bf16[3,1,224,1024]{3,2,1,0:T(8,128)(2,1)S(1)}, bf16[3,1,224,1024]{3,2,1,0:T(8,128)(2,1)S(1)}, u32[]{:S(2)}, u32[]{:S(2)}) collective-permute-start(bf16[3,1,224,1024]{3,2,1,0:T(8,128)(2,1)S(1)} %pad_maximum_fusion.1), channel_id=1, source_target_pairs={{0,4},{4,0},{1,5},{5,1},{2,6},{6,2},{3,7},{7,3},{8,12},{12,8},{9,1... | collective-permute-start | bytes 4128776 | tf_op jit(solution)/shard_map/ppermute | solution.py:19
  17.0 1.9 collective-permute-start.1
  19.0 28.2 %collective-permute-done = bf16[3,1,224,1024]{3,2,1,0:T(8,128)(2,1)S(1)} collective-permute-done((bf16[3,1,224,1024]{3,2,1,0:T(8,128)(2,1)S(1)}, bf16[3,1,224,1024]{3,2,1,0:T(8,128)(2,1)S(1)}, u32[]{:S(2)}, u32[]{:S(2)}) %collective-permute-start) | collective-permute-done | bytes 1376288 | tf_op jit(solution)/shard_map/ppermute | solution.py:19
  47.2 1.9 collective-permute-start.2
  49.1 3.1 %collective-permute-done.2 = bf16[3,1,224,1024]{3,2,1,0:T(8,128)(2,1)S(1)} collective-permute-done((bf16[3,1,224,1024]{3,2,1,0:T(8,128)(2,1)S(1)}, bf16[3,1,224,1024]{3,2,1,0:T(8,128)(2,1)S(1)}, u32[]{:S(2)}, u32[]{:S(2)}) %collective-permute-start.2) | collective-permute-done | bytes 1376288 | tf_op jit(solution)/shard_map/ppermute | solution.py:19
  52.2 3.4 %pad_maximum_fusion.weight_ref = bf16[3,4,224,1024]{3,2,1,0:T(8,128)(2,1)} fusion(bf16[3,1,224,1024]{3,2,1,0:T(8,128)(2,1)S(1)} %collective-permute-done.2, bf16[3,1,224,1024]{3,2,1,0:T(8,128)(2,1)S(1)} %collective-permute-done.1, bf16[3,1,224,1024]{3,2,1,0:T(8,128)(2,1)S(1)} %collective-permute-done, bf16[1,1,224,1024]{3,2,1,0:T(8,128)(2,1)S(1)} %bitcast.112, ...), kind=kLoop, calls=%fused_computation | loop fusion | flops 13762560 | bytes 11010048 | tf_op jit(solution)/shard_map/concatenate | solution.py:212
  55.6 4.8 %all-gather.2.cloned.1.call-done = bf16[1152,1024]{1,0:T(8,128)(2,1)} async-done(((bf16[144,1024]{1,0:T(8,128)(2,1)}), bf16[1152,1024]{1,0:T(8,128)(2,1)}) %all-gather.2.cloned.1.call-update) | async-done | bytes 2359312 | tf_op jit(solution)/shard_map/all_gather | solution.py:208
  60.4 0.9 convert_reduce_fusion
  61.3 0.1 reshape.113
  61.4 0.1 eq.31
  61.5 1.7 copy-done.1
  63.2 7.6 %pick.1 = bf16[4,6,224,128]{3,2,1,0:T(8,128)(2,1)} custom-call(bf16[3,4,224,1024]{3,2,1,0:T(8,128)(2,1)} %pad_maximum_fusion.weight_ref, bf16[8,144,1024]{2,1,0:T(8,128)(2,1)S(1)} %bitcast.98, bf16[8,144,1024]{2,1,0:T(8,128)(2,1)S(1)} %bitcast.99, f32[4,2,512]{2,1,0:T(2,128)S(1)} %compare_convert_fusion.mask_ref), custom_call_target="tpu_custom_call" | custom-call | flops 2818572288 | bytes 8978432 | tf_op jit(solution)/shard_map/pick/pallas_call | solution.py:64
  70.7 4.8 %all-to-all-start = ((bf16[4,6,224,128]{3,2,1,0:T(8,128)(2,1)}), bf16[4,6,224,128]{3,2,1,0:T(8,128)(2,1)S(1)}, u32[]{:S(2)}, u32[]{:S(2)}) async-start(bf16[4,6,224,128]{3,2,1,0:T(8,128)(2,1)} %pick.1), calls=%async_computation | async-start | bytes 2752512 | tf_op jit(solution)/shard_map/all_to_all | solution.py:222
  75.5 0.1 add.48
  75.6 13.3 %all-to-all-done.arrived_ref = bf16[4,6,224,128]{3,2,1,0:T(8,128)(2,1)S(1)} async-done(((bf16[4,6,224,128]{3,2,1,0:T(8,128)(2,1)}), bf16[4,6,224,128]{3,2,1,0:T(8,128)(2,1)S(1)}, u32[]{:S(2)}, u32[]{:S(2)}) %all-to-all-start) | async-done | bytes 1376288 | tf_op jit(solution)/shard_map/all_to_all | solution.py:222
  88.9 0.3 middle.1
  89.2 16.6 %all_to_all.20.shared_ref = bf16[4,6,224,128]{3,2,1,0:T(8,128)(2,1)S(1)} all-to-all(bf16[4,6,224,128]{3,2,1,0:T(8,128)(2,1)S(1)} %middle.1), channel_id=1, replica_groups=mesh['y'=8,'core'=2,'zh'=4,'zl'=2,'x'=4] {'x'}, dimensions={0} | all-to-all | bytes 2752512 | tf_op jit(solution)/shard_map/all_to_all | solution.py:222
  105.8 7.4 %output.1 = (bf16[4,3,224,512]{3,2,1,0:T(8,128)(2,1)}, bf16[8,2,64,1024]{3,2,1,0:T(8,128)(2,1)S(1)}) custom-call(bf16[4,6,224,128]{3,2,1,0:T(8,128)(2,1)S(1)} %all_to_all.20.shared_ref, bf16[3,4,224,1024]{3,2,1,0:T(8,128)(2,1)} %pad_maximum_fusion.weight_ref, f32[4,2,512]{2,1,0:T(2,128)S(1)} %compare_convert_fusion.mask_ref), custom_call_target="tpu_custom_call" | custom-call | flops 2818572288 | bytes 10354688 | tf_op jit(solution)/shard_map/output/pallas_call | solution.py:158
  113.2 1.4 copy-done.3
  114.5 0.0 reduce-scatter.2.cloned.1.call-update
  114.6 0.2 fusion.24
  114.8 1.6 copy-done.12
  116.4 1.1 convolution_convert_fusion
  117.5 1.9 collective-permute-start.3
  119.5 0.1 slice.92
  119.5 0.6 fusion.5
  120.2 2.6 %collective-permute-start.5 = (bf16[2,1,224,1024]{3,2,1,0:T(8,128)(2,1)S(1)}, bf16[2,1,224,1024]{3,2,1,0:T(8,128)(2,1)S(1)}, u32[]{:S(2)}, u32[]{:S(2)}) collective-permute-start(bf16[2,1,224,1024]{3,2,1,0:T(8,128)(2,1)S(1)} %fusion.5), channel_id=1, source_target_pairs={{0,32},{32,0},{1,33},{33,1},{2,34},{34,2},{3,35},{35,3},{4,36},{36... | collective-permute-start | bytes 2752520 | tf_op jit(solution)/shard_map/ppermute | solution.py:19
  122.8 1.1 fusion.27
  123.9 0.4 fusion.23
  124.3 0.4 convert_element_type.70
  124.7 0.4 fusion.4
  125.2 1.3 copy-done.4
  126.5 3.6 %collective-permute-start.4 = (bf16[2,224,1024]{2,1,0:T(8,128)(2,1)S(1)}, bf16[2,224,1024]{2,1,0:T(8,128)(2,1)S(1)}, u32[]{:S(2)}, u32[]{:S(2)}) collective-permute-start(bf16[2,224,1024]{2,1,0:T(8,128)(2,1)S(1)} %fusion.4), channel_id=1, source_target_pairs={{0,4},{4,0},{1,5},{5,1},{2,6},{6,2},{3,7},{7,3},{8,12},{12,8},{9,1... | collective-permute-start | bytes 2752520 | tf_op jit(solution)/shard_map/ppermute | solution.py:19
  130.1 0.6 fusion.28
  130.8 0.2 convert_element_type.74
  131.0 0.1 fusion.13
  131.1 0.9 copy-done.5
  132.0 2.2 %collective-permute-start.6 = (bf16[1,224,1024]{2,1,0:T(8,128)(2,1)S(1)}, bf16[1,224,1024]{2,1,0:T(8,128)(2,1)S(1)}, u32[]{:S(2)}, u32[]{:S(2)}) collective-permute-start(bf16[1,224,1024]{2,1,0:T(8,128)(2,1)S(1)} %fusion.13), channel_id=1, source_target_pairs={{0,4},{4,0},{1,5},{5,1},{2,6},{6,2},{3,7},{7,3},{8,12},{12,8},{9,1... | collective-permute-start | bytes 1376264 | tf_op jit(solution)/shard_map/ppermute | solution.py:19
  134.2 26.2 %collective-permute-done.6 = bf16[1,224,1024]{2,1,0:T(8,128)(2,1)S(1)} collective-permute-done((bf16[1,224,1024]{2,1,0:T(8,128)(2,1)S(1)}, bf16[1,224,1024]{2,1,0:T(8,128)(2,1)S(1)}, u32[]{:S(2)}, u32[]{:S(2)}) %collective-permute-start.6) | collective-permute-done | bytes 458784 | tf_op jit(solution)/shard_map/ppermute | solution.py:19
  160.5 5.1 %reduce-scatter.2.cloned.1.call-done = bf16[128,1024]{1,0:T(8,128)(2,1)} async-done(((bf16[1024,1024]{1,0:T(8,128)(2,1)}), bf16[128,1024]{1,0:T(8,128)(2,1)}) %reduce-scatter.2.cloned.1.call-update) | async-done | bytes 262160 | tf_op jit(solution)/shard_map/reduce_scatter | solution.py:228
  165.6 1.0 copy.31
  166.5 18.1 %all_to_all.21 = bf16[4,2,16,1024]{3,2,1,0:T(8,128)(2,1)S(1)} all-to-all(bf16[4,2,16,1024]{3,2,1,0:T(8,128)(2,1)S(1)} %copy.31), channel_id=1, replica_groups=mesh['y'=8,'core'=2,'zh'=4,'zl'=2,'x'=4] {'zh'}, dimensions={0} | all-to-all | bytes 524288 | tf_op jit(solution)/shard_map/all_to_all | solution.py:254
  184.7 0.9 broadcast_in_dim.24
  185.6 3.5 %all-to-all-start.3 = ((bf16[8,2,16,1024]{3,2,1,0:T(8,128)(2,1)}), bf16[8,2,16,1024]{3,2,1,0:T(8,128)(2,1)S(1)}, u32[]{:S(2)}, u32[]{:S(2)}) async-start(bf16[8,2,16,1024]{3,2,1,0:T(8,128)(2,1)} %broadcast_in_dim.24), calls=%async_computation.4 | async-start | bytes 1048576 | tf_op jit(solution)/shard_map/all_to_all | solution.py:33
  189.1 2.2 %fusion.2 = bf16[2,224,1024]{2,1,0:T(8,128)(2,1)S(1)} fusion(f32[2,224,1024]{2,1,0:T(8,128)S(1)} %bitcast.103, f32[2,2,224,1024]{3,2,1,0:T(8,128)} %copy-done.4, bf16[2,224,1024]{2,1,0:T(8,128)(2,1)S(1)} %collective-permute-done.4), kind=kLoop, calls=%fused_computation.4 | loop fusion | flops 1835008 | bytes 5505024 | tf_op jit(solution)/shard_map/convert_element_type | solution.py:249
  191.3 1.0 fusion.25
  192.3 0.8 copy-done.6
  193.1 1.0 fusion.9
  194.1 10.5 %all-to-all-done.3 = bf16[8,2,16,1024]{3,2,1,0:T(8,128)(2,1)S(1)} async-done(((bf16[8,2,16,1024]{3,2,1,0:T(8,128)(2,1)}), bf16[8,2,16,1024]{3,2,1,0:T(8,128)(2,1)S(1)}, u32[]{:S(2)}, u32[]{:S(2)}) %all-to-all-start.3) | async-done | bytes 524320 | tf_op jit(solution)/shard_map/all_to_all | solution.py:33
  204.7 0.7 copy.33
  205.4 0.7 copy.32
  (34 shorter events, 0.2 us)
Async XLA Ops:
  7.2 0.7 copy-start
  7.2 53.2 %all-gather.2.cloned.1.call-start = ((), (), s32[]{:S(2)}) async-start(), calls=%async_computation.5 | async-start | bytes 2654208 | tf_op jit(solution)/shard_map/all_gather | solution.py:208
  10.5 41.7 %copy-start.9 = (bf16[4,56,1024]{2,1,0:T(8,128)(2,1)S(1)}, bf16[4,56,1024]{2,1,0:T(8,128)(2,1)}, u32[]{:S(2)}) copy-start(bf16[4,56,1024]{2,1,0:T(8,128)(2,1)} %param.14) | copy-start | bytes 1376260
  10.5 41.7 %copy-start.10 = (bf16[4,56,1024]{2,1,0:T(8,128)(2,1)S(1)}, bf16[4,56,1024]{2,1,0:T(8,128)(2,1)}, u32[]{:S(2)}) copy-start(bf16[4,56,1024]{2,1,0:T(8,128)(2,1)} %param.13) | copy-start | bytes 1376260
  10.5 41.7 %copy-start.11 = (bf16[4,56,1024]{2,1,0:T(8,128)(2,1)S(1)}, bf16[4,56,1024]{2,1,0:T(8,128)(2,1)}, u32[]{:S(2)}) copy-start(bf16[4,56,1024]{2,1,0:T(8,128)(2,1)} %param.12) | copy-start | bytes 1376260
  12.8 34.5 %collective-permute-start = (bf16[3,1,224,1024]{3,2,1,0:T(8,128)(2,1)S(1)}, bf16[3,1,224,1024]{3,2,1,0:T(8,128)(2,1)S(1)}, u32[]{:S(2)}, u32[]{:S(2)}) collective-permute-start(bf16[3,1,224,1024]{3,2,1,0:T(8,128)(2,1)S(1)} %pad_maximum_fusion.1), channel_id=1, source_target_pairs={{0,4},{4,0},{1,5},{5,1},{2,6},{6,2},{3,7},{7,3},{8,12},{12,8},{9,1... | collective-permute-start | bytes 4128776 | tf_op jit(solution)/shard_map/ppermute | solution.py:19
  17.0 32.1 %collective-permute-start.1 = (bf16[3,1,224,1024]{3,2,1,0:T(8,128)(2,1)S(1)}, bf16[3,1,224,1024]{3,2,1,0:T(8,128)(2,1)S(1)}, u32[]{:S(2)}, u32[]{:S(2)}) collective-permute-start(bf16[3,1,224,1024]{3,2,1,0:T(8,128)(2,1)S(1)} %pad_maximum_fusion.1), channel_id=1, source_target_pairs={{0,32},{32,0},{1,33},{33,1},{2,34},{34,2},{3,35},{35,3},{4,36},{36... | collective-permute-start | bytes 4128776 | tf_op jit(solution)/shard_map/ppermute | solution.py:19
  47.2 5.0 %collective-permute-start.2 = (bf16[3,1,224,1024]{3,2,1,0:T(8,128)(2,1)S(1)}, bf16[3,1,224,1024]{3,2,1,0:T(8,128)(2,1)S(1)}, u32[]{:S(2)}, u32[]{:S(2)}) collective-permute-start(bf16[3,1,224,1024]{3,2,1,0:T(8,128)(2,1)S(1)} %collective-permute-done), channel_id=1, source_target_pairs={{0,32},{32,0},{1,33},{33,1},{2,34},{34,2},{3,35},{35,3},{4,36},{36... | collective-permute-start | bytes 4128776 | tf_op jit(solution)/shard_map/ppermute | solution.py:19
  61.5 1.7 copy-start.1
  70.7 18.2 %all-to-all-start = ((bf16[4,6,224,128]{3,2,1,0:T(8,128)(2,1)}), bf16[4,6,224,128]{3,2,1,0:T(8,128)(2,1)S(1)}, u32[]{:S(2)}, u32[]{:S(2)}) async-start(bf16[4,6,224,128]{3,2,1,0:T(8,128)(2,1)} %pick.1), calls=%async_computation | async-start | bytes 2752512 | tf_op jit(solution)/shard_map/all_to_all | solution.py:222
  75.5 90.1 %reduce-scatter.2.cloned.1.call-start = ((), (), s32[]{:S(2)}) async-start(), calls=%async_computation.6 | async-start | bytes 2359296 | tf_op jit(solution)/shard_map/reduce_scatter | solution.py:228
  105.7 8.8 %copy-start.2 = (bf16[1152,1024]{1,0:T(8,128)(2,1)S(1)}, bf16[1152,1024]{1,0:T(8,128)(2,1)}, u32[]{:S(2)}) copy-start(bf16[1152,1024]{1,0:T(8,128)(2,1)} %all-gather.2.cloned.1.call-done) | copy-start | bytes 7077892
  113.2 1.4 copy-start.3
  114.6 1.8 copy-start.12
  117.5 6.8 %collective-permute-start.3 = (bf16[2,2,224,1024]{3,2,1,0:T(8,128)(2,1)S(1)}, bf16[2,2,224,1024]{3,2,1,0:T(8,128)(2,1)S(1)}, u32[]{:S(2)}, u32[]{:S(2)}) collective-permute-start(bf16[2,2,224,1024]{3,2,1,0:T(8,128)(2,1)S(1)} %convolution_convert_fusion), channel_id=1, source_target_pairs={{0,32},{32,0},{1,33},{33,1},{2,34},{34,2},{3,35},{35,3},{4,36},{36... | collective-permute-start | bytes 5505032 | tf_op jit(solution)/shard_map/ppermute | solution.py:19
  120.2 10.6 %collective-permute-start.5 = (bf16[2,1,224,1024]{3,2,1,0:T(8,128)(2,1)S(1)}, bf16[2,1,224,1024]{3,2,1,0:T(8,128)(2,1)S(1)}, u32[]{:S(2)}, u32[]{:S(2)}) collective-permute-start(bf16[2,1,224,1024]{3,2,1,0:T(8,128)(2,1)S(1)} %fusion.5), channel_id=1, source_target_pairs={{0,32},{32,0},{1,33},{33,1},{2,34},{34,2},{3,35},{35,3},{4,36},{36... | collective-permute-start | bytes 2752520 | tf_op jit(solution)/shard_map/ppermute | solution.py:19
  124.7 1.8 copy-start.4
  126.5 34.0 %collective-permute-start.4 = (bf16[2,224,1024]{2,1,0:T(8,128)(2,1)S(1)}, bf16[2,224,1024]{2,1,0:T(8,128)(2,1)S(1)}, u32[]{:S(2)}, u32[]{:S(2)}) collective-permute-start(bf16[2,224,1024]{2,1,0:T(8,128)(2,1)S(1)} %fusion.4), channel_id=1, source_target_pairs={{0,4},{4,0},{1,5},{5,1},{2,6},{6,2},{3,7},{7,3},{8,12},{12,8},{9,1... | collective-permute-start | bytes 2752520 | tf_op jit(solution)/shard_map/ppermute | solution.py:19
  130.7 1.2 copy-start.5
  131.0 3.3 %copy-start.7 = (f32[2,1,224,1024]{3,2,1,0:T(8,128)}, f32[2,1,224,1024]{3,2,1,0:T(8,128)S(1)}, u32[]{:S(2)}) copy-start(f32[2,1,224,1024]{3,2,1,0:T(8,128)S(1)} %convert_element_type.74) | copy-start | bytes 5505028
  132.0 28.5 %collective-permute-start.6 = (bf16[1,224,1024]{2,1,0:T(8,128)(2,1)S(1)}, bf16[1,224,1024]{2,1,0:T(8,128)(2,1)S(1)}, u32[]{:S(2)}, u32[]{:S(2)}) collective-permute-start(bf16[1,224,1024]{2,1,0:T(8,128)(2,1)S(1)} %fusion.13), channel_id=1, source_target_pairs={{0,4},{4,0},{1,5},{5,1},{2,6},{6,2},{3,7},{7,3},{8,12},{12,8},{9,1... | collective-permute-start | bytes 1376264 | tf_op jit(solution)/shard_map/ppermute | solution.py:19
  160.5 5.1 %copy-start.13 = (bf16[1,224,1024]{2,1,0:T(8,128)(2,1)}, bf16[1,224,1024]{2,1,0:T(8,128)(2,1)S(1)}, u32[]{:S(2)}) copy-start(bf16[1,224,1024]{2,1,0:T(8,128)(2,1)S(1)} %collective-permute-done.6) | copy-start | bytes 1376260
  185.6 19.1 %all-to-all-start.3 = ((bf16[8,2,16,1024]{3,2,1,0:T(8,128)(2,1)}), bf16[8,2,16,1024]{3,2,1,0:T(8,128)(2,1)S(1)}, u32[]{:S(2)}, u32[]{:S(2)}) async-start(bf16[8,2,16,1024]{3,2,1,0:T(8,128)(2,1)} %broadcast_in_dim.24), calls=%async_computation.4 | async-start | bytes 1048576 | tf_op jit(solution)/shard_map/all_to_all | solution.py:33
  189.1 3.2 %copy-start.8 = (f32[2,1,224,1024]{3,2,1,0:T(8,128)S(1)}, f32[2,1,224,1024]{3,2,1,0:T(8,128)}, u32[]{:S(2)}) copy-start(f32[2,1,224,1024]{3,2,1,0:T(8,128)} %copy-done.7) | copy-start | bytes 5505028
  189.1 3.2 %copy-start.14 = (bf16[1,224,1024]{2,1,0:T(8,128)(2,1)S(1)}, bf16[1,224,1024]{2,1,0:T(8,128)(2,1)}, u32[]{:S(2)}) copy-start(bf16[1,224,1024]{2,1,0:T(8,128)(2,1)} %copy-done.13) | copy-start | bytes 1376260
  191.3 1.8 copy-start.6
Sparse Core Ops, SparseCore 0:
  11.4 48.9 all-gather.1
  114.7 50.8 reduce-scatter.1

commit v4 on v3

v4 whole, which is shorter than its diff:
```python
import functools
import jax
import jax.numpy as jnp
from jax import lax
from jax.experimental import pallas as pl
from jax.experimental.pallas import tpu as pltpu
from jax.sharding import Mesh, PartitionSpec as P

F32 = jnp.float32
BF16 = jnp.bfloat16
VMEM_BYTES = 24 * 1024 * 1024


def short(value):
    return lax.reduce_precision(value, exponent_bits=8, mantissa_bits=7)


def swap(value, axis):
    return lax.ppermute(value, axis, [(0, 1), (1, 0)])


def contract_last(left, right):
    return lax.dot_general(left, right, (((1,), (1,)), ((), ())), preferred_element_type=F32)


def contract_first(left, right):
    return lax.dot_general(left, right, (((0,), (0,)), ((), ())), preferred_element_type=F32)


def spread(value, axis, count):
    copies = jnp.broadcast_to(value[None], (count,) + value.shape)
    copies = lax.optimization_barrier(copies)
    return lax.all_to_all(copies, axis, split_axis=0, concat_axis=0, tiled=True)


def pick_kernel(experts, *refs):
    *weight_refs, rows_ref, mask_ref, out_ref = refs
    rows = rows_ref[...].reshape(-1, rows_ref.shape[2])
    units = weight_refs[0].shape[1] // experts
    nx, top, _, share = out_ref.shape
    picked = [[] for _ in range(top)]
    for weight_ref in weight_refs:
        sums = contract_last(weight_ref[0], rows)
        for k in range(top):
            value = None
            for e in range(experts):
                term = sums[e * units : (e + 1) * units] * mask_ref[e, k : k + 1]
                value = term if value is None else value + term
            picked[k].append(value)
    for k in range(top):
        value = jnp.concatenate(picked[k], axis=0).astype(BF16)
        for q in range(nx):
            out_ref[q, k] = value[:, q * share : (q + 1) * share]


def pick(weights, experts, everything, mask, rows, nx):
    parts = len(weights)
    mats, stored, width = weights[0].shape
    top, total = mask.shape[1:]
    ny = everything.shape[0]
    many = parts * stored // experts
    return pl.pallas_call(
        functools.partial(pick_kernel, experts),
        grid=(mats,),
        in_specs=[pl.BlockSpec((1, stored, width), lambda m: (m, 0, 0))] * parts
        + [
            pl.BlockSpec((ny, rows, width), lambda m: (0, m // (mats - 1), 0)),
            pl.BlockSpec((experts, top, total), lambda m: (0, 0, 0)),
        ],
        out_specs=pl.BlockSpec((nx, top, many, total // nx), lambda m: (0, m, 0, 0)),
        out_shape=jax.ShapeDtypeStruct((nx, mats * top, many, total // nx), BF16),
        compiler_params=pltpu.CompilerParams(vmem_limit_bytes=VMEM_BYTES),
        cost_estimate=pl.CostEstimate(
            flops=2 * mats * parts * stored * width * total,
            bytes_accessed=2 * mats * (parts * stored * width + top * many * total)
            + 4 * total * width,
            transcendentals=0,
        ),
        name="pick",
    )(*weights, everything, mask)


def middle_kernel(top, arrived_ref, scale_ref, out_ref):
    nx = arrived_ref.shape[0]

    def add_up(which):
        value = arrived_ref[0, which].astype(F32)
        for q in range(1, nx):
            value = value + arrived_ref[q, which].astype(F32)
        return value

    for k in range(top):
        scale = scale_ref[k : k + 1]
        gate, up, dh = add_up(k), add_up(top + k), scale * add_up(2 * top + k)
        sg = jax.nn.sigmoid(gate)
        active = gate * sg
        dgate = (dh * up * sg * (1.0 + gate * (1.0 - sg))).astype(BF16)
        dup = (dh * active).astype(BF16)
        hidden = (scale * (active * up)).astype(BF16)
        for q in range(nx):
            out_ref[q, k] = dgate
            out_ref[q, top + k] = dup
            out_ref[q, 2 * top + k] = hidden


def middle(arrived, scale):
    return pl.pallas_call(
        functools.partial(middle_kernel, scale.shape[0]),
        out_shape=jax.ShapeDtypeStruct(arrived.shape, BF16),
        compiler_params=pltpu.CompilerParams(vmem_limit_bytes=VMEM_BYTES),
        cost_estimate=pl.CostEstimate(
            flops=6 * arrived.size, bytes_accessed=4 * arrived.size, transcendentals=arrived.size
        ),
        name="middle",
    )(arrived, scale)


def output_kernel(experts, parts, *refs):
    weight_refs = refs[:parts]
    shared_ref, mask_ref, kept_ref, sent_ref, out_ref, sum_ref = refs[parts:]
    step = pl.program_id(0)
    nx, top, _, share = shared_ref.shape
    units = weight_refs[0].shape[1] // experts
    ny, nh, _, small, width = out_ref.shape
    values = [[shared_ref[q, k].astype(F32) for k in range(top)] for q in range(nx)]
    product = None
    for p in range(parts):
        pieces = []
        for e in range(experts):
            line = []
            for q in range(nx):
                piece = None
                for k in range(top):
                    value = values[q][k][p * units : (p + 1) * units]
                    term = value * mask_ref[e, k : k + 1, q * share : (q + 1) * share]
                    piece = term if piece is None else piece + term
                line.append(piece)
            pieces.append(jnp.concatenate(line, axis=1))
        wide = jnp.concatenate(pieces, axis=0).astype(BF16)
        if p < parts // 2:
            kept_ref[p, 0] = wide
        else:
            sent_ref[p - parts // 2, 0] = wide
        term = contract_first(wide, weight_refs[p][0])
        product = term if product is None else product + term

    @pl.when(step == 0)
    def _():
        out_ref[:, :, 0] = product.astype(BF16).reshape(ny, nh, small, width)

    @pl.when(step == 1)
    def _():
        sum_ref[...] = product

    @pl.when(step == 2)
    def _():
        total = (sum_ref[...] + product).astype(BF16)
        out_ref[:, :, 0] = total.reshape(ny, nh, small, width)


def output(shared, weights, experts, mask, ny, nh):
    parts = len(weights)
    mats, stored, width = weights[0].shape
    top, total = mask.shape[1:]
    nx, _, many, share = shared.shape
    small = total // (ny * nh)

    def matrix(step):
        return lax.rem(step + mats - 1, mats)

    return pl.pallas_call(
        functools.partial(output_kernel, experts, parts),
        grid=(mats,),
        in_specs=[pl.BlockSpec((1, stored, width), lambda i: (matrix(i), 0, 0))] * parts
        + [
            pl.BlockSpec((nx, top, many, share), lambda i: (0, matrix(i), 0, 0)),
            pl.BlockSpec((experts, top, total), lambda i: (0, 0, 0)),
        ],
        out_specs=[
            pl.BlockSpec((parts // 2, 1, stored, total), lambda i: (0, matrix(i), 0, 0)),
            pl.BlockSpec((parts // 2, 1, stored, total), lambda i: (0, matrix(i), 0, 0)),
            pl.BlockSpec((ny, nh, 1, small, width), lambda i: (0, 0, (i + 1) // 2, 0, 0)),
        ],
        out_shape=[
            jax.ShapeDtypeStruct((parts // 2, mats, stored, total), BF16),
            jax.ShapeDtypeStruct((parts // 2, mats, stored, total), BF16),
            jax.ShapeDtypeStruct((ny, nh, 2, small, width), BF16),
        ],
        scratch_shapes=[pltpu.VMEM((total, width), F32)],
        compiler_params=pltpu.CompilerParams(vmem_limit_bytes=2 * VMEM_BYTES),
        cost_estimate=pl.CostEstimate(
            flops=2 * mats * parts * stored * width * total,
            bytes_accessed=2 * (mats * parts * stored * (width + total) + 2 * total * width),
            transcendentals=0,
        ),
        name="output",
    )(*weights, shared, mask)


def body(tokens, slot_ids, gate_values, slot_expert, w_gate, w_up, w_down, cotangent):
    block, width = tokens.shape
    experts, units, _ = w_gate.shape
    ny, nh, nl, nx = (lax.axis_size(a) for a in ("y", "zh", "zl", "x"))
    top = slot_ids.shape[1]
    rows = block // nl
    total = ny * rows
    share = total // nx
    many = 2 * nl * units
    stored = experts * units

    def own_rows(value):
        return lax.dynamic_slice_in_dim(value, lax.axis_index("zl") * rows, rows, axis=0)

    ids, values = own_rows(slot_ids), own_rows(gate_values)
    numbers = jnp.arange(slot_expert.shape[0], dtype=jnp.int32)
    chosen = jnp.sum(
        jnp.where(ids[:, :, None] == numbers, slot_expert[None, None, :], 0), axis=-1
    ).astype(F32)
    part0 = short(values)
    part1 = short(values - part0)
    part2 = short(values - part0 - part1)
    meta = jnp.stack([chosen, part0, part1, part2]).transpose(0, 2, 1).astype(BF16)
    facts_of = 4 * top * rows
    meta = jnp.pad(meta.reshape(1, facts_of), ((0, 15), (0, width - facts_of)))
    packed = jnp.concatenate([own_rows(tokens), own_rows(cotangent), meta], axis=0)
    held = packed.shape[0]
    everything = lax.all_gather(packed, "y", axis=0, tiled=True).reshape(ny, held, width)

    own = jnp.stack([w_gate, w_up, w_down]).reshape(3, stored, width)
    near = swap(own, "zl")
    weights = [own, near, swap(own, "core"), swap(near, "core")]

    facts = everything[:, 2 * rows, :facts_of].reshape(ny, 4, top, rows).astype(F32)
    facts = facts.transpose(1, 2, 0, 3).reshape(4, top, total)
    scale = facts[1] + facts[2] + facts[3]
    mask = (facts[0][None] == jnp.arange(experts, dtype=F32)[:, None, None]).astype(F32)
    own_scale = lax.dynamic_slice_in_dim(scale, lax.axis_index("x") * share, share, axis=1)

    def exchange(value):
        return lax.all_to_all(value, "x", split_axis=0, concat_axis=0, tiled=True)

    mask, own_scale = lax.optimization_barrier((mask, own_scale))
    picked = pick(weights, experts, everything, mask, rows, nx)
    shared = exchange(middle(exchange(picked), own_scale))
    wide_kept, wide_sent, parts = output(shared, weights, experts, mask, ny, nh)
    small = rows // nh
    parts = lax.psum_scatter(
        parts.reshape(ny * 2 * rows, width), "y", scatter_dimension=0, tiled=True
    )

    rows_x = everything[:, :rows].reshape(total, width)
    rows_c = everything[:, rows : 2 * rows].reshape(total, width)

    def products(wide):
        groups = ((wide[:, :2], rows_x), (wide[:, 2:], rows_c))
        return [
            jnp.dot(left.reshape(-1, total), right, preferred_element_type=F32).reshape(
                nl, -1, stored, width
            )
            for left, right in groups
        ]

    sent = [swap(value.astype(BF16), "core").astype(F32) for value in products(wide_sent)]
    kept = products(wide_kept)
    near = [swap((a[1] + b[1]).astype(BF16), "zl") for a, b in zip(kept, sent)]
    parts, near[0], near[1] = lax.optimization_barrier((parts, near[0], near[1]))
    done = [
        (a[0] + b[0] + c.astype(F32)).astype(BF16).reshape(-1, experts, units, width)
        for a, b, c in zip(kept, sent, near)
    ]

    parts = parts.reshape(nh, 2, small, width)
    parts = lax.all_to_all(parts, "zh", split_axis=0, concat_axis=0, tiled=True)
    parts = jnp.sum(parts.astype(F32), axis=0).astype(BF16)
    ends = spread(parts, ("zh", "zl"), nh * nl)
    ends = ends.reshape(nh, nl, 2, small, width).transpose(2, 1, 0, 3, 4).reshape(2, block, width)
    return (ends[0], ends[1], done[0][0], done[0][1], done[1][0])


def solution(mesh):
    dp, ep, mp = mesh.shape["dp"], mesh.shape["expert"], mesh.shape["mp"]
    split = Mesh(
        mesh.devices.reshape(dp // 2, 2, ep // 2, 2, mp), ("y", "core", "zh", "zl", "x")
    )
    rows = ("y", "core")
    stored = P(None, ("y", "core", "zh", "zl"), "x")
    return jax.shard_map(
        body,
        mesh=split,
        in_specs=(
            P(rows, "x"),
            P(rows, None),
            P(rows, None),
            P(),
            stored,
            stored,
            stored,
            P(rows, "x"),
        ),
        out_specs=(P(rows, "x"), P(rows, "x"), stored, stored, stored),
        check_vma=False,
    )
```

time: 216 us -> 208 us (0.963)
  blocking collectives: 34.7 us -> 53.2 us
  waiting for transfers between devices: 91.3 us -> 76.8 us
  starting transfers between devices: 26.8 us -> 21.8 us
  other arithmetic: 12.4 us -> 8.99 us
  Pallas kernels: 15.3 us -> 13.1 us
    all_to_all x1 -> x2, blocking collectives: 16.6 us -> 35.9 us  [exchange(): return lax.all_to_all(value, 'x', split_axis=0, concat_axis=0, tiled=True)]
    all_to_all x1 -> x0, waiting for transfers between devices: 13.3 us -> none  [exchange(): return lax.all_to_all(value, 'x', split_axis=0, concat_axis=0, tiled=True)]
    all_gather x1, waiting for transfers between devices: 4.77 us -> 11.2 us  [body(): lax.all_gather(packed, 'y', axis=0, tiled=True).reshape(ny, held, width)]
    reduce_scatter x1, waiting for transfers between devices: 5.08 us -> 0.01 us  [body(): lax.psum_scatter(parts.reshape(ny * 2 * rows, width), 'y', scatter_dimens...]
    all_to_all x1 -> x0, starting transfers between devices: 4.8 us -> none  [exchange(): return lax.all_to_all(value, 'x', split_axis=0, concat_axis=0, tiled=True)]
    concatenate x1 -> x0, other arithmetic: 3.38 us -> none  [body(): jnp.concatenate([own, near, swap(own, 'core'), swap(near, 'core')], axis=1)]
    ppermute x7, waiting for transfers between devices: 57.6 us -> 54.5 us  [swap(): return lax.ppermute(value, axis, [(0, 1), (1, 0)])]
    unnamed x30 -> x36, local copies, waits for them, and re-layouts: 8.3 us -> 8.88 us
  transfers between devices with their start and end apart: 11 -> 10, of which waited for: 7 -> 4; matrix products, arithmetic and copies ran while one was open for 7% -> 6% of each run, Pallas kernels for 0% -> 0%
where the time goes in v4:
time: 208 us; the launch traced here: 206 us
  waiting for transfers between devices  76.8 us (37%)
  blocking collectives  53.2 us (26%)
  starting transfers between devices  21.8 us (10%)
  between operations  14.4 us (7%)
  local copies, waits for them, and re-layouts  14.3 us (7%)
  Pallas kernels  13.1 us (6%)
  other arithmetic  8.99 us (4%)
  matrix products  3.55 us (2%)
    ppermute x7, waiting for transfers between devices, swap(): return lax.ppermute(value, axis, [(0, 1), (1, 0)])  54.5 us
    all_to_all x2, blocking collectives, exchange(): return lax.all_to_all(value, 'x', split_axis=0, concat_axis=0, tiled=True)  35.9 us
    ppermute x7, starting transfers between devices, swap(): return lax.ppermute(value, axis, [(0, 1), (1, 0)])  18.3 us
    all_to_all x1, blocking collectives, body(): parts = lax.all_to_all(parts, 'zh', split_axis=0, concat_axis=0, tiled=True)  17.4 us
    all_gather x1, waiting for transfers between devices, body(): lax.all_gather(packed, 'y', axis=0, tiled=True).reshape(ny, held, width)  11.2 us
    all_to_all x1, waiting for transfers between devices, spread(): return lax.all_to_all(copies, axis, split_axis=0, concat_axis=0, tiled=True)  11.1 us
    unnamed x36, local copies, waits for them, and re-layouts  8.88 us
    pallas_call x1, Pallas kernels, output(): pl.pallas_call(functools.partial(output_kernel, experts, parts), grid=(ma...  7.2 us
  transfers between devices with their start and end apart: 10, of which 4 were waited for; matrix products, arithmetic and copies ran while one was open for 6% of the time, Pallas kernels for 0%

profile of v4, /device:TPU:6, one launch (start us, length us, event | category | flops | bytes accessed | tf_op | source)
XLA Modules:
  0.0 206.3 jit_solution(4002706128576290121)
XLA Ops:
  7.2 0.0 copy-start
  7.2 0.0 all-gather.2.cloned.1.call-start
  7.2 0.8 fusion.21
  8.0 0.1 constant_dynamic-slice_fusion.2
  8.1 0.7 select_reduce_fusion
  8.8 0.1 reshape.104
  8.9 1.0 constant_dynamic-slice_fusion.3
  9.9 0.7 fusion.16
  10.6 0.0 all-gather.2.cloned.1.call-update
  10.7 0.0 reduce-scatter.2.cloned.1.call-start
  10.7 1.4 pad_maximum_fusion.refs_0_
  12.2 4.3 %collective-permute-start = (bf16[3,224,1024]{2,1,0:T(8,128)(2,1)S(1)}, bf16[3,224,1024]{2,1,0:T(8,128)(2,1)S(1)}, u32[]{:S(2)}, u32[]{:S(2)}) collective-permute-start(bf16[3,224,1024]{2,1,0:T(8,128)(2,1)S(1)} %pad_maximum_fusion.refs_0_), channel_id=1, source_target_pairs={{0,4},{4,0},{1,5},{5,1},{2,6},{6,2},{3,7},{7,3},{8,12},{12,8},{9,1... | collective-permute-start | bytes 4128776 | tf_op jit(solution)/shard_map/ppermute | solution.py:19
  16.5 1.9 collective-permute-start.1
  18.4 28.2 %collective-permute-done.refs_1_ = bf16[3,224,1024]{2,1,0:T(8,128)(2,1)S(1)} collective-permute-done((bf16[3,224,1024]{2,1,0:T(8,128)(2,1)S(1)}, bf16[3,224,1024]{2,1,0:T(8,128)(2,1)S(1)}, u32[]{:S(2)}, u32[]{:S(2)}) %collective-permute-start) | collective-permute-done | bytes 1376288 | tf_op jit(solution)/shard_map/ppermute | solution.py:19
  46.6 1.9 collective-permute-start.2
  48.6 11.2 %all-gather.2.cloned.1.call-done = bf16[1152,1024]{1,0:T(8,128)(2,1)} async-done(((bf16[144,1024]{1,0:T(8,128)(2,1)}), bf16[1152,1024]{1,0:T(8,128)(2,1)}) %all-gather.2.cloned.1.call-update) | async-done | bytes 2359312 | tf_op jit(solution)/shard_map/all_gather | solution.py:227
  59.7 0.9 fusion.17
  60.6 0.1 reshape.113
  60.8 0.1 eq.31
  60.8 0.1 add.48
  60.9 0.0 collective-permute-done.1.refs_2_
  60.9 0.0 collective-permute-done.2.refs_3_
  61.0 1.7 copy-done.1
  62.6 5.7 %pick.1 = bf16[4,6,224,128]{3,2,1,0:T(8,128)(2,1)S(1)} custom-call(bf16[3,224,1024]{2,1,0:T(8,128)(2,1)S(1)} %pad_maximum_fusion.refs_0_, bf16[3,224,1024]{2,1,0:T(8,128)(2,1)S(1)} %collective-permute-done.refs_1_, bf16[3,224,1024]{2,1,0:T(8,128)(2,1)} %collective-permute-done.1.refs_2_, bf16[3,224,1024]{2,1,0:T(8,128)(2,1)} %collective-permute-done.2.refs_3_, ...), custom_call_target="tpu_custom_call" | custom-call | flops 2818572288 | bytes 8978432 | tf_op jit(solution)/shard_map/pick/pallas_call | solution.py:62
  68.3 17.9 %all_to_all.20.arrived_ref = bf16[4,6,224,128]{3,2,1,0:T(8,128)(2,1)S(1)} all-to-all(bf16[4,6,224,128]{3,2,1,0:T(8,128)(2,1)S(1)} %pick.1), channel_id=1, replica_groups=mesh['y'=8,'core'=2,'zh'=4,'zl'=2,'x'=4] {'x'}, dimensions={0} | all-to-all | bytes 2752512 | tf_op jit(solution)/shard_map/all_to_all | solution.py:240
  86.2 0.3 middle.1
  86.5 17.9 %all_to_all.21.refs_4_ = bf16[4,6,224,128]{3,2,1,0:T(8,128)(2,1)} all-to-all(bf16[4,6,224,128]{3,2,1,0:T(8,128)(2,1)S(1)} %middle.1), channel_id=1, replica_groups=mesh['y'=8,'core'=2,'zh'=4,'zl'=2,'x'=4] {'x'}, dimensions={0} | all-to-all | bytes 2752512 | tf_op jit(solution)/shard_map/all_to_all | solution.py:240
  104.5 7.2 %output.1 = (bf16[2,3,224,512]{3,2,1,0:T(8,128)(2,1)S(1)}, bf16[2,3,224,512]{3,2,1,0:T(8,128)(2,1)S(1)}, bf16[8,4,2,16,1024]{4,3,2,1,0:T(8,128)(2,1)}) custom-call(bf16[3,224,1024]{2,1,0:T(8,128)(2,1)S(1)} %copy-done.4, bf16[3,224,1024]{2,1,0:T(8,128)(2,1)S(1)} %copy-done.8, bf16[3,224,1024]{2,1,0:T(8,128)(2,1)} %collective-permute-done.1.refs_2_, ...), custom_call_target="tpu_custom_call" | custom-call | flops 2818572288 | bytes 10354688 | tf_op jit(solution)/shard_map/output/pallas_call | solution.py:171
  111.7 1.1 copy-done.5
  112.8 1.2 copy-done.9
  114.0 0.0 reduce-scatter.2.cloned.1.call-update
  114.0 0.2 fusion.25
  114.3 1.1 copy-done.10
  115.4 1.1 convolution_convert_fusion
  116.5 1.9 collective-permute-start.3
  118.4 0.1 slice.86
  118.5 0.7 fusion.5
  119.2 2.4 %collective-permute-start.5 = (bf16[2,1,224,1024]{3,2,1,0:T(8,128)(2,1)S(1)}, bf16[2,1,224,1024]{3,2,1,0:T(8,128)(2,1)S(1)}, u32[]{:S(2)}, u32[]{:S(2)}) collective-permute-start(bf16[2,1,224,1024]{3,2,1,0:T(8,128)(2,1)S(1)} %fusion.5), channel_id=1, source_target_pairs={{0,32},{32,0},{1,33},{33,1},{2,34},{34,2},{3,35},{35,3},{4,36},{36... | collective-permute-start | bytes 2752520 | tf_op jit(solution)/shard_map/ppermute | solution.py:19
  121.6 1.1 fusion.28
  122.7 0.4 fusion.24
  123.1 0.0 collective-permute-done.3
  123.1 0.4 convert_element_type.70
  123.5 0.4 fusion.4
  124.0 1.3 copy-done.11
  125.3 3.5 %collective-permute-start.4 = (bf16[2,224,1024]{2,1,0:T(8,128)(2,1)S(1)}, bf16[2,224,1024]{2,1,0:T(8,128)(2,1)S(1)}, u32[]{:S(2)}, u32[]{:S(2)}) collective-permute-start(bf16[2,224,1024]{2,1,0:T(8,128)(2,1)S(1)} %fusion.4), channel_id=1, source_target_pairs={{0,4},{4,0},{1,5},{5,1},{2,6},{6,2},{3,7},{7,3},{8,12},{12,8},{9,1... | collective-permute-start | bytes 2752520 | tf_op jit(solution)/shard_map/ppermute | solution.py:19
  128.9 0.6 fusion.29
  129.5 0.0 collective-permute-done.5
  129.5 0.2 convert_element_type.74
  129.8 0.1 fusion.13
  129.9 0.9 copy-done.12
  130.7 2.3 %collective-permute-start.6 = (bf16[1,224,1024]{2,1,0:T(8,128)(2,1)S(1)}, bf16[1,224,1024]{2,1,0:T(8,128)(2,1)S(1)}, u32[]{:S(2)}, u32[]{:S(2)}) collective-permute-start(bf16[1,224,1024]{2,1,0:T(8,128)(2,1)S(1)} %fusion.13), channel_id=1, source_target_pairs={{0,4},{4,0},{1,5},{5,1},{2,6},{6,2},{3,7},{7,3},{8,12},{12,8},{9,1... | collective-permute-start | bytes 1376264 | tf_op jit(solution)/shard_map/ppermute | solution.py:19
  133.0 26.3 %collective-permute-done.6 = bf16[1,224,1024]{2,1,0:T(8,128)(2,1)S(1)} collective-permute-done((bf16[1,224,1024]{2,1,0:T(8,128)(2,1)S(1)}, bf16[1,224,1024]{2,1,0:T(8,128)(2,1)S(1)}, u32[]{:S(2)}, u32[]{:S(2)}) %collective-permute-start.6) | collective-permute-done | bytes 458784 | tf_op jit(solution)/shard_map/ppermute | solution.py:19
  159.3 0.8 copy-done.16
  160.1 17.4 %all_to_all.22 = bf16[4,2,16,1024]{3,2,1,0:T(8,128)(2,1)S(1)} all-to-all(bf16[4,2,16,1024]{3,2,1,0:T(8,128)(2,1)} %bitcast.114), channel_id=1, replica_groups=mesh['y'=8,'core'=2,'zh'=4,'zl'=2,'x'=4] {'zh'}, dimensions={0} | all-to-all | bytes 524288 | tf_op jit(solution)/shard_map/all_to_all | solution.py:273
  177.5 0.8 broadcast_in_dim.24
  178.3 3.5 %all-to-all-start.3 = ((bf16[8,2,16,1024]{3,2,1,0:T(8,128)(2,1)}), bf16[8,2,16,1024]{3,2,1,0:T(8,128)(2,1)S(1)}, u32[]{:S(2)}, u32[]{:S(2)}) async-start(bf16[8,2,16,1024]{3,2,1,0:T(8,128)(2,1)} %broadcast_in_dim.24), calls=%async_computation.4 | async-start | bytes 1048576 | tf_op jit(solution)/shard_map/all_to_all | solution.py:33
  181.8 0.0 copy-start.17
  181.8 2.2 %fusion.2 = bf16[2,224,1024]{2,1,0:T(8,128)(2,1)S(1)} fusion(f32[2,224,1024]{2,1,0:T(8,128)S(1)} %bitcast.99, f32[2,2,224,1024]{3,2,1,0:T(8,128)} %copy-done.11, bf16[2,224,1024]{2,1,0:T(8,128)(2,1)S(1)} %collective-permute-done.4), kind=kLoop, calls=%fused_computation.3 | loop fusion | flops 1835008 | bytes 5505024 | tf_op jit(solution)/shard_map/convert_element_type | solution.py:268
  184.0 1.0 fusion.26
  185.0 0.8 copy-done.13
  185.9 1.0 fusion.9
  186.9 11.1 %all-to-all-done.3 = bf16[8,2,16,1024]{3,2,1,0:T(8,128)(2,1)S(1)} async-done(((bf16[8,2,16,1024]{3,2,1,0:T(8,128)(2,1)}), bf16[8,2,16,1024]{3,2,1,0:T(8,128)(2,1)S(1)}, u32[]{:S(2)}, u32[]{:S(2)}) %all-to-all-start.3) | async-done | bytes 524320 | tf_op jit(solution)/shard_map/all_to_all | solution.py:33
  198.0 0.7 copy.22
  198.7 0.7 copy.23
  (37 shorter events, 0.2 us)
Async XLA Ops:
  7.2 0.8 copy-start
  7.2 52.6 %all-gather.2.cloned.1.call-start = ((), (), s32[]{:S(2)}) async-start(), calls=%async_computation.5 | async-start | bytes 2654208 | tf_op jit(solution)/shard_map/all_gather | solution.py:227
  10.7 148.6 %reduce-scatter.2.cloned.1.call-start = ((), (), s32[]{:S(2)}) async-start(), calls=%async_computation.6 | async-start | bytes 2359296 | tf_op jit(solution)/shard_map/reduce_scatter | solution.py:247
  12.2 56.1 %copy-start.3 = (bf16[3,224,1024]{2,1,0:T(8,128)(2,1)}, bf16[3,224,1024]{2,1,0:T(8,128)(2,1)S(1)}, u32[]{:S(2)}) copy-start(bf16[3,224,1024]{2,1,0:T(8,128)(2,1)S(1)} %pad_maximum_fusion.refs_0_) | copy-start | bytes 4128772
  12.2 34.5 %collective-permute-start = (bf16[3,224,1024]{2,1,0:T(8,128)(2,1)S(1)}, bf16[3,224,1024]{2,1,0:T(8,128)(2,1)S(1)}, u32[]{:S(2)}, u32[]{:S(2)}) collective-permute-start(bf16[3,224,1024]{2,1,0:T(8,128)(2,1)S(1)} %pad_maximum_fusion.refs_0_), channel_id=1, source_target_pairs={{0,4},{4,0},{1,5},{5,1},{2,6},{6,2},{3,7},{7,3},{8,12},{12,8},{9,1... | collective-permute-start | bytes 4128776 | tf_op jit(solution)/shard_map/ppermute | solution.py:19
  16.5 44.5 %collective-permute-start.1 = (bf16[3,224,1024]{2,1,0:T(8,128)(2,1)S(1)}, bf16[3,224,1024]{2,1,0:T(8,128)(2,1)}, u32[]{:S(2)}, u32[]{:S(2)}) collective-permute-start(bf16[3,224,1024]{2,1,0:T(8,128)(2,1)S(1)} %pad_maximum_fusion.refs_0_), channel_id=1, source_target_pairs={{0,32},{32,0},{1,33},{33,1},{2,34},{34,2},{3,35},{35,3},{4,36},{36... | collective-permute-start | bytes 4128776 | tf_op jit(solution)/shard_map/ppermute | solution.py:19
  46.6 21.7 %copy-start.7 = (bf16[3,224,1024]{2,1,0:T(8,128)(2,1)}, bf16[3,224,1024]{2,1,0:T(8,128)(2,1)S(1)}, u32[]{:S(2)}) copy-start(bf16[3,224,1024]{2,1,0:T(8,128)(2,1)S(1)} %collective-permute-done.refs_1_) | copy-start | bytes 4128772
  46.6 14.3 %collective-permute-start.2 = (bf16[3,224,1024]{2,1,0:T(8,128)(2,1)S(1)}, bf16[3,224,1024]{2,1,0:T(8,128)(2,1)}, u32[]{:S(2)}, u32[]{:S(2)}) collective-permute-start(bf16[3,224,1024]{2,1,0:T(8,128)(2,1)S(1)} %collective-permute-done.refs_1_), channel_id=1, source_target_pairs={{0,32},{32,0},{1,33},{33,1},{2,34},{34,2},{3,35},{35,3},{4,36},{36... | collective-permute-start | bytes 4128776 | tf_op jit(solution)/shard_map/ppermute | solution.py:19
  60.9 1.7 copy-start.1
  86.5 18.0 %copy-start.4 = (bf16[3,224,1024]{2,1,0:T(8,128)(2,1)S(1)}, bf16[3,224,1024]{2,1,0:T(8,128)(2,1)}, u32[]{:S(2)}) copy-start(bf16[3,224,1024]{2,1,0:T(8,128)(2,1)} %copy-done.3) | copy-start | bytes 4128772
  86.5 18.0 %copy-start.8 = (bf16[3,224,1024]{2,1,0:T(8,128)(2,1)S(1)}, bf16[3,224,1024]{2,1,0:T(8,128)(2,1)}, u32[]{:S(2)}) copy-start(bf16[3,224,1024]{2,1,0:T(8,128)(2,1)} %copy-done.7) | copy-start | bytes 4128772
  104.5 9.5 %copy-start.2 = (bf16[1152,1024]{1,0:T(8,128)(2,1)S(1)}, bf16[1152,1024]{1,0:T(8,128)(2,1)}, u32[]{:S(2)}) copy-start(bf16[1152,1024]{1,0:T(8,128)(2,1)} %all-gather.2.cloned.1.call-done) | copy-start | bytes 7077892
  111.7 1.1 copy-start.5
  112.8 1.2 copy-start.9
  114.0 1.3 copy-start.10
  115.3 3.1 %copy-start.6 = (bf16[2,3,224,512]{3,2,1,0:T(8,128)(2,1)S(1)}, bf16[2,3,224,512]{3,2,1,0:T(8,128)(2,1)}, u32[]{:S(2)}) copy-start(bf16[2,3,224,512]{3,2,1,0:T(8,128)(2,1)} %copy-done.5) | copy-start | bytes 4128772
  116.5 6.6 %collective-permute-start.3 = (bf16[2,2,224,1024]{3,2,1,0:T(8,128)(2,1)S(1)}, bf16[2,2,224,1024]{3,2,1,0:T(8,128)(2,1)S(1)}, u32[]{:S(2)}, u32[]{:S(2)}) collective-permute-start(bf16[2,2,224,1024]{3,2,1,0:T(8,128)(2,1)S(1)} %convolution_convert_fusion), channel_id=1, source_target_pairs={{0,32},{32,0},{1,33},{33,1},{2,34},{34,2},{3,35},{35,3},{4,36},{36... | collective-permute-start | bytes 5505032 | tf_op jit(solution)/shard_map/ppermute | solution.py:19
  119.2 10.3 %collective-permute-start.5 = (bf16[2,1,224,1024]{3,2,1,0:T(8,128)(2,1)S(1)}, bf16[2,1,224,1024]{3,2,1,0:T(8,128)(2,1)S(1)}, u32[]{:S(2)}, u32[]{:S(2)}) collective-permute-start(bf16[2,1,224,1024]{3,2,1,0:T(8,128)(2,1)S(1)} %fusion.5), channel_id=1, source_target_pairs={{0,32},{32,0},{1,33},{33,1},{2,34},{34,2},{3,35},{35,3},{4,36},{36... | collective-permute-start | bytes 2752520 | tf_op jit(solution)/shard_map/ppermute | solution.py:19
  123.5 1.8 copy-start.11
  125.3 34.0 %collective-permute-start.4 = (bf16[2,224,1024]{2,1,0:T(8,128)(2,1)S(1)}, bf16[2,224,1024]{2,1,0:T(8,128)(2,1)S(1)}, u32[]{:S(2)}, u32[]{:S(2)}) collective-permute-start(bf16[2,224,1024]{2,1,0:T(8,128)(2,1)S(1)} %fusion.4), channel_id=1, source_target_pairs={{0,4},{4,0},{1,5},{5,1},{2,6},{6,2},{3,7},{7,3},{8,12},{12,8},{9,1... | collective-permute-start | bytes 2752520 | tf_op jit(solution)/shard_map/ppermute | solution.py:19
  129.5 1.2 copy-start.12
  129.7 3.3 %copy-start.14 = (f32[2,1,224,1024]{3,2,1,0:T(8,128)}, f32[2,1,224,1024]{3,2,1,0:T(8,128)S(1)}, u32[]{:S(2)}) copy-start(f32[2,1,224,1024]{3,2,1,0:T(8,128)S(1)} %convert_element_type.74) | copy-start | bytes 5505028
  130.7 28.6 %collective-permute-start.6 = (bf16[1,224,1024]{2,1,0:T(8,128)(2,1)S(1)}, bf16[1,224,1024]{2,1,0:T(8,128)(2,1)S(1)}, u32[]{:S(2)}, u32[]{:S(2)}) collective-permute-start(bf16[1,224,1024]{2,1,0:T(8,128)(2,1)S(1)} %fusion.13), channel_id=1, source_target_pairs={{0,4},{4,0},{1,5},{5,1},{2,6},{6,2},{3,7},{7,3},{8,12},{12,8},{9,1... | collective-permute-start | bytes 1376264 | tf_op jit(solution)/shard_map/ppermute | solution.py:19
  159.3 0.8 copy-start.16
  178.3 19.6 %all-to-all-start.3 = ((bf16[8,2,16,1024]{3,2,1,0:T(8,128)(2,1)}), bf16[8,2,16,1024]{3,2,1,0:T(8,128)(2,1)S(1)}, u32[]{:S(2)}, u32[]{:S(2)}) async-start(bf16[8,2,16,1024]{3,2,1,0:T(8,128)(2,1)} %broadcast_in_dim.24), calls=%async_computation.4 | async-start | bytes 1048576 | tf_op jit(solution)/shard_map/all_to_all | solution.py:33
  181.8 3.2 %copy-start.15 = (f32[2,1,224,1024]{3,2,1,0:T(8,128)S(1)}, f32[2,1,224,1024]{3,2,1,0:T(8,128)}, u32[]{:S(2)}) copy-start(f32[2,1,224,1024]{3,2,1,0:T(8,128)} %copy-done.14) | copy-start | bytes 5505028
  181.8 3.2 %copy-start.17 = (bf16[1,224,1024]{2,1,0:T(8,128)(2,1)S(1)}, bf16[1,224,1024]{2,1,0:T(8,128)(2,1)}, u32[]{:S(2)}) copy-start(bf16[1,224,1024]{2,1,0:T(8,128)(2,1)} %copy-done.16) | copy-start | bytes 1376260
  184.0 1.8 copy-start.13
Sparse Core Ops, SparseCore 0:
  10.8 48.9 all-gather.1
  114.1 43.6 reduce-scatter.1

commit v5 on v4

--- a/solution.py
+++ b/solution.py
@@ -33,9 +33,38 @@
     return lax.all_to_all(copies, axis, split_axis=0, concat_axis=0, tiled=True)
 
 
-def pick_kernel(experts, *refs):
-    *weight_refs, rows_ref, mask_ref, out_ref = refs
-    rows = rows_ref[...].reshape(-1, rows_ref.shape[2])
+def whole(memory_space):
+    return pl.BlockSpec(memory_space=memory_space)
+
+
+def rows_of(every_ref, rows_ref, sems, mats):
+    matrix = pl.program_id(0)
+    rows = rows_ref.shape[2]
+    loads = [
+        pltpu.make_async_copy(every_ref.at[:, pl.ds(i * rows, rows)], rows_ref.at[i], sems.at[i])
+        for i in range(2)
+    ]
+
+    @pl.when(matrix == 0)
+    def _():
+        loads[0].start()
+        loads[1].start()
+        loads[0].wait()
+
+    @pl.when(matrix == mats - 1)
+    def _():
+        loads[1].wait()
+
+    return rows_ref[matrix // (mats - 1)].reshape(-1, rows_ref.shape[3])
+
+
+def rows_scratch(ny, rows, width):
+    return [pltpu.VMEM((2, ny, rows, width), BF16), pltpu.SemaphoreType.DMA((2,))]
+
+
+def pick_kernel(experts, mats, *refs):
+    *weight_refs, every_ref, mask_ref, out_ref, rows_ref, sems = refs
+    rows = rows_of(every_ref, rows_ref, sems, mats)
     units = weight_refs[0].shape[1] // experts
     nx, top, _, share = out_ref.shape
     picked = [[] for _ in range(top)]
@@ -60,15 +89,13 @@
     ny = everything.shape[0]
     many = parts * stored // experts
     return pl.pallas_call(
-        functools.partial(pick_kernel, experts),
+        functools.partial(pick_kernel, experts, mats),
         grid=(mats,),
         in_specs=[pl.BlockSpec((1, stored, width), lambda m: (m, 0, 0))] * parts
-        + [
-            pl.BlockSpec((ny, rows, width), lambda m: (0, m // (mats - 1), 0)),
-            pl.BlockSpec((experts, top, total), lambda m: (0, 0, 0)),
-        ],
+        + [whole(pltpu.HBM), pl.BlockSpec((experts, top, total), lambda m: (0, 0, 0))],
         out_specs=pl.BlockSpec((nx, top, many, total // nx), lambda m: (0, m, 0, 0)),
         out_shape=jax.ShapeDtypeStruct((nx, mats * top, many, total // nx), BF16),
+        scratch_shapes=rows_scratch(ny, rows, width),
         compiler_params=pltpu.CompilerParams(vmem_limit_bytes=VMEM_BYTES),
         cost_estimate=pl.CostEstimate(
             flops=2 * mats * parts * stored * width * total,
@@ -115,32 +142,31 @@
     )(arrived, scale)
 
 
+def widen(shared_ref, mask_ref, experts, units, part):
+    nx, top, _, share = shared_ref.shape
+    pieces = []
+    for e in range(experts):
+        line = []
+        for q in range(nx):
+            piece = None
+            for k in range(top):
+                value = shared_ref[q, k].astype(F32)[part * units : (part + 1) * units]
+                term = value * mask_ref[e, k : k + 1, q * share : (q + 1) * share]
+                piece = term if piece is None else piece + term
+            line.append(piece)
+        pieces.append(jnp.concatenate(line, axis=1))
+    return jnp.concatenate(pieces, axis=0).astype(BF16)
+
+
 def output_kernel(experts, parts, *refs):
     weight_refs = refs[:parts]
-    shared_ref, mask_ref, kept_ref, sent_ref, out_ref, sum_ref = refs[parts:]
+    shared_ref, mask_ref, out_ref, sum_ref = refs[parts:]
     step = pl.program_id(0)
-    nx, top, _, share = shared_ref.shape
     units = weight_refs[0].shape[1] // experts
     ny, nh, _, small, width = out_ref.shape
-    values = [[shared_ref[q, k].astype(F32) for k in range(top)] for q in range(nx)]
     product = None
     for p in range(parts):
-        pieces = []
-        for e in range(experts):
-            line = []
-            for q in range(nx):
-                piece = None
-                for k in range(top):
-                    value = values[q][k][p * units : (p + 1) * units]
-                    term = value * mask_ref[e, k : k + 1, q * share : (q + 1) * share]
-                    piece = term if piece is None else piece + term
-                line.append(piece)
-            pieces.append(jnp.concatenate(line, axis=1))
-        wide = jnp.concatenate(pieces, axis=0).astype(BF16)
-        if p < parts // 2:
-            kept_ref[p, 0] = wide
-        else:
-            sent_ref[p - parts // 2, 0] = wide
+        wide = widen(shared_ref, mask_ref, experts, units, p)
         term = contract_first(wide, weight_refs[p][0])
         product = term if product is None else product + term
 
@@ -176,25 +202,59 @@
             pl.BlockSpec((nx, top, many, share), lambda i: (0, matrix(i), 0, 0)),
             pl.BlockSpec((experts, top, total), lambda i: (0, 0, 0)),
         ],
-        out_specs=[
-            pl.BlockSpec((parts // 2, 1, stored, total), lambda i: (0, matrix(i), 0, 0)),
-            pl.BlockSpec((parts // 2, 1, stored, total), lambda i: (0, matrix(i), 0, 0)),
-            pl.BlockSpec((ny, nh, 1, small, width), lambda i: (0, 0, (i + 1) // 2, 0, 0)),
-        ],
-        out_shape=[
-            jax.ShapeDtypeStruct((parts // 2, mats, stored, total), BF16),
-            jax.ShapeDtypeStruct((parts // 2, mats, stored, total), BF16),
-            jax.ShapeDtypeStruct((ny, nh, 2, small, width), BF16),
-        ],
+        out_specs=pl.BlockSpec((ny, nh, 1, small, width), lambda i: (0, 0, (i + 1) // 2, 0, 0)),
+        out_shape=jax.ShapeDtypeStruct((ny, nh, 2, small, width), BF16),
         scratch_shapes=[pltpu.VMEM((total, width), F32)],
-        compiler_params=pltpu.CompilerParams(vmem_limit_bytes=2 * VMEM_BYTES),
+        compiler_params=pltpu.CompilerParams(vmem_limit_bytes=VMEM_BYTES),
         cost_estimate=pl.CostEstimate(
             flops=2 * mats * parts * stored * width * total,
-            bytes_accessed=2 * (mats * parts * stored * (width + total) + 2 * total * width),
+            bytes_accessed=2 * (mats * parts * stored * width + shared.size + 2 * total * width),
             transcendentals=0,
         ),
         name="output",
     )(*weights, shared, mask)
+
+
+def gradient_kernel(experts, part, start, shared_ref, mask_ref, every_ref, out_ref, rows_ref, sems):
+    rows = rows_ref.shape[1]
+    load = pltpu.make_async_copy(every_ref.at[:, pl.ds(start, rows)], rows_ref, sems.at[0])
+
+    @pl.when(pl.program_id(0) == 0)
+    def _():
+        load.start()
+        load.wait()
+
+    values = rows_ref[...].reshape(-1, rows_ref.shape[2])
+    units = out_ref.shape[2] // experts
+    for p in range(out_ref.shape[0]):
+        wide = widen(shared_ref, mask_ref, experts, units, part + p)
+        out_ref[p, 0] = jnp.dot(wide, values, preferred_element_type=F32).astype(BF16)
+
+
+def gradient(shared, mask, everything, first, mats, part, parts, start, units, rows):
+    experts, top, total = mask.shape
+    nx, _, many, share = shared.shape
+    ny, _, width = everything.shape
+    stored = experts * units
+    return pl.pallas_call(
+        functools.partial(gradient_kernel, experts, part, start),
+        grid=(mats,),
+        in_specs=[
+            pl.BlockSpec((nx, top, many, share), lambda m: (0, first + m, 0, 0)),
+            pl.BlockSpec((experts, top, total), lambda m: (0, 0, 0)),
+            whole(pltpu.HBM),
+        ],
+        out_specs=pl.BlockSpec((parts, 1, stored, width), lambda m: (0, m, 0, 0)),
+        out_shape=jax.ShapeDtypeStruct((parts, mats, stored, width), BF16),
+        scratch_shapes=[pltpu.VMEM((ny, rows, width), BF16), pltpu.SemaphoreType.DMA((1,))],
+        compiler_params=pltpu.CompilerParams(vmem_limit_bytes=VMEM_BYTES),
+        cost_estimate=pl.CostEstimate(
+            flops=2 * mats * parts * stored * width * total,
+            bytes_accessed=2 * (mats * parts * stored * width + shared.size + total * width),
+            transcendentals=0,
+        ),
+        name="gradient",
+    )(shared, mask, everything)
 
 
 def body(tokens, slot_ids, gate_values, slot_expert, w_gate, w_up, w_down, cotangent):
@@ -242,39 +302,46 @@
     mask, own_scale = lax.optimization_barrier((mask, own_scale))
     picked = pick(weights, experts, everything, mask, rows, nx)
     shared = exchange(middle(exchange(picked), own_scale))
-    wide_kept, wide_sent, parts = output(shared, weights, experts, mask, ny, nh)
+    parts = output(shared, weights, experts, mask, ny, nh)
     small = rows // nh
-    parts = lax.psum_scatter(
+    parts, shared = lax.optimization_barrier((parts, shared))
+    scattered = lax.psum_scatter(
         parts.reshape(ny * 2 * rows, width), "y", scatter_dimension=0, tiled=True
     )
 
-    rows_x = everything[:, :rows].reshape(total, width)
-    rows_c = everything[:, rows : 2 * rows].reshape(total, width)
-
-    def products(wide):
-        groups = ((wide[:, :2], rows_x), (wide[:, 2:], rows_c))
-        return [
-            jnp.dot(left.reshape(-1, total), right, preferred_element_type=F32).reshape(
-                nl, -1, stored, width
-            )
-            for left, right in groups
-        ]
-
-    sent = [swap(value.astype(BF16), "core").astype(F32) for value in products(wide_sent)]
-    kept = products(wide_kept)
-    near = [swap((a[1] + b[1]).astype(BF16), "zl") for a, b in zip(kept, sent)]
-    parts, near[0], near[1] = lax.optimization_barrier((parts, near[0], near[1]))
-    done = [
-        (a[0] + b[0] + c.astype(F32)).astype(BF16).reshape(-1, experts, units, width)
-        for a, b, c in zip(kept, sent, near)
-    ]
-
-    parts = parts.reshape(nh, 2, small, width)
+    def product(first, mats, part):
+        start = rows if first == 2 else 0
+        return gradient(shared, mask, everything, first, mats, part, nl, start, units, rows)
+
+    def near_of(kept, sent):
+        return swap((kept[1].astype(F32) + sent[1].astype(F32)).astype(BF16), "zl")
+
+    sent_down = product(2, 1, nl)
+    sent_down, shared = lax.optimization_barrier((sent_down, shared))
+    sent_down = swap(sent_down, "core")
+    sent = product(0, 2, nl)
+    sent, shared = lax.optimization_barrier((sent, shared))
+    sent = swap(sent, "core")
+    kept_down = product(2, 1, 0)
+    near_down = near_of(kept_down, sent_down)
+    kept = product(0, 2, 0)
+    near = near_of(kept, sent)
+
+    parts = scattered.reshape(nh, 2, small, width)
     parts = lax.all_to_all(parts, "zh", split_axis=0, concat_axis=0, tiled=True)
     parts = jnp.sum(parts.astype(F32), axis=0).astype(BF16)
+    parts, near_down, near = lax.optimization_barrier((parts, near_down, near))
     ends = spread(parts, ("zh", "zl"), nh * nl)
     ends = ends.reshape(nh, nl, 2, small, width).transpose(2, 1, 0, 3, 4).reshape(2, block, width)
-    return (ends[0], ends[1], done[0][0], done[0][1], done[1][0])
+
+    def finish(kept, sent, near):
+        done = sum(value.astype(F32) for value in (kept[0], sent[0], near)).astype(BF16)
+        return done.reshape(-1, experts, units, width)
+
+    (grad_down,) = finish(kept_down, sent_down, near_down)
+    grad_gate, grad_up = finish(kept, sent, near)
+
+    return (ends[0], ends[1], grad_gate, grad_up, grad_down)
 
 
 def solution(mesh):

time: 208 us -> 200 us (0.962)
  waiting for transfers between devices: 76.8 us -> 71.8 us
  Pallas kernels: 13.1 us -> 17.1 us
  local copies, waits for them, and re-layouts: 14.3 us -> 10.4 us
  matrix products: 3.55 us -> 0 us
  other arithmetic: 8.99 us -> 11.2 us
    ppermute x7, waiting for transfers between devices: 54.5 us -> 28.3 us  [swap(): return lax.ppermute(value, axis, [(0, 1), (1, 0)])]
    reduce_scatter x1, waiting for transfers between devices: 0.01 us -> 24.6 us  [body(): lax.psum_scatter(parts.reshape(ny * 2 * rows, width), 'y', scatter_dimens...]
    pallas_call x1 -> x5, Pallas kernels: 5.65 us -> 10.4 us  [the longest x1 5.68 us: pick(): pl.pallas_call(functools.partial(pick_kernel, experts, mats), grid=(mats,...]
    dot_general x4 -> x0, matrix products: 3.55 us -> none  [products(): jnp.dot(left.reshape(-1, total), right, preferred_element_type=F32)]
    all_to_all x1, waiting for transfers between devices: 11.1 us -> 7.68 us  [spread(): return lax.all_to_all(copies, axis, split_axis=0, concat_axis=0, tiled=True)]
    unnamed x36 -> x30, local copies, waits for them, and re-layouts: 8.88 us -> 5.71 us
    convert_element_type x6 -> x4, other arithmetic: 4.35 us -> 6.53 us  [the longest x2 4 us: finish(): sum((value.astype(F32) for value in (kept[0], sent[0], near))).astype(BF16)]
  transfers between devices with their start and end apart: 10 -> 10, of which waited for: 4 -> 4; matrix products, arithmetic and copies ran while one was open for 6% -> 5% of each run, Pallas kernels for 0% -> 2%
where the time goes in v5:
time: 200 us; the launch traced here: 199 us
  waiting for transfers between devices  71.8 us (36%)
  blocking collectives  51.8 us (26%)
  starting transfers between devices  21.8 us (11%)
  Pallas kernels  17.1 us (9%)
  between operations  14.4 us (7%)
  other arithmetic  11.2 us (6%)
  local copies, waits for them, and re-layouts  10.4 us (5%)
    all_to_all x2, blocking collectives, exchange(): return lax.all_to_all(value, 'x', split_axis=0, concat_axis=0, tiled=True)  35.1 us
    ppermute x7, waiting for transfers between devices, swap(): return lax.ppermute(value, axis, [(0, 1), (1, 0)])  28.3 us
    reduce_scatter x1, waiting for transfers between devices, body(): lax.psum_scatter(parts.reshape(ny * 2 * rows, width), 'y', scatter_dimens...  24.6 us
    ppermute x7, starting transfers between devices, swap(): return lax.ppermute(value, axis, [(0, 1), (1, 0)])  18.3 us
    all_to_all x1, blocking collectives, body(): parts = lax.all_to_all(parts, 'zh', split_axis=0, concat_axis=0, tiled=True)  16.7 us
    all_gather x1, waiting for transfers between devices, body(): lax.all_gather(packed, 'y', axis=0, tiled=True).reshape(ny, held, width)  11.2 us
    all_to_all x1, waiting for transfers between devices, spread(): return lax.all_to_all(copies, axis, split_axis=0, concat_axis=0, tiled=True)  7.68 us
    pallas_call x1, Pallas kernels, output(): pl.pallas_call(functools.partial(output_kernel, experts, parts), grid=(ma...  6.34 us
  transfers between devices with their start and end apart: 10, of which 4 were waited for; matrix products, arithmetic and copies ran while one was open for 5% of the time, Pallas kernels for 2%

profile of v5, /device:TPU:6, one launch (start us, length us, event | category | flops | bytes accessed | tf_op | source)
XLA Modules:
  0.0 198.6 jit_solution(14440487765955485255)
XLA Ops:
  7.2 0.0 copy-start
  7.2 0.0 all-gather.2.cloned.1.call-start
  7.2 0.6 copy-done
  7.9 0.1 constant_dynamic-slice_fusion.2
  7.9 0.7 select_reduce_fusion
  8.7 0.8 fusion.10
  9.4 0.1 reshape.141
  9.5 1.0 constant_dynamic-slice_fusion.3
  10.5 0.7 fusion.5
  11.2 0.0 all-gather.2.cloned.1.call-update
  11.3 0.0 reduce-scatter.2.cloned.1.call-start
  11.3 1.4 pad_maximum_fusion.refs_0_
  12.8 0.0 copy-start.8
  12.8 4.3 %collective-permute-start = (bf16[3,224,1024]{2,1,0:T(8,128)(2,1)S(1)}, bf16[3,224,1024]{2,1,0:T(8,128)(2,1)S(1)}, u32[]{:S(2)}, u32[]{:S(2)}) collective-permute-start(bf16[3,224,1024]{2,1,0:T(8,128)(2,1)S(1)} %pad_maximum_fusion.refs_0_), channel_id=1, source_target_pairs={{0,4},{4,0},{1,5},{5,1},{2,6},{6,2},{3,7},{7,3},{8,12},{12,8},{9,1... | collective-permute-start | bytes 4128776 | tf_op jit(solution)/shard_map/ppermute | solution.py:19
  17.1 1.9 collective-permute-start.1
  19.0 28.2 %collective-permute-done.refs_1_ = bf16[3,224,1024]{2,1,0:T(8,128)(2,1)S(1)} collective-permute-done((bf16[3,224,1024]{2,1,0:T(8,128)(2,1)S(1)}, bf16[3,224,1024]{2,1,0:T(8,128)(2,1)S(1)}, u32[]{:S(2)}, u32[]{:S(2)}) %collective-permute-start) | collective-permute-done | bytes 1376288 | tf_op jit(solution)/shard_map/ppermute | solution.py:19
  47.2 1.9 collective-permute-start.2
  49.2 11.2 %all-gather.2.cloned.1.call-done = bf16[1152,1024]{1,0:T(8,128)(2,1)} async-done(((bf16[144,1024]{1,0:T(8,128)(2,1)}), bf16[1152,1024]{1,0:T(8,128)(2,1)}) %all-gather.2.cloned.1.call-update) | async-done | bytes 2359312 | tf_op jit(solution)/shard_map/all_gather | solution.py:287
  60.4 0.9 fusion.6
  61.2 0.1 reshape.146
  61.4 0.1 add.68
  61.4 0.1 eq.31
  61.5 0.0 collective-permute-done.1.refs_2_
  61.5 0.0 collective-permute-done.2.refs_3_
  61.5 0.0 copy-start.1
  61.6 1.7 copy-done.1
  63.2 5.7 %pick.1 = bf16[4,6,224,128]{3,2,1,0:T(8,128)(2,1)S(1)} custom-call(bf16[3,224,1024]{2,1,0:T(8,128)(2,1)S(1)} %pad_maximum_fusion.refs_0_, bf16[3,224,1024]{2,1,0:T(8,128)(2,1)S(1)} %collective-permute-done.refs_1_, bf16[3,224,1024]{2,1,0:T(8,128)(2,1)} %collective-permute-done.1.refs_2_, bf16[3,224,1024]{2,1,0:T(8,128)(2,1)} %collective-permute-done.2.refs_3_, ...), custom_call_target="tpu_custom_call" | custom-call | flops 2818572288 | bytes 8978432 | tf_op jit(solution)/shard_map/pick/pallas_call | solution.py:91
  68.9 0.0 copy-done.8
  68.9 17.9 %all_to_all.20.arrived_ref = bf16[4,6,224,128]{3,2,1,0:T(8,128)(2,1)S(1)} all-to-all(bf16[4,6,224,128]{3,2,1,0:T(8,128)(2,1)S(1)} %pick.1), channel_id=1, replica_groups=mesh['y'=8,'core'=2,'zh'=4,'zl'=2,'x'=4] {'x'}, dimensions={0} | all-to-all | bytes 2752512 | tf_op jit(solution)/shard_map/all_to_all | solution.py:300
  86.9 0.3 middle.1
  87.2 0.0 copy-start.9
  87.2 0.0 copy-start.11
  87.2 17.2 %all_to_all.21.refs_4_.shared_ref = bf16[4,6,224,128]{3,2,1,0:T(8,128)(2,1)S(1)} all-to-all(bf16[4,6,224,128]{3,2,1,0:T(8,128)(2,1)S(1)} %middle.1), channel_id=1, replica_groups=mesh['y'=8,'core'=2,'zh'=4,'zl'=2,'x'=4] {'x'}, dimensions={0} | all-to-all | bytes 2752512 | tf_op jit(solution)/shard_map/all_to_all | solution.py:300
  104.3 0.0 copy-done.9
  104.3 6.3 %output.1 = bf16[8,4,2,16,1024]{4,3,2,1,0:T(8,128)(2,1)S(1)} custom-call(bf16[3,224,1024]{2,1,0:T(8,128)(2,1)S(1)} %copy-done.9, bf16[3,224,1024]{2,1,0:T(8,128)(2,1)S(1)} %copy-done.11, bf16[3,224,1024]{2,1,0:T(8,128)(2,1)} %collective-permute-done.1.refs_2_, bf16[3,224,1024]{2,1,0:T(8,128)(2,1)} %collective-permute-done.2.refs_3_, ...), custom_call_target="tpu_custom_call" | custom-call | flops 2818572288 | bytes 8978432 | tf_op jit(solution)/shard_map/output/pallas_call | solution.py:197
  110.7 1.3 copy-done.7
  112.0 0.0 reduce-scatter.2.cloned.1.call-update
  112.1 1.3 copy-done.4
  113.4 0.8 gradient.4
  114.2 1.6 gradient.5
  115.8 1.9 collective-permute-start.5
  117.7 2.4 %collective-permute-start.3 = (bf16[2,1,224,1024]{3,2,1,0:T(8,128)(2,1)S(1)}, bf16[2,1,224,1024]{3,2,1,0:T(8,128)(2,1)S(1)}, u32[]{:S(2)}, u32[]{:S(2)}) collective-permute-start(bf16[2,1,224,1024]{3,2,1,0:T(8,128)(2,1)S(1)} %gradient.4), channel_id=1, source_target_pairs={{0,32},{32,0},{1,33},{33,1},{2,34},{34,2},{3,35},{35,3},{4,36},{36... | collective-permute-start | bytes 2752520 | tf_op jit(solution)/shard_map/ppermute | solution.py:19
  120.1 1.6 gradient.7
  121.8 0.0 collective-permute-done.5
  121.8 1.6 fusion.1
  123.4 3.6 %collective-permute-start.6 = (bf16[2,224,1024]{2,1,0:T(8,128)(2,1)}, bf16[2,224,1024]{2,1,0:T(8,128)(2,1)}, u32[]{:S(2)}, u32[]{:S(2)}) collective-permute-start(bf16[2,224,1024]{2,1,0:T(8,128)(2,1)} %fusion.1), channel_id=1, source_target_pairs={{0,4},{4,0},{1,5},{5,1},{2,6},{6,2},{3,7},{7,3},{8,12},{12,8},{9,1... | collective-permute-start | bytes 2752520 | tf_op jit(solution)/shard_map/ppermute | solution.py:19
  127.0 0.8 gradient.6
  127.7 0.0 collective-permute-done.3
  127.8 0.9 fusion.4
  128.7 0.2 copy-done.13
  128.9 2.3 %collective-permute-start.4 = (bf16[1,224,1024]{2,1,0:T(8,128)(2,1)}, bf16[1,224,1024]{2,1,0:T(8,128)(2,1)}, u32[]{:S(2)}, u32[]{:S(2)}) collective-permute-start(bf16[1,224,1024]{2,1,0:T(8,128)(2,1)} %fusion.4), channel_id=1, source_target_pairs={{0,4},{4,0},{1,5},{5,1},{2,6},{6,2},{3,7},{7,3},{8,12},{12,8},{9,1... | collective-permute-start | bytes 1376264 | tf_op jit(solution)/shard_map/ppermute | solution.py:19
  131.2 24.6 %reduce-scatter.2.cloned.1.call-done = bf16[128,1024]{1,0:T(8,128)(2,1)} async-done(((bf16[1024,1024]{1,0:T(8,128)(2,1)}), bf16[128,1024]{1,0:T(8,128)(2,1)}) %reduce-scatter.2.cloned.1.call-update) | async-done | bytes 262160 | tf_op jit(solution)/shard_map/reduce_scatter | solution.py:308
  155.9 16.7 %all_to_all.22 = bf16[4,2,16,1024]{3,2,1,0:T(8,128)(2,1)S(1)} all-to-all(bf16[4,2,16,1024]{3,2,1,0:T(8,128)(2,1)} %bitcast.57), channel_id=1, replica_groups=mesh['y'=8,'core'=2,'zh'=4,'zl'=2,'x'=4] {'zh'}, dimensions={0} | all-to-all | bytes 524288 | tf_op jit(solution)/shard_map/all_to_all | solution.py:331
  172.6 0.0 collective-permute-done.4
  172.6 0.0 collective-permute-done.6
  172.6 0.9 broadcast_in_dim.24
  173.5 3.5 %all-to-all-start.3 = ((bf16[8,2,16,1024]{3,2,1,0:T(8,128)(2,1)}), bf16[8,2,16,1024]{3,2,1,0:T(8,128)(2,1)S(1)}, u32[]{:S(2)}, u32[]{:S(2)}) async-start(bf16[8,2,16,1024]{3,2,1,0:T(8,128)(2,1)} %broadcast_in_dim.24), calls=%async_computation.4 | async-start | bytes 1048576 | tf_op jit(solution)/shard_map/all_to_all | solution.py:33
  177.0 2.0 fusion
  179.0 1.0 fusion.13
  180.0 0.5 copy-done.14
  180.5 2.0 %fusion.2 = bf16[1,224,1024]{2,1,0:T(8,128)(2,1)} fusion(bf16[1,224,1024]{2,1,0:T(8,128)(2,1)} %collective-permute-done.4, bf16[2,1,224,1024]{3,2,1,0:T(8,128)(2,1)S(1)} %copy-done.14, bf16[2,1,224,1024]{3,2,1,0:T(8,128)(2,1)S(1)} %gradient.6), kind=kLoop, calls=%fused_computation.6 | loop fusion | flops 1376256 | bytes 1835008 | tf_op jit(solution)/shard_map/convert_element_type | solution.py:338
  182.5 7.7 %all-to-all-done.3 = bf16[8,2,16,1024]{3,2,1,0:T(8,128)(2,1)S(1)} async-done(((bf16[8,2,16,1024]{3,2,1,0:T(8,128)(2,1)}), bf16[8,2,16,1024]{3,2,1,0:T(8,128)(2,1)S(1)}, u32[]{:S(2)}, u32[]{:S(2)}) %all-to-all-start.3) | async-done | bytes 524320 | tf_op jit(solution)/shard_map/all_to_all | solution.py:33
  190.3 0.7 copy.23
  191.0 0.7 copy.22
  (25 shorter events, 0.2 us)
Async XLA Ops:
  7.2 0.7 copy-start
  7.2 53.2 %all-gather.2.cloned.1.call-start = ((), (), s32[]{:S(2)}) async-start(), calls=%async_computation.5 | async-start | bytes 2654208 | tf_op jit(solution)/shard_map/all_gather | solution.py:287
  11.3 144.6 %reduce-scatter.2.cloned.1.call-start = ((), (), s32[]{:S(2)}) async-start(), calls=%async_computation.6 | async-start | bytes 2359296 | tf_op jit(solution)/shard_map/reduce_scatter | solution.py:308
  12.8 56.1 %copy-start.8 = (bf16[3,224,1024]{2,1,0:T(8,128)(2,1)}, bf16[3,224,1024]{2,1,0:T(8,128)(2,1)S(1)}, u32[]{:S(2)}) copy-start(bf16[3,224,1024]{2,1,0:T(8,128)(2,1)S(1)} %pad_maximum_fusion.refs_0_) | copy-start | bytes 4128772
  12.8 34.5 %collective-permute-start = (bf16[3,224,1024]{2,1,0:T(8,128)(2,1)S(1)}, bf16[3,224,1024]{2,1,0:T(8,128)(2,1)S(1)}, u32[]{:S(2)}, u32[]{:S(2)}) collective-permute-start(bf16[3,224,1024]{2,1,0:T(8,128)(2,1)S(1)} %pad_maximum_fusion.refs_0_), channel_id=1, source_target_pairs={{0,4},{4,0},{1,5},{5,1},{2,6},{6,2},{3,7},{7,3},{8,12},{12,8},{9,1... | collective-permute-start | bytes 4128776 | tf_op jit(solution)/shard_map/ppermute | solution.py:19
  17.1 44.5 %collective-permute-start.1 = (bf16[3,224,1024]{2,1,0:T(8,128)(2,1)S(1)}, bf16[3,224,1024]{2,1,0:T(8,128)(2,1)}, u32[]{:S(2)}, u32[]{:S(2)}) collective-permute-start(bf16[3,224,1024]{2,1,0:T(8,128)(2,1)S(1)} %pad_maximum_fusion.refs_0_), channel_id=1, source_target_pairs={{0,32},{32,0},{1,33},{33,1},{2,34},{34,2},{3,35},{35,3},{4,36},{36... | collective-permute-start | bytes 4128776 | tf_op jit(solution)/shard_map/ppermute | solution.py:19
  47.2 21.7 %copy-start.10 = (bf16[3,224,1024]{2,1,0:T(8,128)(2,1)}, bf16[3,224,1024]{2,1,0:T(8,128)(2,1)S(1)}, u32[]{:S(2)}) copy-start(bf16[3,224,1024]{2,1,0:T(8,128)(2,1)S(1)} %collective-permute-done.refs_1_) | copy-start | bytes 4128772
  47.2 14.3 %collective-permute-start.2 = (bf16[3,224,1024]{2,1,0:T(8,128)(2,1)S(1)}, bf16[3,224,1024]{2,1,0:T(8,128)(2,1)}, u32[]{:S(2)}, u32[]{:S(2)}) collective-permute-start(bf16[3,224,1024]{2,1,0:T(8,128)(2,1)S(1)} %collective-permute-done.refs_1_), channel_id=1, source_target_pairs={{0,32},{32,0},{1,33},{33,1},{2,34},{34,2},{3,35},{35,3},{4,36},{36... | collective-permute-start | bytes 4128776 | tf_op jit(solution)/shard_map/ppermute | solution.py:19
  61.5 1.7 copy-start.1
  87.2 17.2 %copy-start.9 = (bf16[3,224,1024]{2,1,0:T(8,128)(2,1)S(1)}, bf16[3,224,1024]{2,1,0:T(8,128)(2,1)}, u32[]{:S(2)}) copy-start(bf16[3,224,1024]{2,1,0:T(8,128)(2,1)} %copy-done.8) | copy-start | bytes 4128772
  87.2 17.2 %copy-start.11 = (bf16[3,224,1024]{2,1,0:T(8,128)(2,1)S(1)}, bf16[3,224,1024]{2,1,0:T(8,128)(2,1)}, u32[]{:S(2)}) copy-start(bf16[3,224,1024]{2,1,0:T(8,128)(2,1)} %copy-done.10) | copy-start | bytes 4128772
  104.3 6.4 %copy-start.3 = (bf16[4,6,224,128]{3,2,1,0:T(8,128)(2,1)}, bf16[4,6,224,128]{3,2,1,0:T(8,128)(2,1)S(1)}, u32[]{:S(2)}) copy-start(bf16[4,6,224,128]{3,2,1,0:T(8,128)(2,1)S(1)} %all_to_all.21.refs_4_.shared_ref) | copy-start | bytes 4128772
  104.3 7.7 %copy-start.2 = (bf16[1152,1024]{1,0:T(8,128)(2,1)S(1)}, bf16[1152,1024]{1,0:T(8,128)(2,1)}, u32[]{:S(2)}) copy-start(bf16[1152,1024]{1,0:T(8,128)(2,1)} %all-gather.2.cloned.1.call-done) | copy-start | bytes 7077892
  110.7 1.3 copy-start.7
  112.1 1.3 copy-start.4
  115.8 6.0 %collective-permute-start.5 = (bf16[2,2,224,1024]{3,2,1,0:T(8,128)(2,1)S(1)}, bf16[2,2,224,1024]{3,2,1,0:T(8,128)(2,1)S(1)}, u32[]{:S(2)}, u32[]{:S(2)}) collective-permute-start(bf16[2,2,224,1024]{3,2,1,0:T(8,128)(2,1)S(1)} %gradient.5), channel_id=1, source_target_pairs={{0,32},{32,0},{1,33},{33,1},{2,34},{34,2},{3,35},{35,3},{4,36},{36... | collective-permute-start | bytes 5505032 | tf_op jit(solution)/shard_map/ppermute | solution.py:19
  117.7 10.0 %collective-permute-start.3 = (bf16[2,1,224,1024]{3,2,1,0:T(8,128)(2,1)S(1)}, bf16[2,1,224,1024]{3,2,1,0:T(8,128)(2,1)S(1)}, u32[]{:S(2)}, u32[]{:S(2)}) collective-permute-start(bf16[2,1,224,1024]{3,2,1,0:T(8,128)(2,1)S(1)} %gradient.4), channel_id=1, source_target_pairs={{0,32},{32,0},{1,33},{33,1},{2,34},{34,2},{3,35},{35,3},{4,36},{36... | collective-permute-start | bytes 2752520 | tf_op jit(solution)/shard_map/ppermute | solution.py:19
  121.8 6.0 %copy-start.5 = (bf16[2,2,224,1024]{3,2,1,0:T(8,128)(2,1)}, bf16[2,2,224,1024]{3,2,1,0:T(8,128)(2,1)S(1)}, u32[]{:S(2)}) copy-start(bf16[2,2,224,1024]{3,2,1,0:T(8,128)(2,1)S(1)} %gradient.7) | copy-start | bytes 5505028
  121.8 6.0 %copy-start.12 = (bf16[2,2,224,1024]{3,2,1,0:T(8,128)(2,1)}, bf16[2,2,224,1024]{3,2,1,0:T(8,128)(2,1)S(1)}, u32[]{:S(2)}) copy-start(bf16[2,2,224,1024]{3,2,1,0:T(8,128)(2,1)S(1)} %collective-permute-done.5) | copy-start | bytes 5505028
  123.4 49.2 %collective-permute-start.6 = (bf16[2,224,1024]{2,1,0:T(8,128)(2,1)}, bf16[2,224,1024]{2,1,0:T(8,128)(2,1)}, u32[]{:S(2)}, u32[]{:S(2)}) collective-permute-start(bf16[2,224,1024]{2,1,0:T(8,128)(2,1)} %fusion.1), channel_id=1, source_target_pairs={{0,4},{4,0},{1,5},{5,1},{2,6},{6,2},{3,7},{7,3},{8,12},{12,8},{9,1... | collective-permute-start | bytes 2752520 | tf_op jit(solution)/shard_map/ppermute | solution.py:19
  127.8 1.2 copy-start.13
  127.8 49.2 %copy-start.6 = (bf16[2,2,224,1024]{3,2,1,0:T(8,128)(2,1)S(1)}, bf16[2,2,224,1024]{3,2,1,0:T(8,128)(2,1)}, u32[]{:S(2)}) copy-start(bf16[2,2,224,1024]{3,2,1,0:T(8,128)(2,1)} %copy-done.5) | copy-start | bytes 5505028
  128.9 43.7 %collective-permute-start.4 = (bf16[1,224,1024]{2,1,0:T(8,128)(2,1)}, bf16[1,224,1024]{2,1,0:T(8,128)(2,1)}, u32[]{:S(2)}, u32[]{:S(2)}) collective-permute-start(bf16[1,224,1024]{2,1,0:T(8,128)(2,1)} %fusion.4), channel_id=1, source_target_pairs={{0,4},{4,0},{1,5},{5,1},{2,6},{6,2},{3,7},{7,3},{8,12},{12,8},{9,1... | collective-permute-start | bytes 1376264 | tf_op jit(solution)/shard_map/ppermute | solution.py:19
  173.5 16.7 %all-to-all-start.3 = ((bf16[8,2,16,1024]{3,2,1,0:T(8,128)(2,1)}), bf16[8,2,16,1024]{3,2,1,0:T(8,128)(2,1)S(1)}, u32[]{:S(2)}, u32[]{:S(2)}) async-start(bf16[8,2,16,1024]{3,2,1,0:T(8,128)(2,1)} %broadcast_in_dim.24), calls=%async_computation.4 | async-start | bytes 1048576 | tf_op jit(solution)/shard_map/all_to_all | solution.py:33
  179.0 1.5 copy-start.14
Sparse Core Ops, SparseCore 0:
  11.4 48.9 all-gather.1
  112.2 43.6 reduce-scatter.1

commit v6 on v5

--- a/solution.py
+++ b/solution.py
@@ -25,12 +25,6 @@
 
 def contract_first(left, right):
     return lax.dot_general(left, right, (((0,), (0,)), ((), ())), preferred_element_type=F32)
-
-
-def spread(value, axis, count):
-    copies = jnp.broadcast_to(value[None], (count,) + value.shape)
-    copies = lax.optimization_barrier(copies)
-    return lax.all_to_all(copies, axis, split_axis=0, concat_axis=0, tiled=True)
 
 
 def whole(memory_space):
@@ -203,7 +197,7 @@
             pl.BlockSpec((experts, top, total), lambda i: (0, 0, 0)),
         ],
         out_specs=pl.BlockSpec((ny, nh, 1, small, width), lambda i: (0, 0, (i + 1) // 2, 0, 0)),
-        out_shape=jax.ShapeDtypeStruct((ny, nh, 2, small, width), BF16),
+        out_shape=pltpu.HBM((ny, nh, 2, small, width), BF16),
         scratch_shapes=[pltpu.VMEM((total, width), F32)],
         compiler_params=pltpu.CompilerParams(vmem_limit_bytes=VMEM_BYTES),
         cost_estimate=pl.CostEstimate(
@@ -330,8 +324,9 @@
     parts = scattered.reshape(nh, 2, small, width)
     parts = lax.all_to_all(parts, "zh", split_axis=0, concat_axis=0, tiled=True)
     parts = jnp.sum(parts.astype(F32), axis=0).astype(BF16)
-    parts, near_down, near = lax.optimization_barrier((parts, near_down, near))
-    ends = spread(parts, ("zh", "zl"), nh * nl)
+    copies = jnp.broadcast_to(parts[None], (nh * nl,) + parts.shape)
+    copies, near_down, near = lax.optimization_barrier((copies, near_down, near))
+    ends = lax.all_to_all(copies, ("zh", "zl"), split_axis=0, concat_axis=0, tiled=True)
     ends = ends.reshape(nh, nl, 2, small, width).transpose(2, 1, 0, 3, 4).reshape(2, block, width)
 
     def finish(kept, sent, near):

time: 200 us -> 200 us (level)
    unnamed x30 -> x28, local copies, waits for them, and re-layouts: 5.71 us -> 4.38 us
where the time goes in v6:
time: 200 us; the launch traced here: 199 us
  waiting for transfers between devices  71.7 us (36%)
  blocking collectives  52.4 us (26%)
  starting transfers between devices  21.8 us (11%)
  Pallas kernels  18 us (9%)
  between operations  14.4 us (7%)
  other arithmetic  11.2 us (6%)
  local copies, waits for them, and re-layouts  9.1 us (5%)
    all_to_all x2, blocking collectives, exchange(): return lax.all_to_all(value, 'x', split_axis=0, concat_axis=0, tiled=True)  35.1 us
    ppermute x7, waiting for transfers between devices, swap(): return lax.ppermute(value, axis, [(0, 1), (1, 0)])  28.3 us
    reduce_scatter x1, waiting for transfers between devices, body(): lax.psum_scatter(parts.reshape(ny * 2 * rows, width), 'y', scatter_dimens...  24.5 us
    ppermute x7, starting transfers between devices, swap(): return lax.ppermute(value, axis, [(0, 1), (1, 0)])  18.3 us
    all_to_all x1, blocking collectives, body(): parts = lax.all_to_all(parts, 'zh', split_axis=0, concat_axis=0, tiled=True)  17.3 us
    all_gather x1, waiting for transfers between devices, body(): lax.all_gather(packed, 'y', axis=0, tiled=True).reshape(ny, held, width)  11.2 us
    all_to_all x1, waiting for transfers between devices, body(): lax.all_to_all(copies, ('zh', 'zl'), split_axis=0, concat_axis=0, tiled=T...  7.68 us
    pallas_call x1, Pallas kernels, output(): pl.pallas_call(functools.partial(output_kernel, experts, parts), grid=(ma...  7.21 us
  transfers between devices with their start and end apart: 10, of which 4 were waited for; matrix products, arithmetic and copies ran while one was open for 5% of the time, Pallas kernels for 2%

profile of v6, /device:TPU:6, one launch (start us, length us, event | category | flops | bytes accessed | tf_op | source)
XLA Modules:
  0.0 198.6 jit_solution(17061545744461463683)
XLA Ops:
  7.2 0.0 copy-start
  7.2 0.0 all-gather.2.cloned.1.call-start
  7.2 0.6 copy-done
  7.9 0.1 constant_dynamic-slice_fusion.2
  7.9 0.7 select_reduce_fusion
  8.7 0.8 fusion.10
  9.4 0.1 reshape.141
  9.5 1.0 constant_dynamic-slice_fusion.3
  10.5 0.7 fusion.5
  11.2 0.0 all-gather.2.cloned.1.call-update
  11.3 0.0 reduce-scatter.2.cloned.1.call-start
  11.3 1.4 pad_maximum_fusion.refs_0_
  12.8 0.0 copy-start.7
  12.8 4.3 %collective-permute-start = (bf16[3,224,1024]{2,1,0:T(8,128)(2,1)S(1)}, bf16[3,224,1024]{2,1,0:T(8,128)(2,1)S(1)}, u32[]{:S(2)}, u32[]{:S(2)}) collective-permute-start(bf16[3,224,1024]{2,1,0:T(8,128)(2,1)S(1)} %pad_maximum_fusion.refs_0_), channel_id=1, source_target_pairs={{0,4},{4,0},{1,5},{5,1},{2,6},{6,2},{3,7},{7,3},{8,12},{12,8},{9,1... | collective-permute-start | bytes 4128776 | tf_op jit(solution)/shard_map/ppermute | solution.py:19
  17.1 1.9 collective-permute-start.1
  19.0 28.2 %collective-permute-done.refs_1_ = bf16[3,224,1024]{2,1,0:T(8,128)(2,1)S(1)} collective-permute-done((bf16[3,224,1024]{2,1,0:T(8,128)(2,1)S(1)}, bf16[3,224,1024]{2,1,0:T(8,128)(2,1)S(1)}, u32[]{:S(2)}, u32[]{:S(2)}) %collective-permute-start) | collective-permute-done | bytes 1376288 | tf_op jit(solution)/shard_map/ppermute | solution.py:19
  47.2 1.9 collective-permute-start.2
  49.2 11.2 %all-gather.2.cloned.1.call-done = bf16[1152,1024]{1,0:T(8,128)(2,1)} async-done(((bf16[144,1024]{1,0:T(8,128)(2,1)}), bf16[1152,1024]{1,0:T(8,128)(2,1)}) %all-gather.2.cloned.1.call-update) | async-done | bytes 2359312 | tf_op jit(solution)/shard_map/all_gather | solution.py:281
  60.4 0.9 fusion.6
  61.2 0.1 reshape.146
  61.4 0.1 add.68
  61.4 0.1 eq.31
  61.5 0.0 collective-permute-done.1.refs_2_
  61.5 0.0 collective-permute-done.2.refs_3_
  61.5 0.0 copy-start.1
  61.6 1.7 copy-done.1
  63.2 5.8 %pick.1 = bf16[4,6,224,128]{3,2,1,0:T(8,128)(2,1)S(1)} custom-call(bf16[3,224,1024]{2,1,0:T(8,128)(2,1)S(1)} %pad_maximum_fusion.refs_0_, bf16[3,224,1024]{2,1,0:T(8,128)(2,1)S(1)} %collective-permute-done.refs_1_, bf16[3,224,1024]{2,1,0:T(8,128)(2,1)} %collective-permute-done.1.refs_2_, bf16[3,224,1024]{2,1,0:T(8,128)(2,1)} %collective-permute-done.2.refs_3_, ...), custom_call_target="tpu_custom_call" | custom-call | flops 2818572288 | bytes 8978432 | tf_op jit(solution)/shard_map/pick/pallas_call | solution.py:85
  69.0 0.0 copy-done.7
  69.0 0.0 copy-done.9
  69.0 17.9 %all_to_all.20.arrived_ref = bf16[4,6,224,128]{3,2,1,0:T(8,128)(2,1)S(1)} all-to-all(bf16[4,6,224,128]{3,2,1,0:T(8,128)(2,1)S(1)} %pick.1), channel_id=1, replica_groups=mesh['y'=8,'core'=2,'zh'=4,'zl'=2,'x'=4] {'x'}, dimensions={0} | all-to-all | bytes 2752512 | tf_op jit(solution)/shard_map/all_to_all | solution.py:294
  86.9 0.3 middle.1
  87.2 0.0 copy-start.8
  87.2 0.0 copy-start.10
  87.2 17.2 %all_to_all.21.refs_4_.shared_ref = bf16[4,6,224,128]{3,2,1,0:T(8,128)(2,1)S(1)} all-to-all(bf16[4,6,224,128]{3,2,1,0:T(8,128)(2,1)S(1)} %middle.1), channel_id=1, replica_groups=mesh['y'=8,'core'=2,'zh'=4,'zl'=2,'x'=4] {'x'}, dimensions={0} | all-to-all | bytes 2752512 | tf_op jit(solution)/shard_map/all_to_all | solution.py:294
  104.4 0.0 copy-done.8
  104.4 7.2 %output.1 = bf16[8,4,2,16,1024]{4,3,2,1,0:T(8,128)(2,1)} custom-call(bf16[3,224,1024]{2,1,0:T(8,128)(2,1)S(1)} %copy-done.8, bf16[3,224,1024]{2,1,0:T(8,128)(2,1)S(1)} %copy-done.10, bf16[3,224,1024]{2,1,0:T(8,128)(2,1)} %collective-permute-done.1.refs_2_, bf16[3,224,1024]{2,1,0:T(8,128)(2,1)} %collective-permute-done.2.refs_3_, ...), custom_call_target="tpu_custom_call" | custom-call | flops 2818572288 | bytes 8978432 | tf_op jit(solution)/shard_map/output/pallas_call | solution.py:191
  111.6 0.0 reduce-scatter.2.cloned.1.call-update
  111.7 1.3 copy-done.4
  113.0 0.8 gradient.4
  113.8 1.6 gradient.5
  115.4 1.9 collective-permute-start.5
  117.3 2.4 %collective-permute-start.3 = (bf16[2,1,224,1024]{3,2,1,0:T(8,128)(2,1)S(1)}, bf16[2,1,224,1024]{3,2,1,0:T(8,128)(2,1)S(1)}, u32[]{:S(2)}, u32[]{:S(2)}) collective-permute-start(bf16[2,1,224,1024]{3,2,1,0:T(8,128)(2,1)S(1)} %gradient.4), channel_id=1, source_target_pairs={{0,32},{32,0},{1,33},{33,1},{2,34},{34,2},{3,35},{35,3},{4,36},{36... | collective-permute-start | bytes 2752520 | tf_op jit(solution)/shard_map/ppermute | solution.py:19
  119.8 1.6 gradient.7
  121.4 0.0 collective-permute-done.5
  121.4 1.6 fusion.1
  123.0 3.5 %collective-permute-start.6 = (bf16[2,224,1024]{2,1,0:T(8,128)(2,1)}, bf16[2,224,1024]{2,1,0:T(8,128)(2,1)}, u32[]{:S(2)}, u32[]{:S(2)}) collective-permute-start(bf16[2,224,1024]{2,1,0:T(8,128)(2,1)} %fusion.1), channel_id=1, source_target_pairs={{0,4},{4,0},{1,5},{5,1},{2,6},{6,2},{3,7},{7,3},{8,12},{12,8},{9,1... | collective-permute-start | bytes 2752520 | tf_op jit(solution)/shard_map/ppermute | solution.py:19
  126.6 0.8 gradient.6
  127.4 0.0 collective-permute-done.3
  127.4 0.9 fusion.4
  128.4 0.2 copy-done.12
  128.6 2.3 %collective-permute-start.4 = (bf16[1,224,1024]{2,1,0:T(8,128)(2,1)}, bf16[1,224,1024]{2,1,0:T(8,128)(2,1)}, u32[]{:S(2)}, u32[]{:S(2)}) collective-permute-start(bf16[1,224,1024]{2,1,0:T(8,128)(2,1)} %fusion.4), channel_id=1, source_target_pairs={{0,4},{4,0},{1,5},{5,1},{2,6},{6,2},{3,7},{7,3},{8,12},{12,8},{9,1... | collective-permute-start | bytes 1376264 | tf_op jit(solution)/shard_map/ppermute | solution.py:19
  130.8 24.5 %reduce-scatter.2.cloned.1.call-done = bf16[128,1024]{1,0:T(8,128)(2,1)} async-done(((bf16[1024,1024]{1,0:T(8,128)(2,1)}), bf16[128,1024]{1,0:T(8,128)(2,1)}) %reduce-scatter.2.cloned.1.call-update) | async-done | bytes 262160 | tf_op jit(solution)/shard_map/reduce_scatter | solution.py:302
  155.4 17.3 %all_to_all.22 = bf16[4,2,16,1024]{3,2,1,0:T(8,128)(2,1)S(1)} all-to-all(bf16[4,2,16,1024]{3,2,1,0:T(8,128)(2,1)} %bitcast.57), channel_id=1, replica_groups=mesh['y'=8,'core'=2,'zh'=4,'zl'=2,'x'=4] {'zh'}, dimensions={0} | all-to-all | bytes 524288 | tf_op jit(solution)/shard_map/all_to_all | solution.py:325
  172.7 0.0 collective-permute-done.4
  172.7 0.0 collective-permute-done.6
  172.7 0.9 broadcast_in_dim.24
  173.6 3.5 %all-to-all-start.3 = ((bf16[8,2,16,1024]{3,2,1,0:T(8,128)(2,1)}), bf16[8,2,16,1024]{3,2,1,0:T(8,128)(2,1)S(1)}, u32[]{:S(2)}, u32[]{:S(2)}) async-start(bf16[8,2,16,1024]{3,2,1,0:T(8,128)(2,1)} %broadcast_in_dim.24), calls=%async_computation.4 | async-start | bytes 1048576 | tf_op jit(solution)/shard_map/all_to_all | solution.py:329
  177.1 2.0 fusion
  179.1 1.0 fusion.13
  180.1 0.5 copy-done.13
  180.6 2.0 %fusion.2 = bf16[1,224,1024]{2,1,0:T(8,128)(2,1)} fusion(bf16[1,224,1024]{2,1,0:T(8,128)(2,1)} %collective-permute-done.4, bf16[2,1,224,1024]{3,2,1,0:T(8,128)(2,1)S(1)} %copy-done.13, bf16[2,1,224,1024]{3,2,1,0:T(8,128)(2,1)S(1)} %gradient.6), kind=kLoop, calls=%fused_computation.6 | loop fusion | flops 1376256 | bytes 1835008 | tf_op jit(solution)/shard_map/convert_element_type | solution.py:333
  182.6 7.7 %all-to-all-done.3 = bf16[8,2,16,1024]{3,2,1,0:T(8,128)(2,1)S(1)} async-done(((bf16[8,2,16,1024]{3,2,1,0:T(8,128)(2,1)}), bf16[8,2,16,1024]{3,2,1,0:T(8,128)(2,1)S(1)}, u32[]{:S(2)}, u32[]{:S(2)}) %all-to-all-start.3) | async-done | bytes 524320 | tf_op jit(solution)/shard_map/all_to_all | solution.py:329
  190.3 0.7 copy.23
  191.1 0.7 copy.22
  (23 shorter events, 0.2 us)
Async XLA Ops:
  7.2 0.7 copy-start
  7.2 53.2 %all-gather.2.cloned.1.call-start = ((), (), s32[]{:S(2)}) async-start(), calls=%async_computation.5 | async-start | bytes 2654208 | tf_op jit(solution)/shard_map/all_gather | solution.py:281
  11.3 144.1 %reduce-scatter.2.cloned.1.call-start = ((), (), s32[]{:S(2)}) async-start(), calls=%async_computation.6 | async-start | bytes 2359296 | tf_op jit(solution)/shard_map/reduce_scatter | solution.py:302
  12.8 56.2 %copy-start.7 = (bf16[3,224,1024]{2,1,0:T(8,128)(2,1)}, bf16[3,224,1024]{2,1,0:T(8,128)(2,1)S(1)}, u32[]{:S(2)}) copy-start(bf16[3,224,1024]{2,1,0:T(8,128)(2,1)S(1)} %pad_maximum_fusion.refs_0_) | copy-start | bytes 4128772
  12.8 34.5 %collective-permute-start = (bf16[3,224,1024]{2,1,0:T(8,128)(2,1)S(1)}, bf16[3,224,1024]{2,1,0:T(8,128)(2,1)S(1)}, u32[]{:S(2)}, u32[]{:S(2)}) collective-permute-start(bf16[3,224,1024]{2,1,0:T(8,128)(2,1)S(1)} %pad_maximum_fusion.refs_0_), channel_id=1, source_target_pairs={{0,4},{4,0},{1,5},{5,1},{2,6},{6,2},{3,7},{7,3},{8,12},{12,8},{9,1... | collective-permute-start | bytes 4128776 | tf_op jit(solution)/shard_map/ppermute | solution.py:19
  17.1 44.5 %collective-permute-start.1 = (bf16[3,224,1024]{2,1,0:T(8,128)(2,1)S(1)}, bf16[3,224,1024]{2,1,0:T(8,128)(2,1)}, u32[]{:S(2)}, u32[]{:S(2)}) collective-permute-start(bf16[3,224,1024]{2,1,0:T(8,128)(2,1)S(1)} %pad_maximum_fusion.refs_0_), channel_id=1, source_target_pairs={{0,32},{32,0},{1,33},{33,1},{2,34},{34,2},{3,35},{35,3},{4,36},{36... | collective-permute-start | bytes 4128776 | tf_op jit(solution)/shard_map/ppermute | solution.py:19
  47.2 21.8 %copy-start.9 = (bf16[3,224,1024]{2,1,0:T(8,128)(2,1)}, bf16[3,224,1024]{2,1,0:T(8,128)(2,1)S(1)}, u32[]{:S(2)}) copy-start(bf16[3,224,1024]{2,1,0:T(8,128)(2,1)S(1)} %collective-permute-done.refs_1_) | copy-start | bytes 4128772
  47.2 14.3 %collective-permute-start.2 = (bf16[3,224,1024]{2,1,0:T(8,128)(2,1)S(1)}, bf16[3,224,1024]{2,1,0:T(8,128)(2,1)}, u32[]{:S(2)}, u32[]{:S(2)}) collective-permute-start(bf16[3,224,1024]{2,1,0:T(8,128)(2,1)S(1)} %collective-permute-done.refs_1_), channel_id=1, source_target_pairs={{0,32},{32,0},{1,33},{33,1},{2,34},{34,2},{3,35},{35,3},{4,36},{36... | collective-permute-start | bytes 4128776 | tf_op jit(solution)/shard_map/ppermute | solution.py:19
  61.5 1.7 copy-start.1
  87.2 17.2 %copy-start.8 = (bf16[3,224,1024]{2,1,0:T(8,128)(2,1)S(1)}, bf16[3,224,1024]{2,1,0:T(8,128)(2,1)}, u32[]{:S(2)}) copy-start(bf16[3,224,1024]{2,1,0:T(8,128)(2,1)} %copy-done.7) | copy-start | bytes 4128772
  87.2 17.2 %copy-start.10 = (bf16[3,224,1024]{2,1,0:T(8,128)(2,1)S(1)}, bf16[3,224,1024]{2,1,0:T(8,128)(2,1)}, u32[]{:S(2)}) copy-start(bf16[3,224,1024]{2,1,0:T(8,128)(2,1)} %copy-done.9) | copy-start | bytes 4128772
  104.4 7.2 %copy-start.3 = (bf16[4,6,224,128]{3,2,1,0:T(8,128)(2,1)}, bf16[4,6,224,128]{3,2,1,0:T(8,128)(2,1)S(1)}, u32[]{:S(2)}) copy-start(bf16[4,6,224,128]{3,2,1,0:T(8,128)(2,1)S(1)} %all_to_all.21.refs_4_.shared_ref) | copy-start | bytes 4128772
  104.4 7.2 %copy-start.2 = (bf16[1152,1024]{1,0:T(8,128)(2,1)S(1)}, bf16[1152,1024]{1,0:T(8,128)(2,1)}, u32[]{:S(2)}) copy-start(bf16[1152,1024]{1,0:T(8,128)(2,1)} %all-gather.2.cloned.1.call-done) | copy-start | bytes 7077892
  111.7 1.3 copy-start.4
  115.4 6.0 %collective-permute-start.5 = (bf16[2,2,224,1024]{3,2,1,0:T(8,128)(2,1)S(1)}, bf16[2,2,224,1024]{3,2,1,0:T(8,128)(2,1)S(1)}, u32[]{:S(2)}, u32[]{:S(2)}) collective-permute-start(bf16[2,2,224,1024]{3,2,1,0:T(8,128)(2,1)S(1)} %gradient.5), channel_id=1, source_target_pairs={{0,32},{32,0},{1,33},{33,1},{2,34},{34,2},{3,35},{35,3},{4,36},{36... | collective-permute-start | bytes 5505032 | tf_op jit(solution)/shard_map/ppermute | solution.py:19
  117.3 10.0 %collective-permute-start.3 = (bf16[2,1,224,1024]{3,2,1,0:T(8,128)(2,1)S(1)}, bf16[2,1,224,1024]{3,2,1,0:T(8,128)(2,1)S(1)}, u32[]{:S(2)}, u32[]{:S(2)}) collective-permute-start(bf16[2,1,224,1024]{3,2,1,0:T(8,128)(2,1)S(1)} %gradient.4), channel_id=1, source_target_pairs={{0,32},{32,0},{1,33},{33,1},{2,34},{34,2},{3,35},{35,3},{4,36},{36... | collective-permute-start | bytes 2752520 | tf_op jit(solution)/shard_map/ppermute | solution.py:19
  121.4 6.0 %copy-start.5 = (bf16[2,2,224,1024]{3,2,1,0:T(8,128)(2,1)}, bf16[2,2,224,1024]{3,2,1,0:T(8,128)(2,1)S(1)}, u32[]{:S(2)}) copy-start(bf16[2,2,224,1024]{3,2,1,0:T(8,128)(2,1)S(1)} %gradient.7) | copy-start | bytes 5505028
  121.4 6.0 %copy-start.11 = (bf16[2,2,224,1024]{3,2,1,0:T(8,128)(2,1)}, bf16[2,2,224,1024]{3,2,1,0:T(8,128)(2,1)S(1)}, u32[]{:S(2)}) copy-start(bf16[2,2,224,1024]{3,2,1,0:T(8,128)(2,1)S(1)} %collective-permute-done.5) | copy-start | bytes 5505028
  123.0 49.7 %collective-permute-start.6 = (bf16[2,224,1024]{2,1,0:T(8,128)(2,1)}, bf16[2,224,1024]{2,1,0:T(8,128)(2,1)}, u32[]{:S(2)}, u32[]{:S(2)}) collective-permute-start(bf16[2,224,1024]{2,1,0:T(8,128)(2,1)} %fusion.1), channel_id=1, source_target_pairs={{0,4},{4,0},{1,5},{5,1},{2,6},{6,2},{3,7},{7,3},{8,12},{12,8},{9,1... | collective-permute-start | bytes 2752520 | tf_op jit(solution)/shard_map/ppermute | solution.py:19
  127.4 1.2 copy-start.12
  127.4 49.7 %copy-start.6 = (bf16[2,2,224,1024]{3,2,1,0:T(8,128)(2,1)S(1)}, bf16[2,2,224,1024]{3,2,1,0:T(8,128)(2,1)}, u32[]{:S(2)}) copy-start(bf16[2,2,224,1024]{3,2,1,0:T(8,128)(2,1)} %copy-done.5) | copy-start | bytes 5505028
  128.6 44.2 %collective-permute-start.4 = (bf16[1,224,1024]{2,1,0:T(8,128)(2,1)}, bf16[1,224,1024]{2,1,0:T(8,128)(2,1)}, u32[]{:S(2)}, u32[]{:S(2)}) collective-permute-start(bf16[1,224,1024]{2,1,0:T(8,128)(2,1)} %fusion.4), channel_id=1, source_target_pairs={{0,4},{4,0},{1,5},{5,1},{2,6},{6,2},{3,7},{7,3},{8,12},{12,8},{9,1... | collective-permute-start | bytes 1376264 | tf_op jit(solution)/shard_map/ppermute | solution.py:19
  173.6 16.7 %all-to-all-start.3 = ((bf16[8,2,16,1024]{3,2,1,0:T(8,128)(2,1)}), bf16[8,2,16,1024]{3,2,1,0:T(8,128)(2,1)S(1)}, u32[]{:S(2)}, u32[]{:S(2)}) async-start(bf16[8,2,16,1024]{3,2,1,0:T(8,128)(2,1)} %broadcast_in_dim.24), calls=%async_computation.4 | async-start | bytes 1048576 | tf_op jit(solution)/shard_map/all_to_all | solution.py:329
  179.1 1.5 copy-start.13
Sparse Core Ops, SparseCore 0:
  11.4 48.9 all-gather.1
  111.8 43.5 reduce-scatter.1
